TPU v7x, 32 devices: a whole 2x2x4 slice. The times are simulated.
32 devices in a mesh: half: 2 (over y), row: 4 (over z), col: 4 (over x, core).
Axes of the slice: x: 2, y: 2, z: 4, core: 2. Of those that a mesh axis runs over, the one named last changes fastest.
Arguments:
- child_block: bfloat16 [2, 4, 4, 256, 4, 4, 256], P('half', None, 'row', None, None, 'col'), may hold values from -6 to 6
- child_row: bfloat16 [2, 256, 4, 4, 256], P('half', 'row', None, 'col'), may hold values from -6 to 6
- child_col: bfloat16 [2, 256, 4, 4, 256], P('half', 'col', None, 'row'), may hold values from -0.375 to 0.375
- child_pivot_inv: bfloat16 [2, 256, 256], P('half'), may hold values from -0.375 to 0.375
- child_map: int32 [2, 16], replicated, may hold values from 0 to 30, as said below
- parent_row: bfloat16 [256, 4, 8, 256], P('row', None, ('half', 'col')), may hold values from -6 to 6
- parent_col: bfloat16 [256, 8, 4, 256], P(('half', 'col'), None, 'row'), may hold values from -0.375 to 0.375
- parent_pivot_inv: bfloat16 [256, 256], replicated, may hold values from -0.375 to 0.375
- parent_diag: float32 [8, 4, 256], P(None, 'row'), may hold values from 1 to 3
Outputs:
- schur: bfloat16 [8, 4, 256, 4, 8, 256], P(None, 'row', None, None, ('half', 'col'))
Inputs may be any that keep to these rules, and one draw needn't show every extreme that they name: child_map[h, 4 * k + r] = 2 * 4 * k + r + p_h[k] for k and r from 0 to 3, where p_0 and p_1 are permutations of 0 to 3.
All inputs are finite; a program needn't handle non-finite values.
Results may differ from a plain program's by a relative error of at most 0.0041.
The roundings to bfloat16 on the way count: a program that leaves them out, or rounds other values in their place, can miss the bound.
Values may be sent and summed in bfloat16 or wider, within the bound.
No kernel may reach another device: no remote copies, remote signals or barrier semaphores. Data moves between devices by JAX's collectives and lax.ppermute only.
A program may use at most 384 MiB of HBM per device.

v0:
```python
import jax
import jax.numpy as jnp
from jax import lax
from jax.sharding import PartitionSpec as P


def swapped(value, axis, bit):
    mask = 2**bit
    pairs = [(source, source ^ mask) for source in range(lax.axis_size(axis))]
    return lax.ppermute(value, axis, pairs)


def inverse_maps(child_map, parent_tiles):
    targets = jnp.arange(parent_tiles, dtype=jnp.int32)
    matches = child_map[:, None, :] == targets[None, :, None]
    covered = jnp.any(matches, axis=2)
    positions = jnp.arange(child_map.shape[1], dtype=jnp.int32)
    sources = jnp.sum(jnp.where(matches, positions[None, None, :], 0), axis=2)
    return (covered, sources)


def pick_index(keys, wanted):
    positions = jnp.arange(keys.shape[0], dtype=jnp.int32)
    matched = keys[None, :] == wanted[:, None]
    return (jnp.sum(jnp.where(matched, positions[None, :], 0), axis=1), jnp.any(matched, axis=1))


def shards(
    child_block,
    child_row,
    child_col,
    child_pivot_inv,
    child_map,
    parent_row,
    parent_col,
    parent_pivot_inv,
    parent_diag,
):
    grid_size = lax.axis_size("row")
    tile_width = child_pivot_inv.shape[-1]
    my_half = lax.axis_index("half")
    my_row = lax.axis_index("row")
    my_col = lax.axis_index("col")
    local_width = grid_size * tile_width
    parent_height = 2 * grid_size * tile_width
    child_inv = child_pivot_inv[0]
    pieces = (
        lax.all_gather(child_row[0], "row", axis=0, tiled=True),
        lax.all_gather(parent_row, "row", axis=0, tiled=True),
    )
    piece_rows = pieces[0].shape[0]
    child_piece = pieces[0].reshape(piece_rows, local_width)
    parent_piece = pieces[1].reshape(piece_rows, local_width)
    child_sum = jnp.dot(child_inv, child_piece, preferred_element_type=jnp.float32)
    parent_sum = jnp.dot(parent_pivot_inv, parent_piece, preferred_element_type=jnp.float32)
    child_scaled = child_sum
    parent_scaled = parent_sum
    child_scaled = child_scaled.astype(jnp.bfloat16)
    parent_scaled = parent_scaled.astype(jnp.bfloat16)
    piece = lax.all_gather(child_col, "col", axis=1, tiled=True)
    piece_rows = piece.shape[1]
    flattened = piece.reshape(piece_rows, local_width)
    scaled_part = child_scaled
    child_update = lax.dot_general(
        flattened, scaled_part, (((0,), (0,)), ((), ())), preferred_element_type=jnp.float32
    )
    contribution = (
        child_block.reshape(local_width, local_width).astype(jnp.float32) - child_update
    ).astype(jnp.bfloat16)
    tile_grid = contribution.reshape(grid_size, tile_width, grid_size, tile_width)
    parent_rows = grid_size * jnp.arange(2 * grid_size, dtype=jnp.int32) + my_row
    column_slot = my_half * grid_size + my_col
    parent_columns = 2 * grid_size * jnp.arange(grid_size, dtype=jnp.int32) + column_slot
    diag_values = parent_diag.reshape(2 * grid_size, tile_width)
    on_diagonal = (parent_rows[:, None] == parent_columns[None, :]).astype(jnp.float32)
    identity = jnp.eye(tile_width, dtype=jnp.float32)
    diag_term = (
        diag_values[:, :, None, None] * on_diagonal[:, None, :, None] * identity[None, :, None, :]
    ).reshape(parent_height, local_width)
    piece = lax.all_gather(parent_col, ("half", "col"), axis=0, tiled=True)
    piece_rows = piece.shape[0]
    flattened = piece.reshape(piece_rows, parent_height)
    scaled_part = parent_scaled
    parent_front = diag_term - lax.dot_general(
        flattened, scaled_part, (((0,), (0,)), ((), ())), preferred_element_type=jnp.float32
    )
    covered, sources = inverse_maps(child_map, 2 * grid_size * grid_size)
    own_map = jnp.take(child_map, my_half, axis=0).reshape(grid_size, grid_size)
    row_targets = lax.dynamic_index_in_dim(own_map, my_row, 1, keepdims=False)
    col_targets = lax.dynamic_index_in_dim(own_map, my_col, 1, keepdims=False)
    slots_small = jnp.arange(grid_size, dtype=jnp.int32)
    row_pick, row_found = pick_index(row_targets % grid_size, slots_small)
    row_covered = covered[:, parent_rows]
    row_source = sources[:, parent_rows] % grid_size
    col_covered = covered[:, parent_columns]
    col_source = sources[:, parent_columns] % grid_size
    usable = row_covered[:, :, None] & col_covered[:, None, :]
    by_rows = jnp.take(tile_grid, row_pick, axis=0)
    first_section = lax.all_to_all(by_rows, "row", split_axis=0, concat_axis=0, tiled=True)
    col_pick, col_found = pick_index(col_targets % grid_size, slots_small)
    second_section = lax.all_to_all(
        jnp.take(first_section, col_pick, axis=2), "col", split_axis=2, concat_axis=2, tiled=True
    )
    partner = swapped(second_section, "half", 0)
    sibling_pieces = []
    for sibling in range(2):
        holder = jnp.where(my_half == sibling, second_section, partner)
        picked = jnp.take(holder, row_source[sibling], axis=0)
        sibling_pieces.append(jnp.take(picked, col_source[sibling], axis=2))
    front_blocks = parent_front.reshape(2 * grid_size, tile_width, grid_size, tile_width)
    for sibling in range(2):
        mask = usable[sibling][:, None, :, None]
        front_blocks = front_blocks + jnp.where(
            mask, sibling_pieces[sibling].astype(jnp.float32), 0.0
        )
    schur_front = front_blocks.astype(jnp.bfloat16)
    return schur_front.reshape(2 * grid_size, 1, tile_width, grid_size, 1, tile_width)


def solution(mesh):
    return jax.shard_map(
        shards,
        mesh=mesh,
        in_specs=(
            P("half", None, "row", None, None, "col", None),
            P("half", "row", None, "col", None),
            P("half", "col", None, "row", None),
            P("half", None, None),
            P(),
            P("row", None, ("half", "col"), None),
            P(("half", "col"), None, "row", None),
            P(),
            P(None, "row", None),
        ),
        out_specs=P(None, "row", None, None, ("half", "col"), None),
        check_vma=False,
    )
```

profile of v0, /device:TPU:0, one launch (start us, length us, event | category | flops | bytes accessed | tf_op | source)
XLA Modules:
  0.0 245.9 jit_solution(15861298484988127060)
XLA Ops:
  6.5 0.7 fusion.8
  7.4 0.2 dynamic-slice_reduce_fusion.1
  7.6 0.1 select_reduce_fusion.1
  7.7 4.2 %copy.54 = f32[128,8,4,256]{3,1,2,0:T(8,128)} copy(bf16[128,8,4,256]{3,2,1,0:T(4,128)(2,1)} %bitcast.95) | data formatting | bytes 6291456
  11.9 5.4 %copy.48 = f32[1024,1024]{0,1:T(8,128)} copy(f32[1024,1024]{1,0:T(8,128)} %bitcast.91) | data formatting | bytes 8388608 | tf_op jit(solution)/shard_map/convert_element_type | solution.py:68
  17.4 8.6 %all_gather.15 = bf16[1,256,4,1,256]{4,2,3,0,1:T(4,128)(2,1)S(1)} all-gather(bf16[1,64,4,1,256]{4,2,3,0,1:T(4,128)(2,1)S(1)} %bitcast.101), channel_id=1, replica_groups=mesh['half'=2,'row'=4,'col'=4] {'col'}, dimensions={1}, use_global_device_ids=true | all-gather | bytes 655360 | tf_op jit(solution)/shard_map/all_gather | solution.py:60
  26.1 16.4 %all-gather = bf16[1,256,4,1,256]{4,2,3,0,1:T(4,128)(2,1)S(1)} all-gather(bf16[1,64,4,1,256]{4,2,3,0,1:T(4,128)(2,1)S(1)} %bitcast.102), channel_id=2, replica_groups=mesh['half'=2,'row'=4,'col'=4] {'row'}, dimensions={1}, use_global_device_ids=true | all-gather | bytes 655360 | tf_op jit(solution)/shard_map/all_gather | solution.py:48
  42.5 3.1 %fusion.1 = bf16[1024,1024]{0,1:T(8,128)(2,1)S(1)} fusion(f32[1024,1024]{0,1:T(8,128)} %copy.48, bf16[256,1024]{1,0:T(8,128)(2,1)S(1)} %bitcast.93, bf16[256,1024]{1,0:T(8,128)(2,1)S(1)} %bitcast.94, bf16[1,256,256]{2,1,0:T(8,128)(2,1)S(1)} %copy-done.2), kind=kOutput, calls=%fused_computation.14 | convolution fusion | flops 673447936 | bytes 7471104 | tf_op jit(solution)/shard_map/dot_general | solution.py:64
  45.7 2.8 %reshape.219 = bf16[4,256,4,256]{1,0,3,2:T(4,128)(2,1)} reshape(bf16[1024,1024]{0,1:T(8,128)(2,1)S(1)} %fusion.1) | data formatting | bytes 4194304 | tf_op jit(solution)/shard_map/reshape | solution.py:70
  48.4 3.0 %copy.43 = bf16[4,256,4,256]{3,1,2,0:T(8,128)(2,1)S(1)} copy(bf16[4,256,4,256]{1,0,3,2:T(4,128)(2,1)} %reshape.219) | data formatting | bytes 4194304 | tf_op jit(solution)/shard_map/reshape | solution.py:70
  51.4 2.0 gather_fusion.2
  53.4 3.2 %broadcast_select_fusion.2 = bf16[4,256,4,256]{3,1,2,0:T(8,128)(2,1)} fusion(bf16[4,256,4,256]{3,1,2,0:T(8,128)(2,1)} %gather_fusion.2, pred[4]{0:T(512)(128)(4,1)S(1)} %compare_and_fusion.4), kind=kLoop, calls=%fused_computation.19 | loop fusion | flops 1048576 | bytes 4194308 | tf_op jit(solution)/shard_map/jit(_take)/select_n | solution.py:98
  56.6 5.0 %all-to-all-start = ((bf16[4,256,4,256]{3,1,2,0:T(8,128)(2,1)}), bf16[4,256,4,256]{3,1,2,0:T(8,128)(2,1)S(1)}, u32[]{:S(2)}, u32[]{:S(2)}) async-start(bf16[4,256,4,256]{3,1,2,0:T(8,128)(2,1)} %broadcast_select_fusion.2), calls=%async_computation | async-start | bytes 4194304 | tf_op jit(solution)/shard_map/all_to_all | solution.py:99
  61.6 0.7 all-gather.3.cloned.1.call-update
  62.5 0.6 gather_fusion.4
  63.1 0.1 select_reduce_fusion.2
  63.3 0.2 slice_reduce_fusion.1
  63.6 44.0 %all-to-all-done = bf16[4,256,4,256]{3,1,2,0:T(8,128)(2,1)S(1)} async-done(((bf16[4,256,4,256]{3,1,2,0:T(8,128)(2,1)}), bf16[4,256,4,256]{3,1,2,0:T(8,128)(2,1)S(1)}, u32[]{:S(2)}, u32[]{:S(2)}) %all-to-all-start) | async-done | bytes 2097184 | tf_op jit(solution)/shard_map/all_to_all | solution.py:99
  107.6 2.0 gather_fusion.3
  109.6 3.2 %select_bitcast_fusion = bf16[4,256,4,256]{3,1,0,2:T(8,128)(2,1)} fusion(bf16[4,4,256,256]{3,2,1,0:T(8,128)(2,1)} %gather_fusion.3, pred[4]{0:T(512)(128)(4,1)S(1)} %compare_and_fusion.5), kind=kLoop, calls=%fused_computation.18 | loop fusion | flops 1048576 | bytes 4194308 | tf_op jit(solution)/shard_map/jit(_take)/select_n | solution.py:102
  112.8 3.6 %all-to-all-start.1 = ((bf16[4,256,4,256]{3,1,0,2:T(8,128)(2,1)}), bf16[4,256,4,256]{3,1,0,2:T(8,128)(2,1)S(1)}, u32[]{:S(2)}, u32[]{:S(2)}) async-start(bf16[4,256,4,256]{3,1,0,2:T(8,128)(2,1)} %select_bitcast_fusion), calls=%async_computation.1 | async-start | bytes 4194304 | tf_op jit(solution)/shard_map/all_to_all | solution.py:101
  116.4 16.3 %all_gather.12 = bf16[256,4,1,256]{3,1,2,0:T(4,128)(2,1)S(1)} all-gather(bf16[64,4,1,256]{3,1,2,0:T(4,128)(2,1)S(1)} %copy-done.5), channel_id=1, replica_groups=mesh['half'=2,'row'=4,'col'=4] {'row'}, dimensions={0}, use_global_device_ids=true | all-gather | bytes 655360 | tf_op jit(solution)/shard_map/all_gather | solution.py:49
  132.9 3.9 %broadcast_multiply_fusion = f32[8,256,4,256]{1,0,3,2:T(8,128)} fusion(f32[256,256]{0,1:T(8,128)S(1)} %fusion.2, f32[8,256,4]{1,0,2:T(8,128)S(1)} %broadcast_multiply_fusion.1), kind=kLoop, calls=%fused_computation.15 | loop fusion | flops 2097152 | bytes 8683520 | tf_op jit(solution)/shard_map/mul | solution.py:78
  136.8 0.6 gather_fusion.5
  137.4 0.1 copy.34
  137.5 0.6 gather_fusion.1
  138.0 0.6 gather_fusion
  138.6 10.7 %copy.50 = f32[128,8,8,256]{3,1,2,0:T(8,128)} copy(f32[128,8,8,256]{3,2,1,0:T(8,128)} %bitcast.88) | data formatting | bytes 16777216
  149.3 0.9 copy.51
  150.2 0.1 copy.37
  150.4 0.2 slice_reduce_fusion.3
  150.6 1.6 collective-permute-start
  152.4 1.5 copy.52
  153.9 8.3 %bitcast_subtract_fusion = f32[2048,1024]{0,1:T(8,128)} fusion(f32[2048,1024]{0,1:T(8,128)} %bitcast.87, bf16[256,2048]{1,0:T(8,128)(2,1)S(1)} %bitcast.92, bf16[256,256]{1,0:T(8,128)(2,1)S(1)} %copy-done, bf16[256,1024]{1,0:T(8,128)(2,1)} %bitcast.96), kind=kOutput, calls=%fused_computation.10 | convolution fusion | flops 1210318848 | bytes 18481152 | tf_op jit(solution)/shard_map/dot_general | solution.py:84
  162.2 10.7 %copy.53 = f32[128,8,8,256]{3,2,1,0:T(8,128)} copy(f32[128,8,8,256]{3,1,2,0:T(8,128)} %bitcast.89) | data formatting | bytes 16777216
  172.9 9.9 %copy.45 = f32[8,256,4,256]{3,1,0,2:T(8,128)} copy(f32[8,256,4,256]{1,0,3,2:T(8,128)} %bitcast.90) | data formatting | bytes 16777216 | tf_op jit(solution)/shard_map/reshape | solution.py:110
  182.8 13.6 %collective-permute-done = bf16[4,256,4,256]{3,1,0,2:T(8,128)(2,1)} collective-permute-done((bf16[4,256,4,256]{3,1,0,2:T(8,128)(2,1)S(1)}, bf16[4,256,4,256]{3,1,0,2:T(8,128)(2,1)}, u32[]{:S(2)}, u32[]{:S(2)}) %collective-permute-start) | collective-permute-done | bytes 2097184 | tf_op jit(solution)/shard_map/ppermute | solution.py:10
  196.4 1.9 broadcast_select_fusion.4
  198.3 1.6 copy.46
  199.9 0.1 copy.44
  200.0 4.4 %gather_fusion.8 = bf16[8,256,4,256]{3,1,2,0:T(8,128)(2,1)} fusion(bf16[4,256,4,256]{3,1,2,0:T(8,128)(2,1)} %copy.46, s32[1024]{0:T(1024)S(1)} %pad_clamp_fusion.1), kind=kCustom, calls=%fused_computation.2.clone | custom fusion | bytes 8388640 | tf_op jit(solution)/shard_map/jit(_take)/gather | solution.py:108
  204.4 4.7 %broadcast_select_fusion = bf16[8,256,4,256]{3,1,2,0:T(8,128)(2,1)} fusion(bf16[8,256,4,256]{3,1,2,0:T(8,128)(2,1)} %gather_fusion.8, pred[8]{0:T(512)(128)(4,1)S(1)} %get-tuple-element.34), kind=kLoop, calls=%fused_computation.16 | loop fusion | flops 2097152 | bytes 8388616 | tf_op jit(solution)/shard_map/jit(_take)/select_n | solution.py:108
  209.1 5.0 %gather_fusion.9 = bf16[4,8,256,256]{3,2,1,0:T(8,128)(2,1)} fusion(bf16[8,256,4,256]{3,1,2,0:T(8,128)(2,1)} %broadcast_select_fusion, s32[1024]{0:T(1024)S(1)} %pad_clamp_fusion), kind=kCustom, calls=%fused_computation.3.clone | custom fusion | bytes 8388624 | tf_op jit(solution)/shard_map/jit(_take)/gather | solution.py:109
  214.1 2.8 %gather_fusion.6 = bf16[8,256,4,256]{3,1,2,0:T(8,128)(2,1)} fusion(bf16[4,256,4,256]{3,1,2,0:T(8,128)(2,1)S(1)} %copy.44, s32[1024]{0:T(1024)S(1)} %pad_clamp_fusion.3), kind=kCustom, calls=%fused_computation.clone | custom fusion | bytes 8388640 | tf_op jit(solution)/shard_map/jit(_take)/gather | solution.py:108
  216.9 4.7 %broadcast_select_fusion.1 = bf16[8,256,4,256]{3,1,2,0:T(8,128)(2,1)} fusion(bf16[8,256,4,256]{3,1,2,0:T(8,128)(2,1)} %gather_fusion.6, pred[8]{0:T(512)(128)(4,1)S(1)} %get-tuple-element.35), kind=kLoop, calls=%fused_computation.17 | loop fusion | flops 2097152 | bytes 8388616 | tf_op jit(solution)/shard_map/jit(_take)/select_n | solution.py:108
  221.6 5.0 %gather_fusion.7 = bf16[4,8,256,256]{3,2,1,0:T(8,128)(2,1)} fusion(bf16[8,256,4,256]{3,1,2,0:T(8,128)(2,1)} %broadcast_select_fusion.1, s32[1024]{0:T(1024)S(1)} %pad_clamp_fusion.2), kind=kCustom, calls=%fused_computation.1.clone | custom fusion | bytes 8388624 | tf_op jit(solution)/shard_map/jit(_take)/gather | solution.py:109
  226.5 7.3 %fusion = bf16[8,1,256,4,1,256]{5,2,0,3,4,1:T(8,128)(2,1)S(1)} fusion(f32[8,256,4,256]{3,1,0,2:T(8,128)} %copy.45, bf16[4,8,256,256]{3,2,1,0:T(8,128)(2,1)} %gather_fusion.9, bf16[4,8,256,256]{3,2,1,0:T(8,128)(2,1)} %gather_fusion.7, pred[4]{0:T(512)(128)(4,1)S(1)} %get-tuple-element.32, pred[4]{0:T(512)(128)(4,1)S(1)} %get-tuple-element.33, ...), kind=kLoop, calls=%fused_computation.12 | loop fusion | flops 18874368 | bytes 20971592 | tf_op jit(solution)/shard_map/reshape | solution.py:117
  233.8 5.3 %copy.47 = bf16[8,1,256,4,1,256]{5,3,4,2,1,0:T(4,128)(2,1)} copy(bf16[8,1,256,4,1,256]{5,2,0,3,4,1:T(8,128)(2,1)S(1)} %fusion) | data formatting | bytes 8388608 | tf_op jit(solution)/shard_map/reshape | solution.py:117
  (55 shorter events, 1.1 us)
Async XLA Ops:
  6.5 147.4 %copy-start = (bf16[256,256]{1,0:T(8,128)(2,1)S(1)}, bf16[256,256]{1,0:T(8,128)(2,1)}, u32[]{:S(2)}) copy-start(bf16[256,256]{1,0:T(8,128)(2,1)} %param.20) | copy-start | bytes 393220
  11.9 5.4 %copy-start.3 = (bf16[1,64,4,1,256]{4,2,3,1,0:T(4,128)(2,1)S(1)}, bf16[1,64,4,1,256]{4,2,3,1,0:T(4,128)(2,1)}, u32[]{:S(2)}) copy-start(bf16[1,64,4,1,256]{4,2,3,1,0:T(4,128)(2,1)} %param.15) | copy-start | bytes 393220
  11.9 14.1 %copy-start.4 = (bf16[1,64,4,1,256]{4,2,3,1,0:T(4,128)(2,1)S(1)}, bf16[1,64,4,1,256]{4,2,3,1,0:T(4,128)(2,1)}, u32[]{:S(2)}) copy-start(bf16[1,64,4,1,256]{4,2,3,1,0:T(4,128)(2,1)} %param.14) | copy-start | bytes 393220
  11.9 30.6 %copy-start.2 = (bf16[1,256,256]{2,1,0:T(8,128)(2,1)S(1)}, bf16[1,256,256]{2,1,0:T(8,128)(2,1)}, u32[]{:S(2)}) copy-start(bf16[1,256,256]{2,1,0:T(8,128)(2,1)} %param.16) | copy-start | bytes 393220
  53.4 8.9 %copy-start.7 = (s32[2,16]{1,0:T(2,128)S(1)}, s32[2,16]{1,0:T(2,128)}, u32[]{:S(2)}) copy-start(s32[2,16]{1,0:T(2,128)} %param.17) | copy-start | bytes 388
  56.6 50.9 %all-to-all-start = ((bf16[4,256,4,256]{3,1,2,0:T(8,128)(2,1)}), bf16[4,256,4,256]{3,1,2,0:T(8,128)(2,1)S(1)}, u32[]{:S(2)}, u32[]{:S(2)}) async-start(bf16[4,256,4,256]{3,1,2,0:T(8,128)(2,1)} %broadcast_select_fusion.2), calls=%async_computation | async-start | bytes 4194304 | tf_op jit(solution)/shard_map/all_to_all | solution.py:99
  61.6 90.8 %all-gather.3.cloned.1.call-start = ((), (), s32[]{:S(2)}) async-start(), calls=%async_computation.2 | async-start | bytes 1179648 | tf_op jit(solution)/shard_map/all_gather | solution.py:80
  109.6 6.8 %copy-start.6 = (f32[8,1,256]{2,1,0:T(1,128)S(1)}, f32[8,1,256]{2,1,0:T(1,128)}, u32[]{:S(2)}) copy-start(f32[8,1,256]{2,1,0:T(1,128)} %param.21) | copy-start | bytes 24580
  109.6 6.9 %copy-start.5 = (bf16[64,4,1,256]{3,1,2,0:T(4,128)(2,1)S(1)}, bf16[64,4,1,256]{3,1,2,0:T(4,128)(2,1)}, u32[]{:S(2)}) copy-start(bf16[64,4,1,256]{3,1,2,0:T(4,128)(2,1)} %param.18) | copy-start | bytes 393220
  112.8 37.8 %all-to-all-start.1 = ((bf16[4,256,4,256]{3,1,0,2:T(8,128)(2,1)}), bf16[4,256,4,256]{3,1,0,2:T(8,128)(2,1)S(1)}, u32[]{:S(2)}, u32[]{:S(2)}) async-start(bf16[4,256,4,256]{3,1,0,2:T(8,128)(2,1)} %select_bitcast_fusion), calls=%async_computation.1 | async-start | bytes 4194304 | tf_op jit(solution)/shard_map/all_to_all | solution.py:101
  150.6 45.8 %collective-permute-start = (bf16[4,256,4,256]{3,1,0,2:T(8,128)(2,1)S(1)}, bf16[4,256,4,256]{3,1,0,2:T(8,128)(2,1)}, u32[]{:S(2)}, u32[]{:S(2)}) collective-permute-start(bf16[4,256,4,256]{3,1,0,2:T(8,128)(2,1)S(1)} %all-to-all-done.1), channel_id=1, source_target_pairs={{0,16},{16,0},{1,17},{17,1},{2,18},{18,2},{3,19},{19,3},{4,20},{20... | collective-permute-start | bytes 6291464 | tf_op jit(solution)/shard_map/ppermute | solution.py:10
  226.5 12.6 %copy-start.1 = (bf16[256,256]{1,0:T(8,128)(2,1)S(1)}, bf16[256,256]{1,0:T(8,128)(2,1)}, u32[]{:S(2)}) copy-start(bf16[256,256]{1,0:T(8,128)(2,1)} %param.20) | copy-start | bytes 393220
Sparse Core Ops, SparseCore 0:
  64.3 24.5 all-gather.2
where the time goes:
time: 247 us; the launch traced here: 246 us
  local copies, waits for them, and re-layouts  80.8 us (33%)
  waiting for transfers between devices  58.3 us (24%)
  blocking collectives  41.3 us (17%)
  other arithmetic  30.3 us (12%)
  between operations  13.7 us (6%)
  matrix products  11.4 us (5%)
  starting transfers between devices  10.2 us (4%)
    all_to_all x1, waiting for transfers between devices, shards(): lax.all_to_all(by_rows, 'row', split_axis=0, concat_axis=0, tiled=True)  44 us
    unnamed x24, local copies, waits for them, and re-layouts  28.3 us
    all_gather x1, blocking collectives, shards(): lax.all_gather(child_row[0], 'row', axis=0, tiled=True)  16.4 us
    all_gather x1, blocking collectives, shards(): lax.all_gather(parent_row, 'row', axis=0, tiled=True)  16.3 us
    ppermute x1, waiting for transfers between devices, swapped(): return lax.ppermute(value, axis, pairs)  13.6 us
    dot_general x2, matrix products, shards(): lax.dot_general(flattened, scaled_part, (((0,), (0,)), ((), ())), preferr...  11.4 us
    gather x2, local copies, waits for them, and re-layouts, shards(): sibling_pieces.append(jnp.take(picked, col_source[sibling], axis=2))  9.93 us
    reshape x1, local copies, waits for them, and re-layouts, shards(): parent_front.reshape(2 * grid_size, tile_width, grid_size, tile_width)  9.91 us
  transfers between devices with their start and end apart: 4, of which 2 were waited for; matrix products, arithmetic and copies ran while one was open for 22% of the time, Pallas kernels for 0%

commit v1 on v0

v1 whole, which is shorter than its diff:
```python
import functools

import jax
import jax.numpy as jnp
from jax import lax
from jax.experimental import pallas as pl
from jax.experimental.pallas import tpu as pltpu
from jax.sharding import PartitionSpec as P

F32 = jnp.float32
BF16 = jnp.bfloat16
PLANE = ("half", "col")


def shifted(value, axis, step):
    count = lax.axis_size(axis)
    return lax.ppermute(value, axis, [(i, (i + step) % count) for i in range(count)])


def gathered(value, axis, order):
    parts = {0: value}
    for step in order:
        parts[step] = shifted(value, axis, step)
    return jnp.concatenate([parts[d] for d in range(lax.axis_size(axis))], axis=1)


def far_first(count):
    return sorted(range(1, count), key=lambda d: -d * (count - d))


def chunks_back(matrix, dim, start, count):
    width = matrix.shape[dim] // count
    return jnp.concatenate(
        [
            lax.dynamic_slice_in_dim(matrix, (start - d) % count * width, width, dim)
            for d in range(count)
        ],
        axis=dim,
    )


def update_kernel(picks, block_ref, col_ref, scaled_ref, out_ref):
    update = lax.dot_general(
        col_ref[0], scaled_ref[0], (((0,), (0,)), ((), ())), preferred_element_type=F32
    )
    out_ref[0] = (block_ref[0, 0].astype(F32) - update).astype(BF16)


def updated_row(block, col, scaled, row_pick, col_picks):
    grid, tile = block.shape[0], block.shape[-1]
    picks = jnp.concatenate([row_pick[None], col_picks])
    spec = pltpu.PrefetchScalarGridSpec(
        num_scalar_prefetch=1,
        grid=(grid,),
        in_specs=[
            pl.BlockSpec((1, 1, tile, tile), lambda s, picks: (picks[0], picks[s + 1], 0, 0)),
            pl.BlockSpec((1, tile, tile), lambda s, picks: (picks[0], 0, 0)),
            pl.BlockSpec((1, tile, tile), lambda s, picks: (picks[s + 1], 0, 0)),
        ],
        out_specs=pl.BlockSpec((1, tile, tile), lambda s, picks: (s, 0, 0)),
    )
    return pl.pallas_call(
        update_kernel,
        grid_spec=spec,
        out_shape=jax.ShapeDtypeStruct((grid, tile, tile), BF16),
        cost_estimate=pl.CostEstimate(
            flops=2 * grid * tile**3, bytes_accessed=7 * grid * tile * tile, transcendentals=0
        ),
        name="child_update",
    )(picks, block, col, scaled)


def front_kernel(grid, picks, *refs):
    arrived = refs[:grid]
    col_ref, scaled_ref, diag_ref, weave_ref, out_ref, held, total, rounded, sems = refs[grid:]
    tile = col_ref.shape[-1]
    step = pl.program_id(0)
    copies = [
        pltpu.make_async_copy(arrived[d], held.at[d], sems.at[d]) for d in range(grid)
    ]

    @pl.when(step == 0)
    def _():
        for copy in copies:
            copy.start()
        for copy in copies:
            copy.wait()

    for q in range(grid):
        base = 2 * grid * q
        value = -lax.dot_general(
            col_ref[0], scaled_ref[q], (((0,), (0,)), ((), ())), preferred_element_type=F32
        )
        for child in range(2):
            chunk = picks[child, step]
            usable = picks[2 + child, step] * picks[6 + child, q]
            source = picks[4 + child, q]
            piece = held[chunk, source]
            value = value + jnp.where(usable > 0, piece.astype(F32), 0.0)
        total[...] = value

        @pl.when(picks[8, q] == step)
        def _():
            rows = lax.broadcasted_iota(jnp.int32, (tile, tile), 0)
            columns = lax.broadcasted_iota(jnp.int32, (tile, tile), 1)
            total[...] += jnp.where(rows == columns, diag_ref[0], 0.0)

        rounded[q] = total[...].astype(BF16)
    rows = tile // grid
    for part in range(grid):
        stacked = jnp.concatenate(
            [rounded[q, part * rows : (part + 1) * rows] for q in range(grid)], axis=0
        )
        woven = jnp.dot(weave_ref[...], stacked, preferred_element_type=F32)
        out_ref[0, part * rows : (part + 1) * rows] = woven.reshape(rows, grid, tile).astype(BF16)


def front(arrived, col, scaled, diag, picks):
    grid, tile = scaled.shape[0], scaled.shape[-1]
    rows = tile // grid
    place = jnp.arange(tile, dtype=jnp.int32)
    weave = (place[None, :] == (place % grid * rows + place // grid)[:, None]).astype(BF16)
    whole = lambda *shape: pl.BlockSpec(shape, lambda s, picks: (0,) * len(shape))
    spec = pltpu.PrefetchScalarGridSpec(
        num_scalar_prefetch=1,
        grid=(2 * grid,),
        in_specs=[pl.BlockSpec(memory_space=pl.ANY)] * grid
        + [
            pl.BlockSpec((1, tile, tile), lambda s, picks: (s, 0, 0)),
            whole(grid, tile, tile),
            pl.BlockSpec((1, 1, tile), lambda s, picks: (s, 0, 0)),
            whole(tile, tile),
        ],
        out_specs=pl.BlockSpec((1, tile, grid, tile), lambda s, picks: (s, 0, 0, 0)),
        scratch_shapes=[
            pltpu.VMEM((grid, 2 * grid, tile, tile), BF16),
            pltpu.VMEM((tile, tile), F32),
            pltpu.VMEM((grid, tile, tile), BF16),
            pltpu.SemaphoreType.DMA((grid,)),
        ],
    )
    return pl.pallas_call(
        functools.partial(front_kernel, grid),
        grid_spec=spec,
        out_shape=jax.ShapeDtypeStruct((2 * grid, tile, grid, tile), BF16),
        compiler_params=pltpu.CompilerParams(vmem_limit_bytes=48 * 2**20),
        cost_estimate=pl.CostEstimate(
            flops=8 * grid * grid * tile**3,
            bytes_accessed=12 * grid * grid * tile * tile,
            transcendentals=0,
        ),
        name="front",
    )(picks, *arrived, col, scaled, diag, weave)


def shards(
    child_block,
    child_row,
    child_col,
    child_pivot_inv,
    child_map,
    parent_row,
    parent_col,
    parent_pivot_inv,
    parent_diag,
):
    grid = lax.axis_size("row")
    tile = child_pivot_inv.shape[-1]
    my_half = lax.axis_index("half")
    my_row = lax.axis_index("row")
    my_col = lax.axis_index("col")
    places = jnp.arange(grid, dtype=jnp.int32)
    shift = child_map[:, ::grid] - 2 * grid * places[None, :]
    unshift = jnp.sum(
        jnp.where(shift[:, None, :] == places[None, :, None], places[None, None, :], 0), axis=2
    )
    mine = jnp.sum(jnp.where(jnp.arange(2)[:, None] == my_half, unshift, 0), axis=0)
    leaving = jnp.sum(
        jnp.where(((places - my_col) % grid)[:, None] == places[None, :], mine[None, :], 0), axis=1
    )

    child_rows = gathered(child_row[0, :, :, 0].transpose(1, 0, 2), "row", far_first(grid))
    child_cols = gathered(child_col[0, :, :, 0].transpose(1, 0, 2), "col", far_first(grid))
    parent_rows = gathered(parent_row[:, :, 0].transpose(1, 0, 2), "row", far_first(grid))
    parent_cols = lax.all_gather(parent_col, PLANE, axis=0, tiled=True)[:, :, 0].transpose(1, 0, 2)
    child_inv = chunks_back(chunks_back(child_pivot_inv[0], 0, my_col, grid), 1, my_row, grid)
    parent_inv = chunks_back(parent_pivot_inv, 1, my_row, grid)
    scale = lambda inverse, rows: jnp.einsum(
        "ab,lbj->laj", inverse, rows, preferred_element_type=F32
    ).astype(BF16)
    child_scaled = scale(child_inv, child_rows)

    blocks = child_block[0, :, 0, :, :, 0].transpose(0, 2, 1, 3)
    arrived = {}
    for step in (*far_first(grid), 0):
        row = updated_row(blocks, child_cols, child_scaled, mine[step], leaving)
        arrived[step] = shifted(row, "row", step) if step else row
    for step in (0, *far_first(grid)):
        row = arrived[step]
        arrived[step] = lax.all_to_all(
            jnp.concatenate([row, row]), PLANE, split_axis=0, concat_axis=0, tiled=True
        )
    parent_scaled = scale(parent_inv, parent_rows)

    targets = jnp.arange(2 * grid, dtype=jnp.int32)
    row_shift = jnp.repeat(shift, 2, axis=1)
    row_usable = (my_row < row_shift) == (targets % 2 == 1)[None, :]
    source = (my_col - shift) % grid + grid * jnp.arange(2, dtype=jnp.int32)[:, None]
    col_usable = (my_col < shift) == (my_half == 1)
    on_diagonal = jnp.where(my_row == my_col, 2 * places + my_half, -1)
    wide = lambda a: jnp.pad(a.astype(jnp.int32), ((0, 0), (0, 2 * grid - a.shape[1])))
    picks = jnp.concatenate(
        [row_shift, row_usable.astype(jnp.int32), wide(source), wide(col_usable), wide(on_diagonal[None])]
    )
    return front(
        [arrived[d] for d in range(grid)], parent_cols, parent_scaled, parent_diag, picks
    ).reshape(2 * grid, 1, tile, grid, 1, tile)


def solution(mesh):
    return jax.shard_map(
        shards,
        mesh=mesh,
        in_specs=(
            P("half", None, "row", None, None, "col", None),
            P("half", "row", None, "col", None),
            P("half", "col", None, "row", None),
            P("half", None, None),
            P(),
            P("row", None, ("half", "col"), None),
            P(("half", "col"), None, "row", None),
            P(),
            P(None, "row", None),
        ),
        out_specs=P(None, "row", None, None, ("half", "col"), None),
        check_vma=False,
    )
```

time: 247 us -> 179 us (0.72)
  local copies, waits for them, and re-layouts: 80.8 us -> 11.8 us
  blocking collectives: 41.3 us -> 0 us
  Pallas kernels: 0 us -> 31.3 us
  starting transfers between devices: 10.2 us -> 30.3 us
  other arithmetic: 30.3 us -> 11.3 us
  waiting for transfers between devices: 58.3 us -> 75 us
  matrix products: 11.4 us -> 4.02 us
    ppermute x1 -> x12, waiting for transfers between devices: 13.6 us -> 75 us  [shifted(): lax.ppermute(value, axis, [(i, (i + step) % count) for i in range(count)])]
    all_to_all x2 -> x4, waiting for transfers between devices: 44 us -> 0.01 us  [shards(): lax.all_to_all(jnp.concatenate([row, row]), PLANE, split_axis=0, concat_a...]
    all_gather x3 -> x0, blocking collectives: 41.3 us -> none  [the longest x1 16.4 us: shards(): lax.all_gather(child_row[0], 'row', axis=0, tiled=True)]
    pallas_call x0 -> x5, Pallas kernels: none -> 31.3 us  [the longest x4 18 us: updated_row(): pl.pallas_call(update_kernel, grid_spec=spec, out_shape=jax.ShapeDtypeStr...]
    gather x12 -> x0, local copies, waits for them, and re-layouts: 23.6 us -> none  [the longest x2 9.93 us: shards(): sibling_pieces.append(jnp.take(picked, col_source[sibling], axis=2))]
    reshape x4 -> x1, local copies, waits for them, and re-layouts: 20.9 us -> 0.09 us  [shards(): row_shift = jnp.repeat(shift, 2, axis=1)]
    unnamed x24 -> x17, local copies, waits for them, and re-layouts: 28.3 us -> 9.11 us
    select_n x15 -> x2, other arithmetic: 18.4 us -> 0.02 us  [the longest x1 0.01 us: shards(): (places - my_col) % grid]
  transfers between devices with their start and end apart: 4 -> 17, of which waited for: 2 -> 5; matrix products, arithmetic and copies ran while one was open for 22% -> 11% of each run, Pallas kernels for 0% -> 8%
where the time goes in v1:
time: 179 us; the launch traced here: 178 us
  waiting for transfers between devices  75 us (42%)
  Pallas kernels  31.3 us (17%)
  starting transfers between devices  30.3 us (17%)
  between operations  13.6 us (8%)
  local copies, waits for them, and re-layouts  11.8 us (7%)
  other arithmetic  11.3 us (6%)
  matrix products  4.02 us (2%)
    ppermute x12, waiting for transfers between devices, shifted(): lax.ppermute(value, axis, [(i, (i + step) % count) for i in range(count)])  75 us
    pallas_call x4, Pallas kernels, updated_row(): pl.pallas_call(update_kernel, grid_spec=spec, out_shape=jax.ShapeDtypeStr...  18 us
    all_to_all x4, starting transfers between devices, shards(): lax.all_to_all(jnp.concatenate([row, row]), PLANE, split_axis=0, concat_a...  15.5 us
    ppermute x12, starting transfers between devices, shifted(): lax.ppermute(value, axis, [(i, (i + step) % count) for i in range(count)])  14.8 us
    pallas_call x1, Pallas kernels, front(): pl.pallas_call(functools.partial(front_kernel, grid), grid_spec=spec, out...  13.3 us
    unnamed x17, local copies, waits for them, and re-layouts  9.11 us
    concatenate x4, other arithmetic, shards(): jnp.concatenate([row, row])  6.71 us
    dot_general x2, matrix products, shards(): jnp.einsum('ab,lbj->laj', inverse, rows, preferred_element_type=F32)  4.02 us
  transfers between devices with their start and end apart: 17, of which 5 were waited for; matrix products, arithmetic and copies ran while one was open for 11% of the time, Pallas kernels for 8%

profile of v1, /device:TPU:0, one launch (start us, length us, event | category | flops | bytes accessed | tf_op | source)
XLA Modules:
  0.0 177.5 jit_solution(16615699010153729011)
XLA Ops:
  6.5 0.9 copy.39
  7.5 2.4 %collective-permute-start.2 = (bf16[4,64,256]{2,1,0:T(8,128)(2,1)S(1)}, bf16[4,64,256]{2,1,0:T(8,128)(2,1)S(1)}, u32[]{:S(2)}, u32[]{:S(2)}) collective-permute-start(bf16[4,64,256]{2,1,0:T(8,128)(2,1)S(1)} %bitcast.45), channel_id=1, source_target_pairs={{0,3},{1,0},{2,1},{3,2},{4,7},{5,4},{6,5},{7,6},{8,11},{9,8},{10,9... | collective-permute-start | bytes 393224 | tf_op jit(solution)/shard_map/ppermute | solution.py:17
  9.9 0.6 collective-permute-start.1
  10.5 0.2 collective-permute-start
  10.7 1.1 copy.28
  11.8 3.7 %collective-permute-start.5 = (bf16[4,64,256]{1,2,0:T(8,128)(2,1)S(1)}, bf16[4,64,256]{1,2,0:T(8,128)(2,1)S(1)}, u32[]{:S(2)}, u32[]{:S(2)}) collective-permute-start(bf16[4,64,256]{1,2,0:T(8,128)(2,1)S(1)} %bitcast.49), channel_id=1, source_target_pairs={{0,12},{4,0},{8,4},{12,8},{1,13},{5,1},{9,5},{13,9},{2,14},{6,2},{... | collective-permute-start | bytes 393224 | tf_op jit(solution)/shard_map/ppermute | solution.py:17
  15.5 0.8 slice.15
  16.3 0.1 select_reduce_fusion
  16.5 0.1 fusion.33
  16.6 0.8 dynamic-slice_bitcast_fusion.3
  17.4 0.1 constant_dynamic-slice_fusion.7
  17.6 0.2 select_reduce_fusion.1
  17.7 0.7 fusion.39
  18.4 1.0 collective-permute-start.3
  19.4 3.1 %pad_add_fusion.3 = (s32[5]{0:T(128)}, s32[5]{0:T(128)}, s32[5]{0:T(128)}, s32[5]{0:T(128)}) fusion(s32[1]{0:T(128)} %get-tuple-element.23, s32[4]{0:T(128)S(1)} %select_reduce_fusion.1, s32[1]{0:T(128)} %get-tuple-element.25, s32[1]{0:T(128)} %get-tuple-element.24, s32[1]{0:T(128)} %get-tuple-element.26), kind=kLoop, calls=%fused_computation.86 | loop fusion | flops 20 | bytes 112 | tf_op jit(solution)/shard_map/concatenate | solution.py:51
  22.5 3.3 %copy.38 = bf16[1,4,1,256,4,1,256]{6,3,4,1,5,2,0:T(8,128)(2,1)} copy(bf16[1,4,1,256,4,1,256]{6,4,5,3,2,1,0:T(4,128)(2,1)} %param.9) | data formatting | bytes 4194304 | tf_op args[0]
  25.8 0.8 pad_maximum_fusion.4.col_ref
  26.7 11.9 %collective-permute-done.4 = bf16[4,64,256]{1,2,0:T(8,128)(2,1)S(1)} collective-permute-done((bf16[4,64,256]{1,2,0:T(8,128)(2,1)S(1)}, bf16[4,64,256]{1,2,0:T(8,128)(2,1)S(1)}, u32[]{:S(2)}, u32[]{:S(2)}) %collective-permute-start.4) | collective-permute-done | bytes 131104 | tf_op jit(solution)/shard_map/ppermute | solution.py:17
  38.6 1.4 fusion.scaled_ref
  40.0 4.5 %child_update.4 = bf16[4,256,256]{2,1,0:T(8,128)(2,1)} custom-call(s32[5]{0:T(128)} %get-tuple-element.22.picks, bf16[4,4,256,256]{3,2,1,0:T(8,128)(2,1)} %bitcast.41, bf16[4,256,256]{2,1,0:T(8,128)(2,1)} %pad_maximum_fusion.4.col_ref, bf16[4,256,256]{2,1,0:T(8,128)(2,1)} %fusion.scaled_ref), custom_call_target="tpu_custom_call" | custom-call | flops 134217728 | bytes 1835008 | tf_op jit(solution)/shard_map/child_update/pallas_call | solution.py:62
  44.5 2.3 %pad_maximum_fusion = bf16[8,256,256]{2,1,0:T(8,128)(2,1)} fusion(bf16[4,256,256]{2,1,0:T(8,128)(2,1)} %child_update.4), kind=kLoop, calls=%fused_computation.5 | loop fusion | flops 524288 | bytes 1572864 | tf_op jit(solution)/shard_map/concatenate | solution.py:201
  46.8 3.6 %all-to-all-start = ((bf16[8,256,256]{2,1,0:T(8,128)(2,1)}), bf16[8,256,256]{2,1,0:T(8,128)(2,1)S(1)}, u32[]{:S(2)}, u32[]{:S(2)}) async-start(bf16[8,256,256]{2,1,0:T(8,128)(2,1)} %pad_maximum_fusion), calls=%async_computation | async-start | bytes 2097152 | tf_op jit(solution)/shard_map/all_to_all | solution.py:200
  50.4 4.5 %child_update.5 = bf16[4,256,256]{2,1,0:T(8,128)(2,1)} custom-call(s32[5]{0:T(128)} %get-tuple-element.20.picks, bf16[4,4,256,256]{3,2,1,0:T(8,128)(2,1)} %bitcast.42, bf16[4,256,256]{2,1,0:T(8,128)(2,1)} %pad_maximum_fusion.4.col_ref, bf16[4,256,256]{2,1,0:T(8,128)(2,1)} %fusion.scaled_ref), custom_call_target="tpu_custom_call" | custom-call | flops 134217728 | bytes 1835008 | tf_op jit(solution)/shard_map/child_update/pallas_call | solution.py:62
  54.9 1.3 collective-permute-start.6
  56.2 14.9 %collective-permute-done.6 = bf16[4,256,256]{2,1,0:T(8,128)(2,1)S(1)} collective-permute-done((bf16[4,256,256]{2,1,0:T(8,128)(2,1)}, bf16[4,256,256]{2,1,0:T(8,128)(2,1)S(1)}, u32[]{:S(2)}, u32[]{:S(2)}) %collective-permute-start.6) | collective-permute-done | bytes 524320 | tf_op jit(solution)/shard_map/ppermute | solution.py:17
  71.2 1.1 pad_maximum_fusion.1
  72.3 3.8 %all-to-all-start.1 = ((bf16[8,256,256]{2,1,0:T(8,128)(2,1)}), bf16[8,256,256]{2,1,0:T(8,128)(2,1)S(1)}, u32[]{:S(2)}, u32[]{:S(2)}) async-start(bf16[8,256,256]{2,1,0:T(8,128)(2,1)} %pad_maximum_fusion.1), calls=%async_computation.1 | async-start | bytes 2097152 | tf_op jit(solution)/shard_map/all_to_all | solution.py:200
  76.1 4.5 %child_update.6 = bf16[4,256,256]{2,1,0:T(8,128)(2,1)} custom-call(s32[5]{0:T(128)} %get-tuple-element.21.picks, bf16[4,4,256,256]{3,2,1,0:T(8,128)(2,1)} %bitcast.43, bf16[4,256,256]{2,1,0:T(8,128)(2,1)} %pad_maximum_fusion.4.col_ref, bf16[4,256,256]{2,1,0:T(8,128)(2,1)} %fusion.scaled_ref), custom_call_target="tpu_custom_call" | custom-call | flops 134217728 | bytes 1835008 | tf_op jit(solution)/shard_map/child_update/pallas_call | solution.py:62
  80.6 1.5 collective-permute-start.7
  82.0 24.3 %collective-permute-done.7 = bf16[4,256,256]{2,1,0:T(8,128)(2,1)S(1)} collective-permute-done((bf16[4,256,256]{2,1,0:T(8,128)(2,1)}, bf16[4,256,256]{2,1,0:T(8,128)(2,1)S(1)}, u32[]{:S(2)}, u32[]{:S(2)}) %collective-permute-start.7) | collective-permute-done | bytes 524320 | tf_op jit(solution)/shard_map/ppermute | solution.py:17
  106.3 1.1 pad_maximum_fusion.2
  107.4 3.8 %all-to-all-start.2 = ((bf16[8,256,256]{2,1,0:T(8,128)(2,1)}), bf16[8,256,256]{2,1,0:T(8,128)(2,1)S(1)}, u32[]{:S(2)}, u32[]{:S(2)}) async-start(bf16[8,256,256]{2,1,0:T(8,128)(2,1)} %pad_maximum_fusion.2), calls=%async_computation.2 | async-start | bytes 2097152 | tf_op jit(solution)/shard_map/all_to_all | solution.py:200
  111.3 0.7 copy.30
  112.0 4.5 %child_update.7 = bf16[4,256,256]{2,1,0:T(8,128)(2,1)} custom-call(s32[5]{0:T(128)} %get-tuple-element.19.picks, bf16[4,4,256,256]{3,2,1,0:T(8,128)(2,1)} %bitcast.44, bf16[4,256,256]{2,1,0:T(8,128)(2,1)} %pad_maximum_fusion.4.col_ref, bf16[4,256,256]{2,1,0:T(8,128)(2,1)} %fusion.scaled_ref), custom_call_target="tpu_custom_call" | custom-call | flops 134217728 | bytes 1835008 | tf_op jit(solution)/shard_map/child_update/pallas_call | solution.py:62
  116.5 2.1 %collective-permute-start.8 = (bf16[4,256,256]{2,1,0:T(8,128)(2,1)}, bf16[4,256,256]{2,1,0:T(8,128)(2,1)}, u32[]{:S(2)}, u32[]{:S(2)}) collective-permute-start(bf16[4,256,256]{2,1,0:T(8,128)(2,1)} %child_update.7), channel_id=1, source_target_pairs={{0,12},{4,0},{8,4},{12,8},{1,13},{5,1},{9,5},{13,9},{2,14},{6,2},{... | collective-permute-start | bytes 1572872 | tf_op jit(solution)/shard_map/ppermute | solution.py:17
  118.6 0.9 copy.31
  119.5 1.4 collective-permute-start.10
  120.9 0.6 collective-permute-start.9
  121.7 9.9 %collective-permute-done.8 = bf16[4,256,256]{2,1,0:T(8,128)(2,1)} collective-permute-done((bf16[4,256,256]{2,1,0:T(8,128)(2,1)}, bf16[4,256,256]{2,1,0:T(8,128)(2,1)}, u32[]{:S(2)}, u32[]{:S(2)}) %collective-permute-start.8) | collective-permute-done | bytes 524320 | tf_op jit(solution)/shard_map/ppermute | solution.py:17
  131.5 2.3 %pad_maximum_fusion.3 = bf16[8,256,256]{2,1,0:T(8,128)(2,1)} fusion(bf16[4,256,256]{2,1,0:T(8,128)(2,1)} %collective-permute-done.8), kind=kLoop, calls=%fused_computation.8 | loop fusion | flops 524288 | bytes 1572864 | tf_op jit(solution)/shard_map/concatenate | solution.py:201
  133.8 4.2 %all-to-all-start.3 = ((bf16[8,256,256]{2,1,0:T(8,128)(2,1)}), bf16[8,256,256]{2,1,0:T(8,128)(2,1)}, u32[]{:S(2)}, u32[]{:S(2)}) async-start(bf16[8,256,256]{2,1,0:T(8,128)(2,1)} %pad_maximum_fusion.3), calls=%async_computation.3 | async-start | bytes 2097152 | tf_op jit(solution)/shard_map/all_to_all | solution.py:200
  138.1 0.1 fusion.16.refs_7_
  138.3 0.1 constant_dynamic-slice_fusion.3
  138.5 13.9 %collective-permute-done.10 = bf16[4,64,256]{1,2,0:T(8,128)(2,1)} collective-permute-done((bf16[4,64,256]{1,2,0:T(8,128)(2,1)}, bf16[4,64,256]{1,2,0:T(8,128)(2,1)}, u32[]{:S(2)}, u32[]{:S(2)}) %collective-permute-start.10) | collective-permute-done | bytes 131104 | tf_op jit(solution)/shard_map/ppermute | solution.py:17
  152.4 2.6 %fusion.1.refs_5_ = bf16[4,256,256]{2,1,0:T(8,128)(2,1)} fusion(bf16[4,64,256]{1,2,0:T(8,128)(2,1)} %collective-permute-done.11, bf16[4,64,256]{1,2,0:T(8,128)(2,1)} %collective-permute-done.10, bf16[4,64,256]{1,2,0:T(8,128)(2,1)} %collective-permute-done.9, bf16[4,64,256]{1,2,0:T(8,128)(2,1)} %bitcast.18, bf16[256,64]{1,0:T(8,128)(2,1)S(1)} %get-tuple-element.9, ...), kind=kOutput, calls=%fused_computation.4 | convolution fusion | flops 137101312 | bytes 1179648 | tf_op jit(solution)/shard_map/ab,lbj->laj/dot_general | solution.py:188
  155.0 1.2 copy-done
  156.3 1.0 copy-done.1
  157.3 13.3 %front.1 = bf16[8,256,4,256]{3,2,1,0:T(4,128)(2,1)} custom-call(s32[9,8]{1,0:T(8,128)S(1)} %concatenate.45.picks, bf16[8,256,256]{2,1,0:T(8,128)(2,1)S(1)} %all-to-all-done.refs_0_, bf16[8,256,256]{2,1,0:T(8,128)(2,1)S(1)} %all-to-all-done.1.refs_1_, bf16[8,256,256]{2,1,0:T(8,128)(2,1)S(1)} %all-to-all-done.2.refs_2_, ...), custom_call_target="tpu_custom_call" | custom-call | flops 2147483648 | bytes 12582912 | tf_op jit(solution)/shard_map/front/pallas_call | solution.py:142
  (41 shorter events, 0.4 us)
Async XLA Ops:
  7.5 10.9 %collective-permute-start.2 = (bf16[4,64,256]{2,1,0:T(8,128)(2,1)S(1)}, bf16[4,64,256]{2,1,0:T(8,128)(2,1)S(1)}, u32[]{:S(2)}, u32[]{:S(2)}) collective-permute-start(bf16[4,64,256]{2,1,0:T(8,128)(2,1)S(1)} %bitcast.45), channel_id=1, source_target_pairs={{0,3},{1,0},{2,1},{3,2},{4,7},{5,4},{6,5},{7,6},{8,11},{9,8},{10,9... | collective-permute-start | bytes 393224 | tf_op jit(solution)/shard_map/ppermute | solution.py:17
  9.9 15.9 %collective-permute-start.1 = (bf16[4,64,256]{2,1,0:T(8,128)(2,1)S(1)}, bf16[4,64,256]{2,1,0:T(8,128)(2,1)S(1)}, u32[]{:S(2)}, u32[]{:S(2)}) collective-permute-start(bf16[4,64,256]{2,1,0:T(8,128)(2,1)S(1)} %bitcast.46), channel_id=1, source_target_pairs={{0,2},{1,3},{2,0},{3,1},{4,6},{5,7},{6,4},{7,5},{8,10},{9,11},{10,... | collective-permute-start | bytes 393224 | tf_op jit(solution)/shard_map/ppermute | solution.py:17
  10.5 15.3 %collective-permute-start = (bf16[4,64,256]{2,1,0:T(8,128)(2,1)S(1)}, bf16[4,64,256]{2,1,0:T(8,128)(2,1)S(1)}, u32[]{:S(2)}, u32[]{:S(2)}) collective-permute-start(bf16[4,64,256]{2,1,0:T(8,128)(2,1)S(1)} %bitcast.47), channel_id=1, source_target_pairs={{0,1},{1,2},{2,3},{3,0},{4,5},{5,6},{6,7},{7,4},{8,9},{9,10},{10,1... | collective-permute-start | bytes 393224 | tf_op jit(solution)/shard_map/ppermute | solution.py:17
  11.8 14.9 %collective-permute-start.5 = (bf16[4,64,256]{1,2,0:T(8,128)(2,1)S(1)}, bf16[4,64,256]{1,2,0:T(8,128)(2,1)S(1)}, u32[]{:S(2)}, u32[]{:S(2)}) collective-permute-start(bf16[4,64,256]{1,2,0:T(8,128)(2,1)S(1)} %bitcast.49), channel_id=1, source_target_pairs={{0,12},{4,0},{8,4},{12,8},{1,13},{5,1},{9,5},{13,9},{2,14},{6,2},{... | collective-permute-start | bytes 393224 | tf_op jit(solution)/shard_map/ppermute | solution.py:17
  15.4 23.2 %collective-permute-start.4 = (bf16[4,64,256]{1,2,0:T(8,128)(2,1)S(1)}, bf16[4,64,256]{1,2,0:T(8,128)(2,1)S(1)}, u32[]{:S(2)}, u32[]{:S(2)}) collective-permute-start(bf16[4,64,256]{1,2,0:T(8,128)(2,1)S(1)} %bitcast.50), channel_id=1, source_target_pairs={{0,8},{4,12},{8,0},{12,4},{1,9},{5,13},{9,1},{13,5},{2,10},{6,14},... | collective-permute-start | bytes 393224 | tf_op jit(solution)/shard_map/ppermute | solution.py:17
  18.4 20.2 %collective-permute-start.3 = (bf16[4,64,256]{1,2,0:T(8,128)(2,1)S(1)}, bf16[4,64,256]{1,2,0:T(8,128)(2,1)S(1)}, u32[]{:S(2)}, u32[]{:S(2)}) collective-permute-start(bf16[4,64,256]{1,2,0:T(8,128)(2,1)S(1)} %bitcast.51), channel_id=1, source_target_pairs={{0,4},{4,8},{8,12},{12,0},{1,5},{5,9},{9,13},{13,1},{2,6},{6,10},{... | collective-permute-start | bytes 393224 | tf_op jit(solution)/shard_map/ppermute | solution.py:17
  46.8 25.4 %all-to-all-start = ((bf16[8,256,256]{2,1,0:T(8,128)(2,1)}), bf16[8,256,256]{2,1,0:T(8,128)(2,1)S(1)}, u32[]{:S(2)}, u32[]{:S(2)}) async-start(bf16[8,256,256]{2,1,0:T(8,128)(2,1)} %pad_maximum_fusion), calls=%async_computation | async-start | bytes 2097152 | tf_op jit(solution)/shard_map/all_to_all | solution.py:200
  54.9 16.3 %collective-permute-start.6 = (bf16[4,256,256]{2,1,0:T(8,128)(2,1)}, bf16[4,256,256]{2,1,0:T(8,128)(2,1)S(1)}, u32[]{:S(2)}, u32[]{:S(2)}) collective-permute-start(bf16[4,256,256]{2,1,0:T(8,128)(2,1)} %child_update.5), channel_id=1, source_target_pairs={{0,4},{4,8},{8,12},{12,0},{1,5},{5,9},{9,13},{13,1},{2,6},{6,10},{... | collective-permute-start | bytes 1572872 | tf_op jit(solution)/shard_map/ppermute | solution.py:17
  72.3 35.1 %all-to-all-start.1 = ((bf16[8,256,256]{2,1,0:T(8,128)(2,1)}), bf16[8,256,256]{2,1,0:T(8,128)(2,1)S(1)}, u32[]{:S(2)}, u32[]{:S(2)}) async-start(bf16[8,256,256]{2,1,0:T(8,128)(2,1)} %pad_maximum_fusion.1), calls=%async_computation.1 | async-start | bytes 2097152 | tf_op jit(solution)/shard_map/all_to_all | solution.py:200
  80.6 30.7 %copy-start.5 = (bf16[32,8,1,256]{3,1,2,0:T(8,128)(2,1)S(1)}, bf16[32,8,1,256]{3,1,2,0:T(8,128)(2,1)}, u32[]{:S(2)}) copy-start(bf16[32,8,1,256]{3,1,2,0:T(8,128)(2,1)} %param.15) | copy-start | bytes 393220
  80.6 25.8 %collective-permute-start.7 = (bf16[4,256,256]{2,1,0:T(8,128)(2,1)}, bf16[4,256,256]{2,1,0:T(8,128)(2,1)S(1)}, u32[]{:S(2)}, u32[]{:S(2)}) collective-permute-start(bf16[4,256,256]{2,1,0:T(8,128)(2,1)} %child_update.6), channel_id=1, source_target_pairs={{0,8},{4,12},{8,0},{12,4},{1,9},{5,13},{9,1},{13,5},{2,10},{6,14},... | collective-permute-start | bytes 1572872 | tf_op jit(solution)/shard_map/ppermute | solution.py:17
  107.4 26.4 %all-to-all-start.2 = ((bf16[8,256,256]{2,1,0:T(8,128)(2,1)}), bf16[8,256,256]{2,1,0:T(8,128)(2,1)S(1)}, u32[]{:S(2)}, u32[]{:S(2)}) async-start(bf16[8,256,256]{2,1,0:T(8,128)(2,1)} %pad_maximum_fusion.2), calls=%async_computation.2 | async-start | bytes 2097152 | tf_op jit(solution)/shard_map/all_to_all | solution.py:200
  111.2 7.3 %copy-start.4 = (bf16[64,4,1,256]{3,1,2,0:T(4,128)(2,1)S(1)}, bf16[64,4,1,256]{3,1,2,0:T(4,128)(2,1)}, u32[]{:S(2)}) copy-start(bf16[64,4,1,256]{3,1,2,0:T(4,128)(2,1)} %param.14) | copy-start | bytes 393220
  111.2 43.8 %all-gather.2.cloned.1.call-start = ((), (), s32[]{:S(2)}) async-start(), calls=%async_computation.4 | async-start | bytes 1179648 | tf_op jit(solution)/shard_map/all_gather | solution.py:185
  116.5 21.8 %copy-start.3 = (bf16[256,256]{1,0:T(8,128)(2,1)S(1)}, bf16[256,256]{1,0:T(8,128)(2,1)}, u32[]{:S(2)}) copy-start(bf16[256,256]{1,0:T(8,128)(2,1)} %param.16) | copy-start | bytes 393220
  116.5 15.0 %collective-permute-start.8 = (bf16[4,256,256]{2,1,0:T(8,128)(2,1)}, bf16[4,256,256]{2,1,0:T(8,128)(2,1)}, u32[]{:S(2)}, u32[]{:S(2)}) collective-permute-start(bf16[4,256,256]{2,1,0:T(8,128)(2,1)} %child_update.7), channel_id=1, source_target_pairs={{0,12},{4,0},{8,4},{12,8},{1,13},{5,1},{9,5},{13,9},{2,14},{6,2},{... | collective-permute-start | bytes 1572872 | tf_op jit(solution)/shard_map/ppermute | solution.py:17
  119.5 19.0 %collective-permute-start.11 = (bf16[4,64,256]{1,2,0:T(8,128)(2,1)}, bf16[4,64,256]{1,2,0:T(8,128)(2,1)}, u32[]{:S(2)}, u32[]{:S(2)}) collective-permute-start(bf16[4,64,256]{1,2,0:T(8,128)(2,1)} %bitcast.18), channel_id=1, source_target_pairs={{0,12},{4,0},{8,4},{12,8},{1,13},{5,1},{9,5},{13,9},{2,14},{6,2},{... | collective-permute-start | bytes 393224 | tf_op jit(solution)/shard_map/ppermute | solution.py:17
  119.5 32.9 %collective-permute-start.10 = (bf16[4,64,256]{1,2,0:T(8,128)(2,1)}, bf16[4,64,256]{1,2,0:T(8,128)(2,1)}, u32[]{:S(2)}, u32[]{:S(2)}) collective-permute-start(bf16[4,64,256]{1,2,0:T(8,128)(2,1)} %bitcast.18), channel_id=1, source_target_pairs={{0,8},{4,12},{8,0},{12,4},{1,9},{5,13},{9,1},{13,5},{2,10},{6,14},... | collective-permute-start | bytes 393224 | tf_op jit(solution)/shard_map/ppermute | solution.py:17
  120.9 31.5 %collective-permute-start.9 = (bf16[4,64,256]{1,2,0:T(8,128)(2,1)}, bf16[4,64,256]{1,2,0:T(8,128)(2,1)}, u32[]{:S(2)}, u32[]{:S(2)}) collective-permute-start(bf16[4,64,256]{1,2,0:T(8,128)(2,1)} %bitcast.18), channel_id=1, source_target_pairs={{0,4},{4,8},{8,12},{12,0},{1,5},{5,9},{9,13},{13,1},{2,6},{6,10},{... | collective-permute-start | bytes 393224 | tf_op jit(solution)/shard_map/ppermute | solution.py:17
  133.8 21.2 %all-to-all-start.3 = ((bf16[8,256,256]{2,1,0:T(8,128)(2,1)}), bf16[8,256,256]{2,1,0:T(8,128)(2,1)}, u32[]{:S(2)}, u32[]{:S(2)}) async-start(bf16[8,256,256]{2,1,0:T(8,128)(2,1)} %pad_maximum_fusion.3), calls=%async_computation.3 | async-start | bytes 2097152 | tf_op jit(solution)/shard_map/all_to_all | solution.py:200
  138.1 16.9 %copy-start.2 = (f32[8,1,256]{2,1,0:T(1,128)S(1)}, f32[8,1,256]{2,1,0:T(1,128)}, u32[]{:S(2)}) copy-start(f32[8,1,256]{2,1,0:T(1,128)} %refs_6_.1) | copy-start | bytes 24580
  155.0 1.2 copy-start
  156.2 1.0 copy-start.1
Sparse Core Ops, SparseCore 0:
  114.0 23.9 all-gather.1

commit v2 on v1

v2 whole, which is shorter than its diff:
```python
import functools

import jax
import jax.numpy as jnp
from jax import lax
from jax.experimental import pallas as pl
from jax.experimental.pallas import tpu as pltpu
from jax.sharding import PartitionSpec as P

F32 = jnp.float32
BF16 = jnp.bfloat16
PLANE = ("half", "col")
TRANSPOSED = (((0,), (0,)), ((), ()))


def after(value, *others):
    return lax.optimization_barrier((value, *others))[0]


def shifted(value, axis, step):
    count = lax.axis_size(axis)
    return lax.ppermute(value, axis, [(i, (i + step) % count) for i in range(count)])


def far_first(count):
    return sorted(range(1, count), key=lambda d: -d * (count - d))


def gathered(value, axis):
    count = lax.axis_size(axis)
    parts = {0: value, **{d: shifted(value, axis, d) for d in far_first(count)}}
    return [parts[d] for d in range(count)]


def chunks_of(matrix, dim, order):
    width = matrix.shape[dim] // len(order)
    return jnp.concatenate(
        [lax.dynamic_slice_in_dim(matrix, i * width, width, dim) for i in order], axis=dim
    )


def scaled_rows(inverse, parts, scaled):
    tile = inverse.shape[0]
    for l in range(parts[0].shape[0]):
        rows = jnp.concatenate([part[l] for part in parts], axis=0)
        scaled[:, l * tile : (l + 1) * tile] = jnp.dot(
            inverse, rows, preferred_element_type=F32
        ).astype(BF16)


def update_kernel(grid, picks, *refs):
    block_ref, inverse_ref = refs[:2]
    rows, cols, outs = (refs[2 + grid * i : 2 + grid * (i + 1)] for i in range(3))
    scaled = refs[-1]
    tile = inverse_ref.shape[0]
    scaled_rows(inverse_ref[...], rows, scaled)
    for d in range(grid):
        k = picks[0, d]
        col = jnp.concatenate([part[k] for part in cols], axis=0)
        update = lax.dot_general(col, scaled[...], TRANSPOSED, preferred_element_type=F32)
        for l in range(grid):
            value = block_ref[k, l].astype(F32) - update[:, l * tile : (l + 1) * tile]
            outs[d][picks[1, l]] = value.astype(BF16)


def contribution(block, inverse, rows, cols, picks):
    grid, tile = block.shape[0], block.shape[-1]
    vmem = pl.BlockSpec(memory_space=pltpu.VMEM)
    return pl.pallas_call(
        functools.partial(update_kernel, grid),
        in_specs=[pl.BlockSpec(memory_space=pltpu.SMEM)] + [vmem] * (2 + 2 * grid),
        out_specs=[vmem] * grid,
        out_shape=[jax.ShapeDtypeStruct((grid, tile, tile), BF16)] * grid,
        scratch_shapes=[pltpu.VMEM((tile, grid * tile), BF16)],
        compiler_params=pltpu.CompilerParams(vmem_limit_bytes=56 * 2**20),
        cost_estimate=pl.CostEstimate(
            flops=2 * grid * (grid + 1) * tile**3,
            bytes_accessed=4 * grid * (grid + 1) * tile * tile,
            transcendentals=0,
        ),
        name="child_update",
    )(picks, block, inverse, *rows, *cols)


def front_kernel(grid, picks, *refs):
    arrived, rows, cols = (refs[grid * i : grid * (i + 1)] for i in range(3))
    other_ref, inverse_ref, diag_ref, weave_ref, out_ref = refs[3 * grid : 3 * grid + 5]
    held, scaled, rounded, sems = refs[3 * grid + 5 :]
    tile = inverse_ref.shape[0]
    step = pl.program_id(0)
    copies = [pltpu.make_async_copy(arrived[d], held.at[d], sems.at[d]) for d in range(grid)]

    @pl.when(step == 0)
    def _():
        for copy in copies:
            copy.start()
        scaled_rows(inverse_ref[...], rows, scaled)
        for copy in copies:
            copy.wait()

    col = jnp.concatenate(
        [part[step] for part in cols] + [other_ref[d, step] for d in range(grid)], axis=0
    )
    update = lax.dot_general(col, scaled[...], TRANSPOSED, preferred_element_type=F32)
    chunks = [picks[child, step] for child in range(2)]
    height = tile // grid
    diagonal = lax.broadcasted_iota(jnp.int32, (tile, tile), 0) == lax.broadcasted_iota(
        jnp.int32, (tile, tile), 1
    )
    for q in range(grid):
        value = -update[:, q * tile : (q + 1) * tile]
        for child in range(2):
            usable = picks[2 + child, step] * picks[6 + child, q]
            piece = held[chunks[child], picks[4 + child, q]]
            value = value + jnp.where(usable > 0, piece.astype(F32), 0.0)
        rounded[q] = value.astype(BF16)

        @pl.when(picks[8, q] == step)
        def _():
            rounded[q] = (value + jnp.where(diagonal, diag_ref[0], 0.0)).astype(BF16)

    for part in range(grid):
        stacked = jnp.concatenate(
            [rounded[q, part * height : (part + 1) * height] for q in range(grid)], axis=0
        )
        woven = jnp.dot(weave_ref[...], stacked, preferred_element_type=F32)
        out_ref[0, part * height : (part + 1) * height] = woven.reshape(
            height, grid, tile
        ).astype(BF16)


def front(arrived, rows, cols, other, inverse, diag, picks):
    grid, tile = len(arrived), inverse.shape[0]
    height = tile // grid
    place = jnp.arange(tile, dtype=jnp.int32)
    weave = (place[None, :] == (place % grid * height + place // grid)[:, None]).astype(BF16)
    whole = lambda a: pl.BlockSpec(a.shape, lambda s, picks: (0,) * a.ndim)
    spec = pltpu.PrefetchScalarGridSpec(
        num_scalar_prefetch=1,
        grid=(2 * grid,),
        in_specs=[pl.BlockSpec(memory_space=pl.ANY)] * grid
        + [whole(a) for a in (*rows, *cols, other, inverse)]
        + [pl.BlockSpec((1, 1, tile), lambda s, picks: (s, 0, 0)), whole(weave)],
        out_specs=pl.BlockSpec((1, tile, grid, tile), lambda s, picks: (s, 0, 0, 0)),
        scratch_shapes=[
            pltpu.VMEM((grid, 2 * grid, tile, tile), BF16),
            pltpu.VMEM((tile, grid * tile), BF16),
            pltpu.VMEM((grid, tile, tile), BF16),
            pltpu.SemaphoreType.DMA((grid,)),
        ],
    )
    return pl.pallas_call(
        functools.partial(front_kernel, grid),
        grid_spec=spec,
        out_shape=jax.ShapeDtypeStruct((2 * grid, tile, grid, tile), BF16),
        compiler_params=pltpu.CompilerParams(vmem_limit_bytes=56 * 2**20),
        cost_estimate=pl.CostEstimate(
            flops=8 * grid * grid * tile**3,
            bytes_accessed=12 * grid * grid * tile * tile,
            transcendentals=0,
        ),
        name="front",
    )(picks, *arrived, *rows, *cols, other, inverse, diag, weave)


def shards(
    child_block,
    child_row,
    child_col,
    child_pivot_inv,
    child_map,
    parent_row,
    parent_col,
    parent_pivot_inv,
    parent_diag,
):
    grid = lax.axis_size("row")
    tile = child_pivot_inv.shape[-1]
    my_half = lax.axis_index("half")
    my_row = lax.axis_index("row")
    my_col = lax.axis_index("col")
    places = jnp.arange(grid, dtype=jnp.int32)
    shift = child_map[:, ::grid] - 2 * grid * places[None, :]
    unshift = jnp.sum(
        jnp.where(shift[:, None, :] == places[None, :, None], places[None, None, :], 0), axis=2
    )
    of_mine = lambda pair: jnp.sum(
        jnp.where(jnp.arange(2)[:, None] == my_half, pair, 0), axis=0
    )
    rows_back = [(my_row - d) % grid for d in range(grid)]
    cols_back = [(my_col - d) % grid for d in range(grid)]

    child_rows = gathered(child_row[0, :, :, 0].transpose(1, 0, 2), "row")
    child_cols = gathered(child_col[0, :, :, 0].transpose(1, 0, 2), "col")
    child_inv = chunks_of(chunks_of(child_pivot_inv[0], 0, cols_back), 1, rows_back)
    block_rows = contribution(
        child_block[0, :, 0, :, :, 0].transpose(0, 2, 1, 3),
        child_inv,
        child_rows,
        child_cols,
        jnp.stack([of_mine(unshift), (my_col + of_mine(shift)) % grid]),
    )

    arrived = {d: shifted(block_rows[d], "row", d) for d in range(1, grid)}
    arrived[0] = block_rows[0]

    parent_rows, parent_cols = after(
        (parent_row[:, :, 0].transpose(1, 0, 2), parent_col[:, :, 0].transpose(1, 0, 2)),
        block_rows[0],
    )
    parent_rows = gathered(parent_rows, "row")
    parent_cols = gathered(parent_cols, "col")
    other_cols = lax.ppermute(jnp.stack(parent_cols), "half", [(0, 1), (1, 0)])
    halves = [(my_half + e) % 2 for e in range(2)]
    parent_inv = chunks_of(
        chunks_of(parent_pivot_inv, 0, [h * grid + c for h in halves for c in cols_back]),
        1,
        rows_back,
    )

    for step in range(grid):
        row = arrived[step]
        arrived[step] = lax.all_to_all(
            jnp.concatenate([row, row]), PLANE, split_axis=0, concat_axis=0, tiled=True
        )

    targets = jnp.arange(2 * grid, dtype=jnp.int32)
    row_shift = jnp.repeat(shift, 2, axis=1)
    row_usable = (my_row < row_shift) == (targets % 2 == 1)[None, :]
    source = (my_col - shift) % grid + grid * jnp.arange(2, dtype=jnp.int32)[:, None]
    col_usable = (my_col < shift) == (my_half == 1)
    on_diagonal = jnp.where(my_row == my_col, 2 * places + my_half, -1)[None]
    wide = lambda a: jnp.pad(a.astype(jnp.int32), ((0, 0), (0, 2 * grid - a.shape[1])))
    picks = jnp.concatenate(
        [wide(a) for a in (row_shift, row_usable, source, col_usable, on_diagonal)]
    )
    return front(
        [arrived[d] for d in range(grid)],
        parent_rows,
        parent_cols,
        other_cols,
        parent_inv,
        parent_diag,
        picks,
    ).reshape(2 * grid, 1, tile, grid, 1, tile)


def solution(mesh):
    return jax.shard_map(
        shards,
        mesh=mesh,
        in_specs=(
            P("half", None, "row", None, None, "col", None),
            P("half", "row", None, "col", None),
            P("half", "col", None, "row", None),
            P("half", None, None),
            P(),
            P("row", None, ("half", "col"), None),
            P(("half", "col"), None, "row", None),
            P(),
            P(None, "row", None),
        ),
        out_specs=P(None, "row", None, None, ("half", "col"), None),
        check_vma=False,
    )
```

time: 179 us -> 147 us (0.82)
  Pallas kernels: 31.3 us -> 16.6 us
  between operations: 13.6 us -> 0.26 us
  waiting for transfers between devices: 75 us -> 67.4 us
  local copies, waits for them, and re-layouts: 11.8 us -> 18.7 us
  matrix products: 4.02 us -> 0 us
  starting transfers between devices: 30.3 us -> 32.3 us
    ppermute x12 -> x15, waiting for transfers between devices: 75 us -> 60 us  [shifted(): lax.ppermute(value, axis, [(i, (i + step) % count) for i in range(count)])]
    pallas_call x4 -> x1, Pallas kernels: 18 us -> 3.98 us  [contribution(): pl.pallas_call(functools.partial(update_kernel, grid), in_specs=[pl.Block...]
    ppermute x0 -> x1, waiting for transfers between devices: none -> 7.1 us  [shards(): other_cols = lax.ppermute(jnp.stack(parent_cols), 'half', [(0, 1), (1, 0)])]
    dot_general x2 -> x0, matrix products: 4.02 us -> none  [shards(): jnp.einsum('ab,lbj->laj', inverse, rows, preferred_element_type=F32)]
    unnamed x17 -> x54, local copies, waits for them, and re-layouts: 9.11 us -> 13.1 us
    concatenate x1 -> x2, local copies, waits for them, and re-layouts: 0.04 us -> 2.54 us  [the longest x1 1.81 us: shards(): jnp.concatenate([wide(a) for a in (row_shift, row_usable, source, col_usa...]
    concatenate x3, other arithmetic: 4 us -> 1.57 us  [chunks_of(): jnp.concatenate([lax.dynamic_slice_in_dim(matrix, i * width, width, dim)...]
    ppermute x12 -> x15, starting transfers between devices: 14.8 us -> 15.9 us  [shifted(): lax.ppermute(value, axis, [(i, (i + step) % count) for i in range(count)])]
  transfers between devices with their start and end apart: 17 -> 20, of which waited for: 5 -> 8; matrix products, arithmetic and copies ran while one was open for 11% -> 16% of each run, Pallas kernels for 8% -> 0%
where the time goes in v2:
time: 147 us; the launch traced here: 146 us
  waiting for transfers between devices  67.4 us (46%)
  starting transfers between devices  32.3 us (22%)
  local copies, waits for them, and re-layouts  18.7 us (13%)
  Pallas kernels  16.6 us (11%)
  other arithmetic  10.7 us (7%)
    ppermute x15, waiting for transfers between devices, shifted(): lax.ppermute(value, axis, [(i, (i + step) % count) for i in range(count)])  60 us
    ppermute x15, starting transfers between devices, shifted(): lax.ppermute(value, axis, [(i, (i + step) % count) for i in range(count)])  15.9 us
    all_to_all x4, starting transfers between devices, shards(): lax.all_to_all(jnp.concatenate([row, row]), PLANE, split_axis=0, concat_a...  14.9 us
    unnamed x54, local copies, waits for them, and re-layouts  13.1 us
    pallas_call x1, Pallas kernels, front(): pl.pallas_call(functools.partial(front_kernel, grid), grid_spec=spec, out...  12.6 us
    ppermute x1, waiting for transfers between devices, shards(): other_cols = lax.ppermute(jnp.stack(parent_cols), 'half', [(0, 1), (1, 0)])  7.1 us
    concatenate x4, other arithmetic, shards(): jnp.concatenate([row, row])  5.54 us
    pallas_call x1, Pallas kernels, contribution(): pl.pallas_call(functools.partial(update_kernel, grid), in_specs=[pl.Block...  3.98 us
  transfers between devices with their start and end apart: 20, of which 8 were waited for; matrix products, arithmetic and copies ran while one was open for 16% of the time, Pallas kernels for 0%

profile of v2, /device:TPU:0, one launch (start us, length us, event | category | flops | bytes accessed | tf_op | source)
XLA Modules:
  0.0 146.0 jit_solution(7330070433477406394)
XLA Ops:
  0.0 1.1 copy.36
  1.1 2.4 %collective-permute-start.5 = (bf16[4,64,256]{2,1,0:T(8,128)(2,1)S(1)}, bf16[4,64,256]{2,1,0:T(8,128)(2,1)S(1)}, u32[]{:S(2)}, u32[]{:S(2)}) collective-permute-start(bf16[4,64,256]{2,1,0:T(8,128)(2,1)S(1)} %bitcast.56), channel_id=1, source_target_pairs={{0,3},{1,0},{2,1},{3,2},{4,7},{5,4},{6,5},{7,6},{8,11},{9,8},{10,9... | collective-permute-start | bytes 393224 | tf_op jit(solution)/shard_map/ppermute | solution.py:22
  4.3 0.9 copy.37
  5.3 3.7 %collective-permute-start.2 = (bf16[4,64,256]{2,1,0:T(8,128)(2,1)S(1)}, bf16[4,64,256]{2,1,0:T(8,128)(2,1)}, u32[]{:S(2)}, u32[]{:S(2)}) collective-permute-start(bf16[4,64,256]{2,1,0:T(8,128)(2,1)S(1)} %bitcast.60), channel_id=1, source_target_pairs={{0,12},{4,0},{8,4},{12,8},{1,13},{5,1},{9,5},{13,9},{2,14},{6,2},{... | collective-permute-start | bytes 393224 | tf_op jit(solution)/shard_map/ppermute | solution.py:22
  8.9 0.8 slice.3
  9.9 0.7 select_reduce_fusion.2
  10.5 0.7 constant_dynamic-update-slice_fusion.7
  11.2 0.7 constant_dynamic-update-slice_fusion.6
  12.0 0.7 constant_dynamic-update-slice_fusion.5
  12.7 0.7 constant_dynamic-update-slice_fusion.4
  13.4 0.7 constant_dynamic-update-slice_fusion.3
  14.1 0.7 constant_dynamic-update-slice_fusion.2
  14.8 0.7 constant_dynamic-update-slice_fusion.1
  15.6 0.8 dynamic-slice_bitcast_fusion.3
  16.4 0.7 constant_dynamic-update-slice_fusion
  17.4 1.1 collective-permute-start
  19.0 1.7 %copy.33 = bf16[1,4,1,256,4,1,256]{6,3,4,1,5,2,0:T(8,128)(2,1)} copy(bf16[1,4,1,256,4,1,256]{6,4,5,3,2,1,0:T(4,128)(2,1)S(1)} %copy-done.4) | data formatting | bytes 4194304 | tf_op args[0]
  20.7 0.8 pad_maximum_fusion.6.refs_1_
  21.5 4.0 %collective-permute-done.refs_3_ = bf16[4,64,256]{2,1,0:T(8,128)(2,1)S(1)} collective-permute-done((bf16[4,64,256]{2,1,0:T(8,128)(2,1)S(1)}, bf16[4,64,256]{2,1,0:T(8,128)(2,1)S(1)}, u32[]{:S(2)}, u32[]{:S(2)}) %collective-permute-start) | collective-permute-done | bytes 131104 | tf_op jit(solution)/shard_map/ppermute | solution.py:22
  25.5 0.6 copy-done.17
  26.2 4.0 %child_update.1 = (bf16[4,256,256]{2,1,0:T(8,128)(2,1)}, bf16[4,256,256]{2,1,0:T(8,128)(2,1)}, bf16[4,256,256]{2,1,0:T(8,128)(2,1)}, bf16[4,256,256]{2,1,0:T(8,128)(2,1)}) custom-call(s32[2,4]{1,0:T(2,128)} %pad_add_fusion.picks, bf16[4,4,256,256]{3,2,1,0:T(8,128)(2,1)} %bitcast.43, bf16[256,256]{1,0:T(8,128)(2,1)} %pad_maximum_fusion.6.refs_1_, ...), custom_call_target="tpu_custom_call" | custom-call | flops 671088640 | bytes 5242880 | tf_op jit(solution)/shard_map/child_update/pallas_call | solution.py:69
  30.1 2.3 %pad_maximum_fusion = bf16[8,256,256]{2,1,0:T(8,128)(2,1)} fusion(bf16[4,256,256]{2,1,0:T(8,128)(2,1)} %get-tuple-element.11), kind=kLoop, calls=%fused_computation.1 | loop fusion | flops 524288 | bytes 1572864 | tf_op jit(solution)/shard_map/concatenate | solution.py:224
  32.4 3.6 %all-to-all-start = ((bf16[8,256,256]{2,1,0:T(8,128)(2,1)}), bf16[8,256,256]{2,1,0:T(8,128)(2,1)S(1)}, u32[]{:S(2)}, u32[]{:S(2)}) async-start(bf16[8,256,256]{2,1,0:T(8,128)(2,1)} %pad_maximum_fusion), calls=%async_computation | async-start | bytes 2097152 | tf_op jit(solution)/shard_map/all_to_all | solution.py:223
  36.1 16.0 %collective-permute-done.6 = bf16[4,256,256]{2,1,0:T(8,128)(2,1)S(1)} collective-permute-done((bf16[4,256,256]{2,1,0:T(8,128)(2,1)S(1)}, bf16[4,256,256]{2,1,0:T(8,128)(2,1)S(1)}, u32[]{:S(2)}, u32[]{:S(2)}) %collective-permute-start.6) | collective-permute-done | bytes 524320 | tf_op jit(solution)/shard_map/ppermute | solution.py:22
  52.1 1.1 pad_maximum_fusion.1
  53.2 3.9 %all-to-all-start.1 = ((bf16[8,256,256]{2,1,0:T(8,128)(2,1)}), bf16[8,256,256]{2,1,0:T(8,128)(2,1)S(1)}, u32[]{:S(2)}, u32[]{:S(2)}) async-start(bf16[8,256,256]{2,1,0:T(8,128)(2,1)} %pad_maximum_fusion.1), calls=%async_computation.1 | async-start | bytes 2097152 | tf_op jit(solution)/shard_map/all_to_all | solution.py:223
  57.1 24.3 %collective-permute-done.7 = bf16[4,256,256]{2,1,0:T(8,128)(2,1)S(1)} collective-permute-done((bf16[4,256,256]{2,1,0:T(8,128)(2,1)S(1)}, bf16[4,256,256]{2,1,0:T(8,128)(2,1)S(1)}, u32[]{:S(2)}, u32[]{:S(2)}) %collective-permute-start.7) | collective-permute-done | bytes 524320 | tf_op jit(solution)/shard_map/ppermute | solution.py:22
  81.4 1.1 pad_maximum_fusion.2
  82.5 3.9 %all-to-all-start.2 = ((bf16[8,256,256]{2,1,0:T(8,128)(2,1)}), bf16[8,256,256]{2,1,0:T(8,128)(2,1)S(1)}, u32[]{:S(2)}, u32[]{:S(2)}) async-start(bf16[8,256,256]{2,1,0:T(8,128)(2,1)} %pad_maximum_fusion.2), calls=%async_computation.2 | async-start | bytes 2097152 | tf_op jit(solution)/shard_map/all_to_all | solution.py:223
  86.4 1.6 %collective-permute-start.8 = (bf16[4,256,256]{2,1,0:T(8,128)(2,1)}, bf16[4,256,256]{2,1,0:T(8,128)(2,1)S(1)}, u32[]{:S(2)}, u32[]{:S(2)}) collective-permute-start(bf16[4,256,256]{2,1,0:T(8,128)(2,1)} %get-tuple-element.14), channel_id=1, source_target_pairs={{0,12},{4,0},{8,4},{12,8},{1,13},{5,1},{9,5},{13,9},{2,14},{6,2},{... | collective-permute-start | bytes 1572872 | tf_op jit(solution)/shard_map/ppermute | solution.py:22
  88.1 0.9 copy.35
  89.1 1.0 copy.34
  90.6 1.5 %collective-permute-start.14 = (bf16[8,32,256]{2,1,0:T(8,128)(2,1)S(1)}, bf16[8,32,256]{2,1,0:T(8,128)(2,1)S(1)}, u32[]{:S(2)}, u32[]{:S(2)}) collective-permute-start(bf16[8,32,256]{2,1,0:T(8,128)(2,1)S(1)} %bitcast.44), channel_id=1, source_target_pairs={{0,3},{1,0},{2,1},{3,2},{4,7},{5,4},{6,5},{7,6},{8,11},{9,8},{10,9... | collective-permute-start | bytes 393224 | tf_op jit(solution)/shard_map/ppermute | solution.py:22
  92.9 8.0 %collective-permute-done.8 = bf16[4,256,256]{2,1,0:T(8,128)(2,1)S(1)} collective-permute-done((bf16[4,256,256]{2,1,0:T(8,128)(2,1)}, bf16[4,256,256]{2,1,0:T(8,128)(2,1)S(1)}, u32[]{:S(2)}, u32[]{:S(2)}) %collective-permute-start.8) | collective-permute-done | bytes 524320 | tf_op jit(solution)/shard_map/ppermute | solution.py:22
  100.9 1.1 pad_maximum_fusion.3
  102.3 3.6 %all-to-all-start.3 = ((bf16[8,256,256]{2,1,0:T(8,128)(2,1)}), bf16[8,256,256]{2,1,0:T(8,128)(2,1)S(1)}, u32[]{:S(2)}, u32[]{:S(2)}) async-start(bf16[8,256,256]{2,1,0:T(8,128)(2,1)} %pad_maximum_fusion.3), calls=%async_computation.3 | async-start | bytes 2097152 | tf_op jit(solution)/shard_map/all_to_all | solution.py:223
  106.5 0.9 pad_maximum_fusion.4
  107.4 1.5 %collective-permute-start.15 = (bf16[4,8,32,256]{3,2,1,0:T(8,128)(2,1)}, bf16[4,8,32,256]{3,2,1,0:T(8,128)(2,1)S(1)}, u32[]{:S(2)}, u32[]{:S(2)}) collective-permute-start(bf16[4,8,32,256]{3,2,1,0:T(8,128)(2,1)} %pad_maximum_fusion.4), channel_id=1, source_target_pairs={{0,16},{16,0},{1,17},{17,1},{2,18},{18,2},{3,19},{19,3},{4,20},{20... | collective-permute-start | bytes 1572872 | tf_op jit(solution)/shard_map/ppermute | solution.py:213
  108.8 0.8 fusion.refs_15_
  109.6 3.4 %collective-permute-start.11 = (bf16[4,64,256]{2,1,0:T(8,128)(2,1)S(1)}, bf16[4,64,256]{2,1,0:T(8,128)(2,1)S(1)}, u32[]{:S(2)}, u32[]{:S(2)}) collective-permute-start(bf16[4,64,256]{2,1,0:T(8,128)(2,1)S(1)} %bitcast.49), channel_id=1, source_target_pairs={{0,12},{4,0},{8,4},{12,8},{1,13},{5,1},{9,5},{13,9},{2,14},{6,2},{... | collective-permute-start | bytes 393224 | tf_op jit(solution)/shard_map/ppermute | solution.py:22
  114.1 0.7 pad.14
  114.8 1.8 %concatenate.27.picks = s32[9,8]{1,0:T(8,128)} concatenate(s32[2,8]{1,0:T(2,128)S(1)} %reshape.113, s32[2,8]{1,0:T(2,128)S(1)} %get-tuple-element.35, s32[2,8]{1,0:T(2,128)S(1)} %pad.14, s32[2,8]{1,0:T(2,128)S(1)} %get-tuple-element.34, s32[1,8]{1,0:T(1,128)} %pad.17), dimensions={0} | concatenate | bytes 576 | tf_op jit(solution)/shard_map/concatenate | solution.py:234
  116.6 0.8 pad_maximum_fusion.7.refs_13_
  117.4 7.1 %collective-permute-done.10.refs_6_ = bf16[4,64,256]{2,1,0:T(8,128)(2,1)} collective-permute-done((bf16[4,64,256]{2,1,0:T(8,128)(2,1)S(1)}, bf16[4,64,256]{2,1,0:T(8,128)(2,1)}, u32[]{:S(2)}, u32[]{:S(2)}) %collective-permute-start.10) | collective-permute-done | bytes 131104 | tf_op jit(solution)/shard_map/ppermute | solution.py:22
  124.5 7.1 %collective-permute-done.15.refs_12_ = bf16[4,8,32,256]{3,2,1,0:T(8,128)(2,1)S(1)} collective-permute-done((bf16[4,8,32,256]{3,2,1,0:T(8,128)(2,1)}, bf16[4,8,32,256]{3,2,1,0:T(8,128)(2,1)S(1)}, u32[]{:S(2)}, u32[]{:S(2)}) %collective-permute-start.15) | collective-permute-done | bytes 524320 | tf_op jit(solution)/shard_map/ppermute | solution.py:213
  131.6 0.7 copy-done.10
  132.4 1.0 copy-done.3
  133.4 12.6 %front.1 = bf16[8,256,4,256]{3,2,1,0:T(4,128)(2,1)} custom-call(s32[9,8]{1,0:T(8,128)} %concatenate.27.picks, bf16[8,256,256]{2,1,0:T(8,128)(2,1)} %copy-done, bf16[8,256,256]{2,1,0:T(8,128)(2,1)} %copy-done.1, bf16[8,256,256]{2,1,0:T(8,128)(2,1)} %copy-done.2, bf16[8,256,256]{2,1,0:T(8,128)(2,1)} %copy-done.3, bf16[4,64,256]{2,1,0:T(8,128)(2,1)} %bitcast.52, ...), custom_call_target="tpu_custom_call" | custom-call | flops 2147483648 | bytes 12582912 | tf_op jit(solution)/shard_map/front/pallas_call | solution.py:152
  (78 shorter events, 5.4 us)
Async XLA Ops:
  0.0 19.0 %copy-start.4 = (bf16[1,4,1,256,4,1,256]{6,4,5,3,2,1,0:T(4,128)(2,1)S(1)}, bf16[1,4,1,256,4,1,256]{6,4,5,3,2,1,0:T(4,128)(2,1)}, u32[]{:S(2)}) copy-start(bf16[1,4,1,256,4,1,256]{6,4,5,3,2,1,0:T(4,128)(2,1)} %param.9) | copy-start | bytes 6291460
  1.1 19.6 %copy-start.11 = (bf16[1,64,4,1,256]{4,1,2,3,0:T(8,128)(2,1)}, bf16[1,64,4,1,256]{4,1,2,3,0:T(8,128)(2,1)S(1)}, u32[]{:S(2)}) copy-start(bf16[1,64,4,1,256]{4,1,2,3,0:T(8,128)(2,1)S(1)} %copy.36) | copy-start | bytes 393220
  1.1 16.3 %collective-permute-start.5 = (bf16[4,64,256]{2,1,0:T(8,128)(2,1)S(1)}, bf16[4,64,256]{2,1,0:T(8,128)(2,1)S(1)}, u32[]{:S(2)}, u32[]{:S(2)}) collective-permute-start(bf16[4,64,256]{2,1,0:T(8,128)(2,1)S(1)} %bitcast.56), channel_id=1, source_target_pairs={{0,3},{1,0},{2,1},{3,2},{4,7},{5,4},{6,5},{7,6},{8,11},{9,8},{10,9... | collective-permute-start | bytes 393224 | tf_op jit(solution)/shard_map/ppermute | solution.py:22
  3.5 17.9 %collective-permute-start.4 = (bf16[4,64,256]{2,1,0:T(8,128)(2,1)S(1)}, bf16[4,64,256]{2,1,0:T(8,128)(2,1)S(1)}, u32[]{:S(2)}, u32[]{:S(2)}) collective-permute-start(bf16[4,64,256]{2,1,0:T(8,128)(2,1)S(1)} %bitcast.57), channel_id=1, source_target_pairs={{0,2},{1,3},{2,0},{3,1},{4,6},{5,7},{6,4},{7,5},{8,10},{9,11},{10,... | collective-permute-start | bytes 393224 | tf_op jit(solution)/shard_map/ppermute | solution.py:22
  4.2 17.3 %collective-permute-start.3 = (bf16[4,64,256]{2,1,0:T(8,128)(2,1)S(1)}, bf16[4,64,256]{2,1,0:T(8,128)(2,1)S(1)}, u32[]{:S(2)}, u32[]{:S(2)}) collective-permute-start(bf16[4,64,256]{2,1,0:T(8,128)(2,1)S(1)} %bitcast.58), channel_id=1, source_target_pairs={{0,1},{1,2},{2,3},{3,0},{4,5},{5,6},{6,7},{7,4},{8,9},{9,10},{10,1... | collective-permute-start | bytes 393224 | tf_op jit(solution)/shard_map/ppermute | solution.py:22
  5.2 15.4 %copy-start.12 = (bf16[1,64,4,1,256]{4,1,2,3,0:T(8,128)(2,1)}, bf16[1,64,4,1,256]{4,1,2,3,0:T(8,128)(2,1)S(1)}, u32[]{:S(2)}) copy-start(bf16[1,64,4,1,256]{4,1,2,3,0:T(8,128)(2,1)S(1)} %copy.37) | copy-start | bytes 393220
  5.3 16.2 %collective-permute-start.2 = (bf16[4,64,256]{2,1,0:T(8,128)(2,1)S(1)}, bf16[4,64,256]{2,1,0:T(8,128)(2,1)}, u32[]{:S(2)}, u32[]{:S(2)}) collective-permute-start(bf16[4,64,256]{2,1,0:T(8,128)(2,1)S(1)} %bitcast.60), channel_id=1, source_target_pairs={{0,12},{4,0},{8,4},{12,8},{1,13},{5,1},{9,5},{13,9},{2,14},{6,2},{... | collective-permute-start | bytes 393224 | tf_op jit(solution)/shard_map/ppermute | solution.py:22
  8.9 12.6 %collective-permute-start.1 = (bf16[4,64,256]{2,1,0:T(8,128)(2,1)S(1)}, bf16[4,64,256]{2,1,0:T(8,128)(2,1)}, u32[]{:S(2)}, u32[]{:S(2)}) collective-permute-start(bf16[4,64,256]{2,1,0:T(8,128)(2,1)S(1)} %bitcast.61), channel_id=1, source_target_pairs={{0,8},{4,12},{8,0},{12,4},{1,9},{5,13},{9,1},{13,5},{2,10},{6,14},... | collective-permute-start | bytes 393224 | tf_op jit(solution)/shard_map/ppermute | solution.py:22
  17.4 3.3 %copy-start.14 = (bf16[4,64,256]{2,1,0:T(8,128)(2,1)}, bf16[4,64,256]{2,1,0:T(8,128)(2,1)S(1)}, u32[]{:S(2)}) copy-start(bf16[4,64,256]{2,1,0:T(8,128)(2,1)S(1)} %collective-permute-done.5.refs_9_) | copy-start | bytes 393220
  17.4 8.1 %collective-permute-start = (bf16[4,64,256]{2,1,0:T(8,128)(2,1)S(1)}, bf16[4,64,256]{2,1,0:T(8,128)(2,1)S(1)}, u32[]{:S(2)}, u32[]{:S(2)}) collective-permute-start(bf16[4,64,256]{2,1,0:T(8,128)(2,1)S(1)} %bitcast.62), channel_id=1, source_target_pairs={{0,4},{4,8},{8,12},{12,0},{1,5},{5,9},{9,13},{13,1},{2,6},{6,10},{... | collective-permute-start | bytes 393224 | tf_op jit(solution)/shard_map/ppermute | solution.py:22
  21.4 4.1 %copy-start.15 = (bf16[4,64,256]{2,1,0:T(8,128)(2,1)}, bf16[4,64,256]{2,1,0:T(8,128)(2,1)S(1)}, u32[]{:S(2)}) copy-start(bf16[4,64,256]{2,1,0:T(8,128)(2,1)S(1)} %collective-permute-done.4.refs_8_) | copy-start | bytes 393220
  21.4 4.1 %copy-start.16 = (bf16[4,64,256]{2,1,0:T(8,128)(2,1)}, bf16[4,64,256]{2,1,0:T(8,128)(2,1)S(1)}, u32[]{:S(2)}) copy-start(bf16[4,64,256]{2,1,0:T(8,128)(2,1)S(1)} %collective-permute-done.3.refs_7_) | copy-start | bytes 393220
  25.5 0.7 copy-start.17
  30.1 5.9 %copy-start.20 = (bf16[4,256,256]{2,1,0:T(8,128)(2,1)S(1)}, bf16[4,256,256]{2,1,0:T(8,128)(2,1)}, u32[]{:S(2)}) copy-start(bf16[4,256,256]{2,1,0:T(8,128)(2,1)} %get-tuple-element.12) | copy-start | bytes 1572868
  32.4 20.7 %all-to-all-start = ((bf16[8,256,256]{2,1,0:T(8,128)(2,1)}), bf16[8,256,256]{2,1,0:T(8,128)(2,1)S(1)}, u32[]{:S(2)}, u32[]{:S(2)}) async-start(bf16[8,256,256]{2,1,0:T(8,128)(2,1)} %pad_maximum_fusion), calls=%async_computation | async-start | bytes 2097152 | tf_op jit(solution)/shard_map/all_to_all | solution.py:223
  36.0 21.0 %copy-start.19 = (bf16[4,256,256]{2,1,0:T(8,128)(2,1)S(1)}, bf16[4,256,256]{2,1,0:T(8,128)(2,1)}, u32[]{:S(2)}) copy-start(bf16[4,256,256]{2,1,0:T(8,128)(2,1)} %get-tuple-element.13) | copy-start | bytes 1572868
  36.0 16.1 %collective-permute-start.6 = (bf16[4,256,256]{2,1,0:T(8,128)(2,1)S(1)}, bf16[4,256,256]{2,1,0:T(8,128)(2,1)S(1)}, u32[]{:S(2)}, u32[]{:S(2)}) collective-permute-start(bf16[4,256,256]{2,1,0:T(8,128)(2,1)S(1)} %copy-done.20), channel_id=1, source_target_pairs={{0,4},{4,8},{8,12},{12,0},{1,5},{5,9},{9,13},{13,1},{2,6},{6,10},{... | collective-permute-start | bytes 1572872 | tf_op jit(solution)/shard_map/ppermute | solution.py:22
  53.2 29.3 %copy-start = (bf16[8,256,256]{2,1,0:T(8,128)(2,1)}, bf16[8,256,256]{2,1,0:T(8,128)(2,1)S(1)}, u32[]{:S(2)}) copy-start(bf16[8,256,256]{2,1,0:T(8,128)(2,1)S(1)} %all-to-all-done.refs_0_) | copy-start | bytes 3145732
  53.2 29.3 %all-to-all-start.1 = ((bf16[8,256,256]{2,1,0:T(8,128)(2,1)}), bf16[8,256,256]{2,1,0:T(8,128)(2,1)S(1)}, u32[]{:S(2)}, u32[]{:S(2)}) async-start(bf16[8,256,256]{2,1,0:T(8,128)(2,1)} %pad_maximum_fusion.1), calls=%async_computation.1 | async-start | bytes 2097152 | tf_op jit(solution)/shard_map/all_to_all | solution.py:223
  57.1 24.4 %collective-permute-start.7 = (bf16[4,256,256]{2,1,0:T(8,128)(2,1)S(1)}, bf16[4,256,256]{2,1,0:T(8,128)(2,1)S(1)}, u32[]{:S(2)}, u32[]{:S(2)}) collective-permute-start(bf16[4,256,256]{2,1,0:T(8,128)(2,1)S(1)} %copy-done.19), channel_id=1, source_target_pairs={{0,8},{4,12},{8,0},{12,4},{1,9},{5,13},{9,1},{13,5},{2,10},{6,14},... | collective-permute-start | bytes 1572872 | tf_op jit(solution)/shard_map/ppermute | solution.py:22
  82.5 19.5 %copy-start.1 = (bf16[8,256,256]{2,1,0:T(8,128)(2,1)}, bf16[8,256,256]{2,1,0:T(8,128)(2,1)S(1)}, u32[]{:S(2)}) copy-start(bf16[8,256,256]{2,1,0:T(8,128)(2,1)S(1)} %all-to-all-done.1.refs_1_) | copy-start | bytes 3145732
  82.5 19.7 %all-to-all-start.2 = ((bf16[8,256,256]{2,1,0:T(8,128)(2,1)}), bf16[8,256,256]{2,1,0:T(8,128)(2,1)S(1)}, u32[]{:S(2)}, u32[]{:S(2)}) async-start(bf16[8,256,256]{2,1,0:T(8,128)(2,1)} %pad_maximum_fusion.2), calls=%async_computation.2 | async-start | bytes 2097152 | tf_op jit(solution)/shard_map/all_to_all | solution.py:223
  86.4 14.5 %collective-permute-start.8 = (bf16[4,256,256]{2,1,0:T(8,128)(2,1)}, bf16[4,256,256]{2,1,0:T(8,128)(2,1)S(1)}, u32[]{:S(2)}, u32[]{:S(2)}) collective-permute-start(bf16[4,256,256]{2,1,0:T(8,128)(2,1)} %get-tuple-element.14), channel_id=1, source_target_pairs={{0,12},{4,0},{8,4},{12,8},{1,13},{5,1},{9,5},{13,9},{2,14},{6,2},{... | collective-permute-start | bytes 1572872 | tf_op jit(solution)/shard_map/ppermute | solution.py:22
  89.1 24.0 %copy-start.6 = (bf16[64,4,1,256]{3,0,1,2:T(8,128)(2,1)}, bf16[64,4,1,256]{3,0,1,2:T(8,128)(2,1)S(1)}, u32[]{:S(2)}) copy-start(bf16[64,4,1,256]{3,0,1,2:T(8,128)(2,1)S(1)} %copy.35) | copy-start | bytes 393220
  90.1 17.3 %copy-start.5 = (bf16[32,8,1,256]{3,0,1,2:T(8,128)(2,1)}, bf16[32,8,1,256]{3,0,1,2:T(8,128)(2,1)S(1)}, u32[]{:S(2)}) copy-start(bf16[32,8,1,256]{3,0,1,2:T(8,128)(2,1)S(1)} %copy.34) | copy-start | bytes 393220
  90.6 15.3 %collective-permute-start.14 = (bf16[8,32,256]{2,1,0:T(8,128)(2,1)S(1)}, bf16[8,32,256]{2,1,0:T(8,128)(2,1)S(1)}, u32[]{:S(2)}, u32[]{:S(2)}) collective-permute-start(bf16[8,32,256]{2,1,0:T(8,128)(2,1)S(1)} %bitcast.44), channel_id=1, source_target_pairs={{0,3},{1,0},{2,1},{3,2},{4,7},{5,4},{6,5},{7,6},{8,11},{9,8},{10,9... | collective-permute-start | bytes 393224 | tf_op jit(solution)/shard_map/ppermute | solution.py:22
  92.1 14.4 %collective-permute-start.13 = (bf16[8,32,256]{2,1,0:T(8,128)(2,1)S(1)}, bf16[8,32,256]{2,1,0:T(8,128)(2,1)S(1)}, u32[]{:S(2)}, u32[]{:S(2)}) collective-permute-start(bf16[8,32,256]{2,1,0:T(8,128)(2,1)S(1)} %bitcast.45), channel_id=1, source_target_pairs={{0,2},{1,3},{2,0},{3,1},{4,6},{5,7},{6,4},{7,5},{8,10},{9,11},{10,... | collective-permute-start | bytes 393224 | tf_op jit(solution)/shard_map/ppermute | solution.py:22
  92.7 13.8 %collective-permute-start.12 = (bf16[8,32,256]{2,1,0:T(8,128)(2,1)S(1)}, bf16[8,32,256]{2,1,0:T(8,128)(2,1)S(1)}, u32[]{:S(2)}, u32[]{:S(2)}) collective-permute-start(bf16[8,32,256]{2,1,0:T(8,128)(2,1)S(1)} %bitcast.46), channel_id=1, source_target_pairs={{0,1},{1,2},{2,3},{3,0},{4,5},{5,6},{6,7},{7,4},{8,9},{9,10},{10,1... | collective-permute-start | bytes 393224 | tf_op jit(solution)/shard_map/ppermute | solution.py:22
  102.0 3.9 %copy-start.18 = (pred[8]{0:T(512)(128)(4,1)S(1)}, pred[8]{0:T(512)(128)(4,1)}, u32[]{:S(2)}) copy-start(pred[8]{0:T(512)(128)(4,1)} %fusion.7) | copy-start | bytes 28
  102.2 29.3 %copy-start.2 = (bf16[8,256,256]{2,1,0:T(8,128)(2,1)}, bf16[8,256,256]{2,1,0:T(8,128)(2,1)S(1)}, u32[]{:S(2)}) copy-start(bf16[8,256,256]{2,1,0:T(8,128)(2,1)S(1)} %all-to-all-done.2.refs_2_) | copy-start | bytes 3145732
  102.3 29.3 %all-to-all-start.3 = ((bf16[8,256,256]{2,1,0:T(8,128)(2,1)}), bf16[8,256,256]{2,1,0:T(8,128)(2,1)S(1)}, u32[]{:S(2)}, u32[]{:S(2)}) async-start(bf16[8,256,256]{2,1,0:T(8,128)(2,1)} %pad_maximum_fusion.3), calls=%async_computation.3 | async-start | bytes 2097152 | tf_op jit(solution)/shard_map/all_to_all | solution.py:223
  105.9 25.7 %copy-start.7 = (bf16[8,32,256]{2,1,0:T(8,128)(2,1)}, bf16[8,32,256]{2,1,0:T(8,128)(2,1)S(1)}, u32[]{:S(2)}) copy-start(bf16[8,32,256]{2,1,0:T(8,128)(2,1)S(1)} %collective-permute-done.14.refs_11_) | copy-start | bytes 393220
  106.5 25.1 %copy-start.8 = (bf16[8,32,256]{2,1,0:T(8,128)(2,1)}, bf16[8,32,256]{2,1,0:T(8,128)(2,1)S(1)}, u32[]{:S(2)}) copy-start(bf16[8,32,256]{2,1,0:T(8,128)(2,1)S(1)} %collective-permute-done.13.refs_10_) | copy-start | bytes 393220
  106.5 25.1 %copy-start.9 = (bf16[8,32,256]{2,1,0:T(8,128)(2,1)}, bf16[8,32,256]{2,1,0:T(8,128)(2,1)S(1)}, u32[]{:S(2)}) copy-start(bf16[8,32,256]{2,1,0:T(8,128)(2,1)S(1)} %collective-permute-done.12.refs_9_) | copy-start | bytes 393220
  107.4 24.2 %collective-permute-start.15 = (bf16[4,8,32,256]{3,2,1,0:T(8,128)(2,1)}, bf16[4,8,32,256]{3,2,1,0:T(8,128)(2,1)S(1)}, u32[]{:S(2)}, u32[]{:S(2)}) collective-permute-start(bf16[4,8,32,256]{3,2,1,0:T(8,128)(2,1)} %pad_maximum_fusion.4), channel_id=1, source_target_pairs={{0,16},{16,0},{1,17},{17,1},{2,18},{18,2},{3,19},{19,3},{4,20},{20... | collective-permute-start | bytes 1572872 | tf_op jit(solution)/shard_map/ppermute | solution.py:213
  109.6 7.8 %collective-permute-start.11 = (bf16[4,64,256]{2,1,0:T(8,128)(2,1)S(1)}, bf16[4,64,256]{2,1,0:T(8,128)(2,1)S(1)}, u32[]{:S(2)}, u32[]{:S(2)}) collective-permute-start(bf16[4,64,256]{2,1,0:T(8,128)(2,1)S(1)} %bitcast.49), channel_id=1, source_target_pairs={{0,12},{4,0},{8,4},{12,8},{1,13},{5,1},{9,5},{13,9},{2,14},{6,2},{... | collective-permute-start | bytes 393224 | tf_op jit(solution)/shard_map/ppermute | solution.py:22
  113.0 11.4 %collective-permute-start.10 = (bf16[4,64,256]{2,1,0:T(8,128)(2,1)S(1)}, bf16[4,64,256]{2,1,0:T(8,128)(2,1)}, u32[]{:S(2)}, u32[]{:S(2)}) collective-permute-start(bf16[4,64,256]{2,1,0:T(8,128)(2,1)S(1)} %bitcast.50), channel_id=1, source_target_pairs={{0,8},{4,12},{8,0},{12,4},{1,9},{5,13},{9,1},{13,5},{2,10},{6,14},... | collective-permute-start | bytes 393224 | tf_op jit(solution)/shard_map/ppermute | solution.py:22
  113.0 11.4 %collective-permute-start.9 = (bf16[4,64,256]{2,1,0:T(8,128)(2,1)S(1)}, bf16[4,64,256]{2,1,0:T(8,128)(2,1)}, u32[]{:S(2)}, u32[]{:S(2)}) collective-permute-start(bf16[4,64,256]{2,1,0:T(8,128)(2,1)S(1)} %bitcast.51), channel_id=1, source_target_pairs={{0,4},{4,8},{8,12},{12,0},{1,5},{5,9},{9,13},{13,1},{2,6},{6,10},{... | collective-permute-start | bytes 393224 | tf_op jit(solution)/shard_map/ppermute | solution.py:22
  117.4 14.2 %copy-start.13 = (bf16[4,64,256]{2,1,0:T(8,128)(2,1)}, bf16[4,64,256]{2,1,0:T(8,128)(2,1)S(1)}, u32[]{:S(2)}) copy-start(bf16[4,64,256]{2,1,0:T(8,128)(2,1)S(1)} %collective-permute-done.11.refs_7_) | copy-start | bytes 393220
  131.6 0.8 copy-start.10
  132.4 1.0 copy-start.3

commit v3 on v2

v3 whole, which is shorter than its diff:
```python
import functools

import jax
import jax.numpy as jnp
from jax import lax
from jax.experimental import pallas as pl
from jax.experimental.pallas import tpu as pltpu
from jax.sharding import PartitionSpec as P

F32 = jnp.float32
BF16 = jnp.bfloat16
PLANE = ("half", "col")
TRANSPOSED = (((0,), (0,)), ((), ()))


def after(value, *others):
    return lax.optimization_barrier((value, *others))[0]


def shifted(value, axis, step):
    count = lax.axis_size(axis)
    return lax.ppermute(value, axis, [(i, (i + step) % count) for i in range(count)])


def exchanged(value, axis, mask):
    return lax.ppermute(value, axis, [(i, i ^ mask) for i in range(lax.axis_size(axis))])


def far_first(count):
    return sorted(range(1, count), key=lambda d: -d * (count - d))


def gathered(value, axis):
    count = lax.axis_size(axis)
    parts = {0: value, **{d: shifted(value, axis, d) for d in far_first(count)}}
    return [parts[d] for d in range(count)]


def gathered_by_bits(value, axis):
    count = lax.axis_size(axis)
    parts = {0: value}
    mask = count // 2
    while mask:
        parts.update({e ^ mask: exchanged(part, axis, mask) for e, part in parts.items()})
        mask //= 2
    return [parts[e] for e in range(count)]


def reordered(matrix, row_chunks, col_chunks):
    size = matrix.shape[0]
    place = jnp.arange(size, dtype=jnp.int32)

    def chooser(chunks):
        width = size // len(chunks)
        wanted = (jnp.stack(chunks)[:, None] * width + jnp.arange(width)).reshape(size, 1)
        return (wanted == place).astype(BF16)

    if row_chunks is not None:
        matrix = jnp.dot(chooser(row_chunks), matrix)
    return jnp.dot(matrix, chooser(col_chunks).T)


def scaled_rows(inverse, parts, scaled):
    tile = inverse.shape[0]
    for l in range(parts[0].shape[0]):
        rows = jnp.concatenate([part[l] for part in parts], axis=0)
        scaled[:, l * tile : (l + 1) * tile] = jnp.dot(
            inverse, rows, preferred_element_type=F32
        ).astype(BF16)


def update_kernel(grid, picks, *refs):
    block_ref, inverse_ref = refs[:2]
    rows, cols, outs = (refs[2 + grid * i : 2 + grid * (i + 1)] for i in range(3))
    scaled = refs[-1]
    tile = inverse_ref.shape[0]
    width = tile // grid
    scaled_rows(inverse_ref[...], rows, scaled)
    for d in range(grid):
        k = picks[0, d]
        start = pl.multiple_of(k * width, width)
        col = jnp.concatenate([part[pl.ds(start, width)] for part in cols], axis=0)
        update = lax.dot_general(col, scaled[...], TRANSPOSED, preferred_element_type=F32)
        for l in range(grid):
            value = block_ref[k, l].astype(F32) - update[:, l * tile : (l + 1) * tile]
            value = value.astype(BF16)
            outs[d][picks[1, l]] = value
            if d == 0:
                outs[d][grid + picks[1, l]] = value


def contribution(block, inverse, rows, cols, picks):
    grid, tile = block.shape[0], block.shape[-1]
    vmem = pl.BlockSpec(memory_space=pltpu.VMEM)
    return pl.pallas_call(
        functools.partial(update_kernel, grid),
        in_specs=[pl.BlockSpec(memory_space=pltpu.SMEM)] + [vmem] * (2 + 2 * grid),
        out_specs=[vmem] * grid,
        out_shape=[
            jax.ShapeDtypeStruct((grid if d else 2 * grid, tile, tile), BF16) for d in range(grid)
        ],
        scratch_shapes=[pltpu.VMEM((tile, grid * tile), BF16)],
        compiler_params=pltpu.CompilerParams(vmem_limit_bytes=56 * 2**20),
        cost_estimate=pl.CostEstimate(
            flops=2 * grid * (grid + 1) * tile**3,
            bytes_accessed=4 * grid * (grid + 1) * tile * tile,
            transcendentals=0,
        ),
        name="child_update",
    )(picks, block, inverse, *rows, *cols)


def panels_kernel(grid, inverse_ref, *refs):
    rows, cols = refs[:grid], refs[grid : 2 * grid]
    other_ref, scaled, turned = refs[2 * grid :]
    tile = inverse_ref.shape[0]
    width = tile // (2 * grid)
    scaled_rows(inverse_ref[...], rows, scaled)
    for k in range(2 * grid):
        here = slice(tile + k * width, tile + (k + 1) * width)
        there = slice(k * width, (k + 1) * width)
        col = [part[here] for part in cols] + [other_ref[e, there] for e in range(grid)]
        turned[k] = jnp.concatenate(col, axis=0).T


def panels(inverse, rows, cols, other):
    grid, tile = len(rows), inverse.shape[0]
    vmem = pl.BlockSpec(memory_space=pltpu.VMEM)
    return pl.pallas_call(
        functools.partial(panels_kernel, grid),
        in_specs=[vmem] * (2 + 2 * grid),
        out_specs=[vmem] * 2,
        out_shape=[
            jax.ShapeDtypeStruct((tile, grid * tile), BF16),
            jax.ShapeDtypeStruct((2 * grid, tile, tile), BF16),
        ],
        compiler_params=pltpu.CompilerParams(vmem_limit_bytes=56 * 2**20),
        cost_estimate=pl.CostEstimate(
            flops=2 * grid * tile**3, bytes_accessed=12 * grid * tile * tile, transcendentals=0
        ),
        name="parent_panels",
    )(inverse, *rows, *cols, other)


def front_kernel(where, picks, *refs):
    grid = len(where)
    count = 1 + max(i for i, _ in where)
    arrived = refs[:count]
    col_ref, scaled_ref, diag_ref, weave_ref, out_ref, held, sems = refs[count:]
    tile = weave_ref.shape[0]
    step = pl.program_id(0)
    copies = [
        pltpu.make_async_copy(arrived[i].at[:, j], held.at[d], sems.at[d])
        for d, (i, j) in enumerate(where)
    ]

    @pl.when(step == 0)
    def _():
        for copy in copies:
            copy.start()

    for d in range(grid):

        @pl.when(picks[9, d] == step)
        def _():
            copies[d].wait()

    update = jnp.dot(col_ref[0], scaled_ref[...], preferred_element_type=F32)
    height = tile // grid
    lanes = 128 if height <= 128 else tile
    for part in range(grid):
        rows = slice(part * height, (part + 1) * height)
        near = part * height // lanes * lanes
        on = lax.broadcasted_iota(jnp.int32, (height, lanes), 0) + (
            part * height - near
        ) == lax.broadcasted_iota(jnp.int32, (height, lanes), 1)
        stacked = []
        for q in range(grid):
            value = -update[rows, q * tile : (q + 1) * tile]
            for child in range(2):
                usable = picks[2 + child, step] * picks[6 + child, q]
                piece = held[picks[child, step], picks[4 + child, q], rows]
                value = value + jnp.where(usable > 0, piece.astype(F32), 0.0)
            entries = jnp.where(picks[8, q] == step, diag_ref[0, :, near : near + lanes], 0.0)
            bands = [value[:, at : at + lanes] for at in range(0, tile, lanes)]
            bands[near // lanes] += jnp.where(on, entries, 0.0)
            stacked.append(jnp.concatenate(bands, axis=1).astype(BF16))
        woven = jnp.dot(
            weave_ref[...], jnp.concatenate(stacked, axis=0), preferred_element_type=F32
        )
        out_ref[0, rows] = woven.reshape(height, grid, tile).astype(BF16)


def front(arrived, where, col, scaled, diag, picks):
    grid, tile = len(where), col.shape[-1]
    height = tile // grid
    place = jnp.arange(tile, dtype=jnp.int32)
    weave = (place[None, :] == (place % grid * height + place // grid)[:, None]).astype(BF16)
    spec = pltpu.PrefetchScalarGridSpec(
        num_scalar_prefetch=1,
        grid=(2 * grid,),
        in_specs=[pl.BlockSpec(memory_space=pl.ANY)] * len(arrived)
        + [
            pl.BlockSpec((1, tile, tile), lambda s, picks: (s, 0, 0)),
            pl.BlockSpec((tile, grid * tile), lambda s, picks: (0, 0)),
            pl.BlockSpec((1, 1, tile), lambda s, picks: (s, 0, 0)),
            pl.BlockSpec((tile, tile), lambda s, picks: (0, 0)),
        ],
        out_specs=pl.BlockSpec((1, tile, grid, tile), lambda s, picks: (s, 0, 0, 0)),
        scratch_shapes=[
            pltpu.VMEM((grid, 2 * grid, tile, tile), BF16),
            pltpu.SemaphoreType.DMA((grid,)),
        ],
    )
    return pl.pallas_call(
        functools.partial(front_kernel, where),
        grid_spec=spec,
        out_shape=jax.ShapeDtypeStruct((2 * grid, tile, grid, tile), BF16),
        compiler_params=pltpu.CompilerParams(vmem_limit_bytes=56 * 2**20),
        cost_estimate=pl.CostEstimate(
            flops=8 * grid * grid * tile**3,
            bytes_accessed=12 * grid * grid * tile * tile,
            transcendentals=0,
        ),
        name="front",
    )(picks, *arrived, col, scaled, diag, weave)


def to_plane(*block_rows):
    return lax.all_to_all(
        jnp.concatenate([jnp.stack(block_rows, axis=1)] * 2),
        PLANE,
        split_axis=0,
        concat_axis=0,
        tiled=True,
    )


def shards(
    child_block,
    child_row,
    child_col,
    child_pivot_inv,
    child_map,
    parent_row,
    parent_col,
    parent_pivot_inv,
    parent_diag,
):
    grid = lax.axis_size("row")
    tile = child_pivot_inv.shape[-1]
    my_half = lax.axis_index("half")
    my_row = lax.axis_index("row")
    my_col = lax.axis_index("col")
    places = jnp.arange(grid, dtype=jnp.int32)
    shift = child_map[:, ::grid] - 2 * grid * places[None, :]
    unshift = jnp.sum(
        jnp.where(shift[:, None, :] == places[None, :, None], places[None, None, :], 0), axis=2
    )
    of_mine = lambda pair: jnp.sum(
        jnp.where(jnp.arange(2)[:, None] == my_half, pair, 0), axis=0
    )
    row_chunks = [(my_row - d) % grid for d in range(grid)]
    col_chunks = [my_col ^ e for e in range(grid)]
    plane_chunks = [(my_half ^ h) * grid + c for h in range(2) for c in col_chunks]

    child_rows = gathered(child_row[0, :, :, 0].transpose(1, 0, 2), "row")
    cols = gathered_by_bits(
        jnp.concatenate(
            [
                child_col[0, :, :, 0].transpose(1, 0, 2).reshape(tile, tile),
                parent_col[:, :, 0].transpose(1, 0, 2).reshape(tile, tile),
            ]
        ),
        "col",
    )
    other_cols = exchanged(jnp.stack([part[tile:] for part in cols]), "half", 1)
    block_rows = contribution(
        child_block[0, :, 0, :, :, 0].transpose(0, 2, 1, 3),
        reordered(child_pivot_inv[0], col_chunks, row_chunks),
        child_rows,
        cols,
        jnp.stack([of_mine(unshift), (my_col + of_mine(shift)) % grid]),
    )

    far = grid // 2
    first = [d for d in range(1, grid) if d != far]
    moved = lax.optimization_barrier([shifted(block_rows[d], "row", d) for d in first])
    staying = lax.all_to_all(
        block_rows[0][:, None], PLANE, split_axis=0, concat_axis=0, tiled=True
    )
    last = shifted(after(block_rows[far], moved), "row", far)
    middle = to_plane(*after(moved, other_cols, staying))
    parent_rows = gathered(after(parent_row[:, :, 0].transpose(1, 0, 2), last), "row")
    ending = to_plane(after(last, middle))
    scaled, turned = panels(
        reordered(parent_pivot_inv, plane_chunks, row_chunks), parent_rows, cols, other_cols
    )
    where = {0: (0, 0), far: (2, 0), **{d: (1, i) for i, d in enumerate(first)}}

    targets = jnp.arange(2 * grid, dtype=jnp.int32)
    row_shift = jnp.repeat(shift, 2, axis=1)
    row_usable = (my_row < row_shift) == (targets % 2 == 1)[None, :]
    source = (my_col - shift) % grid + grid * jnp.arange(2, dtype=jnp.int32)[:, None]
    col_usable = (my_col < shift) == (my_half == 1)
    on_diagonal = jnp.where(my_row == my_col, 2 * places + my_half, -1)[None]
    first_used = 2 * jnp.min(unshift, axis=0)[None]
    wide = lambda a: jnp.pad(a.astype(jnp.int32), ((0, 0), (0, 2 * grid - a.shape[1])))
    picks = jnp.concatenate(
        [wide(a) for a in (row_shift, row_usable, source, col_usable, on_diagonal, first_used)]
    )
    return front(
        [staying, middle, ending],
        [where[d] for d in range(grid)],
        turned,
        scaled,
        parent_diag,
        picks,
    ).reshape(2 * grid, 1, tile, grid, 1, tile)


def solution(mesh):
    return jax.shard_map(
        shards,
        mesh=mesh,
        in_specs=(
            P("half", None, "row", None, None, "col", None),
            P("half", "row", None, "col", None),
            P("half", "col", None, "row", None),
            P("half", None, None),
            P(),
            P("row", None, ("half", "col"), None),
            P(("half", "col"), None, "row", None),
            P(),
            P(None, "row", None),
        ),
        out_specs=P(None, "row", None, None, ("half", "col"), None),
        check_vma=False,
    )
```

time: 147 us -> 129 us (0.88)
  waiting for transfers between devices: 67.4 us -> 59.3 us
  other arithmetic: 10.7 us -> 4.94 us
  local copies, waits for them, and re-layouts: 18.7 us -> 13.4 us
  starting transfers between devices: 32.3 us -> 28.8 us
  matrix products: 0 us -> 2.98 us
  Pallas kernels: 16.6 us -> 19.1 us
    unnamed x54 -> x47, local copies, waits for them, and re-layouts: 13.1 us -> 7.5 us
    concatenate x7 -> x3, other arithmetic: 7.11 us -> 2.8 us  [the longest x2 2.78 us: to_plane(): jnp.concatenate([jnp.stack(block_rows, axis=1)] * 2)]
    ppermute x1 -> x4, waiting for transfers between devices: 7.1 us -> 3.14 us  [exchanged(): lax.ppermute(value, axis, [(i, i ^ mask) for i in range(lax.axis_size(axi...]
    ppermute x15 -> x9, waiting for transfers between devices: 60 us -> 56.2 us  [shifted(): lax.ppermute(value, axis, [(i, (i + step) % count) for i in range(count)])]
    all_to_all x4 -> x3, starting transfers between devices: 14.9 us -> 11.7 us  [the longest x2 7.82 us: to_plane(): lax.all_to_all(jnp.concatenate([jnp.stack(block_rows, axis=1)] * 2), PLAN...]
    dot_general x0 -> x2, matrix products: none -> 2.98 us  [reordered(): return jnp.dot(matrix, chooser(col_chunks).T)]
    ppermute x15 -> x9, starting transfers between devices: 15.9 us -> 13.4 us  [shifted(): lax.ppermute(value, axis, [(i, (i + step) % count) for i in range(count)])]
    ppermute x1 -> x4, starting transfers between devices: 1.47 us -> 3.64 us  [exchanged(): lax.ppermute(value, axis, [(i, i ^ mask) for i in range(lax.axis_size(axi...]
  transfers between devices with their start and end apart: 20 -> 16, of which waited for: 8 -> 6; matrix products, arithmetic and copies ran while one was open for 16% -> 11% of each run, Pallas kernels for 0% -> 2%
where the time goes in v3:
time: 129 us
  waiting for transfers between devices  59.3 us (46%)
  starting transfers between devices  28.8 us (22%)
  Pallas kernels  19.1 us (15%)
  local copies, waits for them, and re-layouts  13.4 us (10%)
  other arithmetic  4.94 us (4%)
  matrix products  2.98 us (2%)
    ppermute x9, waiting for transfers between devices, shifted(): lax.ppermute(value, axis, [(i, (i + step) % count) for i in range(count)])  56.2 us
    ppermute x9, starting transfers between devices, shifted(): lax.ppermute(value, axis, [(i, (i + step) % count) for i in range(count)])  13.4 us
    pallas_call x1, Pallas kernels, front(): pl.pallas_call(functools.partial(front_kernel, where), grid_spec=spec, ou...  11.6 us
    all_to_all x2, starting transfers between devices, to_plane(): lax.all_to_all(jnp.concatenate([jnp.stack(block_rows, axis=1)] * 2), PLAN...  7.82 us
    unnamed x47, local copies, waits for them, and re-layouts  7.5 us
    pallas_call x1, Pallas kernels, contribution(): pl.pallas_call(functools.partial(update_kernel, grid), in_specs=[pl.Block...  4.32 us
    all_to_all x1, starting transfers between devices, shards(): lax.all_to_all(block_rows[0][:, None], PLANE, split_axis=0, concat_axis=0...  3.91 us
    ppermute x4, starting transfers between devices, exchanged(): lax.ppermute(value, axis, [(i, i ^ mask) for i in range(lax.axis_size(axi...  3.64 us
  transfers between devices with their start and end apart: 16, of which 6 were waited for; matrix products, arithmetic and copies ran while one was open for 11% of the time, Pallas kernels for 2%

profile of v3, /device:TPU:0, one launch (start us, length us, event | category | flops | bytes accessed | tf_op | source)
XLA Modules:
  0.0 128.8 jit_solution(15013199044079377374)
XLA Ops:
  0.0 1.0 copy.36
  1.0 5.1 %collective-permute-start.2 = (bf16[4,64,256]{2,1,0:T(8,128)(2,1)S(1)}, bf16[4,64,256]{2,1,0:T(8,128)(2,1)S(1)}, u32[]{:S(2)}, u32[]{:S(2)}) collective-permute-start(bf16[4,64,256]{2,1,0:T(8,128)(2,1)S(1)} %bitcast.68), channel_id=1, source_target_pairs={{0,12},{4,0},{8,4},{12,8},{1,13},{5,1},{9,5},{13,9},{2,14},{6,2},{... | collective-permute-start | bytes 393224 | tf_op jit(solution)/shard_map/ppermute | solution.py:22
  6.1 1.0 collective-permute-start
  7.1 0.9 copy.27
  8.0 0.9 copy.26
  9.0 1.6 %collective-permute-start.4 = (bf16[512,256]{1,0:T(8,128)(2,1)S(1)}, bf16[512,256]{1,0:T(8,128)(2,1)S(1)}, u32[]{:S(2)}, u32[]{:S(2)}) collective-permute-start(bf16[512,256]{1,0:T(8,128)(2,1)S(1)} %pad_maximum_fusion.2.refs_6_.refs_4_), channel_id=1, source_target_pairs={{0,2},{1,3},{2,0},{3,1},{4,6},{5,7},{6,4},{7,5},{8,10},{9,11},{10,... | collective-permute-start | bytes 786440 | tf_op jit(solution)/shard_map/ppermute | solution.py:26
  10.6 0.8 slice.12
  11.3 0.1 select_reduce_fusion
  11.5 0.1 add_multiply_fusion
  11.8 0.1 select_reduce_fusion.2
  11.9 0.1 add.214
  12.0 0.1 add.222
  12.1 1.0 fusion.3.refs_1_
  13.1 3.1 %collective-permute-done.4.refs_8_.refs_6_ = bf16[512,256]{1,0:T(8,128)(2,1)S(1)} collective-permute-done((bf16[512,256]{1,0:T(8,128)(2,1)S(1)}, bf16[512,256]{1,0:T(8,128)(2,1)S(1)}, u32[]{:S(2)}, u32[]{:S(2)}) %collective-permute-start.4) | collective-permute-done | bytes 262176 | tf_op jit(solution)/shard_map/ppermute | solution.py:26
  16.3 0.6 pad_add_fusion.picks
  16.9 3.3 %copy.34 = bf16[1,4,1,256,4,1,256]{6,3,4,1,5,2,0:T(8,128)(2,1)} copy(bf16[1,4,1,256,4,1,256]{6,4,5,3,2,1,0:T(4,128)(2,1)} %param.9) | data formatting | bytes 4194304 | tf_op args[0]
  20.3 0.6 copy-done.12
  21.0 0.1 copy-done.6
  21.1 4.3 %child_update.1 = (bf16[8,256,256]{2,1,0:T(8,128)(2,1)}, bf16[4,256,256]{2,1,0:T(8,128)(2,1)}, bf16[4,256,256]{2,1,0:T(8,128)(2,1)}, bf16[4,256,256]{2,1,0:T(8,128)(2,1)}) custom-call(s32[2,4]{1,0:T(2,128)} %pad_add_fusion.picks, bf16[4,4,256,256]{3,2,1,0:T(8,128)(2,1)} %bitcast.63, bf16[256,256]{1,0:T(8,128)(2,1)} %fusion.3.refs_1_, ...), custom_call_target="tpu_custom_call" | custom-call | flops 671088640 | bytes 5242880 | tf_op jit(solution)/shard_map/child_update/pallas_call | solution.py:95
  25.5 3.9 %all-to-all-start = ((bf16[8,1,256,256]{3,2,1,0:T(8,128)(2,1)}), bf16[8,1,256,256]{3,2,1,0:T(8,128)(2,1)S(1)}, u32[]{:S(2)}, u32[]{:S(2)}) async-start(bf16[8,1,256,256]{3,2,1,0:T(8,128)(2,1)} %bitcast.66), calls=%async_computation | async-start | bytes 2097152 | tf_op jit(solution)/shard_map/all_to_all | solution.py:289
  29.4 2.5 %collective-permute-start.6 = (bf16[4,256,256]{2,1,0:T(8,128)(2,1)}, bf16[4,256,256]{2,1,0:T(8,128)(2,1)S(1)}, u32[]{:S(2)}, u32[]{:S(2)}) collective-permute-start(bf16[4,256,256]{2,1,0:T(8,128)(2,1)} %get-tuple-element.19), channel_id=1, source_target_pairs={{0,4},{4,8},{8,12},{12,0},{1,5},{5,9},{9,13},{13,1},{2,6},{6,10},{... | collective-permute-start | bytes 1572872 | tf_op jit(solution)/shard_map/ppermute | solution.py:22
  31.9 1.4 %collective-permute-start.7 = (bf16[4,256,256]{2,1,0:T(8,128)(2,1)}, bf16[4,256,256]{2,1,0:T(8,128)(2,1)S(1)}, u32[]{:S(2)}, u32[]{:S(2)}) collective-permute-start(bf16[4,256,256]{2,1,0:T(8,128)(2,1)} %get-tuple-element.20), channel_id=1, source_target_pairs={{0,12},{4,0},{8,4},{12,8},{1,13},{5,1},{9,5},{13,9},{2,14},{6,2},{... | collective-permute-start | bytes 1572872 | tf_op jit(solution)/shard_map/ppermute | solution.py:22
  33.4 2.1 %collective-permute-start.8 = (bf16[4,256,256]{2,1,0:T(8,128)(2,1)S(1)}, bf16[4,256,256]{2,1,0:T(8,128)(2,1)}, u32[]{:S(2)}, u32[]{:S(2)}) collective-permute-start(bf16[4,256,256]{2,1,0:T(8,128)(2,1)S(1)} %pad_maximum_fusion.1), channel_id=1, source_target_pairs={{0,16},{16,0},{1,17},{17,1},{2,18},{18,2},{3,19},{19,3},{4,20},{20... | collective-permute-start | bytes 1572872 | tf_op jit(solution)/shard_map/ppermute | solution.py:26
  35.4 10.8 %collective-permute-done.6 = bf16[4,256,256]{2,1,0:T(8,128)(2,1)S(1)} collective-permute-done((bf16[4,256,256]{2,1,0:T(8,128)(2,1)}, bf16[4,256,256]{2,1,0:T(8,128)(2,1)S(1)}, u32[]{:S(2)}, u32[]{:S(2)}) %collective-permute-start.6) | collective-permute-done | bytes 524320 | tf_op jit(solution)/shard_map/ppermute | solution.py:22
  46.2 10.8 %collective-permute-done.7 = bf16[4,256,256]{2,1,0:T(8,128)(2,1)S(1)} collective-permute-done((bf16[4,256,256]{2,1,0:T(8,128)(2,1)}, bf16[4,256,256]{2,1,0:T(8,128)(2,1)S(1)}, u32[]{:S(2)}, u32[]{:S(2)}) %collective-permute-start.7) | collective-permute-done | bytes 524320 | tf_op jit(solution)/shard_map/ppermute | solution.py:22
  57.0 1.6 %maximum_maximum_fusion = bf16[8,2,256,256]{3,2,1,0:T(8,128)(2,1)} fusion(bf16[4,1,256,256]{3,2,1,0:T(8,128)(2,1)S(1)} %bitcast.78, bf16[4,1,256,256]{3,2,1,0:T(8,128)(2,1)S(1)} %bitcast.77), kind=kLoop, calls=%fused_computation | loop fusion | flops 3145728 | bytes 3145728 | tf_op jit(solution)/shard_map/concatenate | solution.py:231
  58.7 4.0 %all-to-all-start.1 = ((bf16[8,2,256,256]{3,2,1,0:T(8,128)(2,1)}), bf16[8,2,256,256]{3,2,1,0:T(8,128)(2,1)S(1)}, u32[]{:S(2)}, u32[]{:S(2)}) async-start(bf16[8,2,256,256]{3,2,1,0:T(8,128)(2,1)} %maximum_maximum_fusion), calls=%async_computation.1 | async-start | bytes 4194304 | tf_op jit(solution)/shard_map/all_to_all | solution.py:230
  62.7 0.7 collective-permute-start.9
  63.3 0.5 pad.20
  63.8 0.5 pad.21
  64.4 0.1 reshape.305
  64.5 0.1 stack.121
  64.7 0.7 add.234
  65.4 23.9 %collective-permute-done.9 = bf16[4,256,256]{2,1,0:T(8,128)(2,1)S(1)} collective-permute-done((bf16[4,256,256]{2,1,0:T(8,128)(2,1)}, bf16[4,256,256]{2,1,0:T(8,128)(2,1)S(1)}, u32[]{:S(2)}, u32[]{:S(2)}) %collective-permute-start.9) | collective-permute-done | bytes 524320 | tf_op jit(solution)/shard_map/ppermute | solution.py:22
  89.3 1.2 pad_maximum_fusion
  90.5 3.8 %all-to-all-start.2 = ((bf16[8,1,256,256]{3,2,1,0:T(8,128)(2,1)}), bf16[8,1,256,256]{3,2,1,0:T(8,128)(2,1)S(1)}, u32[]{:S(2)}, u32[]{:S(2)}) async-start(bf16[8,1,256,256]{3,2,1,0:T(8,128)(2,1)} %pad_maximum_fusion), calls=%async_computation.2 | async-start | bytes 2097152 | tf_op jit(solution)/shard_map/all_to_all | solution.py:230
  94.4 1.2 concatenate.24.picks
  95.6 1.9 %fusion.inverse_ref = bf16[256,256]{1,0:T(8,128)(2,1)} fusion(bf16[256,256]{1,0:T(8,128)(2,1)} %param.16, s32[256]{0:T(256)S(1)} %copy-done.19, s32[256]{0:T(256)S(1)} %add.222), kind=kOutput, calls=%fused_computation.2 | convolution fusion | flops 67239936 | bytes 264192 | tf_op jit(solution)/shard_map/dot_general | solution.py:60
  97.5 2.2 %collective-permute-start.12 = (bf16[4,64,256]{2,1,0:T(8,128)(2,1)S(1)}, bf16[4,64,256]{2,1,0:T(8,128)(2,1)S(1)}, u32[]{:S(2)}, u32[]{:S(2)}) collective-permute-start(bf16[4,64,256]{2,1,0:T(8,128)(2,1)S(1)} %bitcast.72), channel_id=1, source_target_pairs={{0,12},{4,0},{8,4},{12,8},{1,13},{5,1},{9,5},{13,9},{2,14},{6,2},{... | collective-permute-start | bytes 393224 | tf_op jit(solution)/shard_map/ppermute | solution.py:22
  99.7 0.6 collective-permute-start.10
  100.3 0.8 fusion.6.refs_6_
  101.0 2.7 %collective-permute-done.12.refs_3_ = bf16[4,64,256]{2,1,0:T(8,128)(2,1)S(1)} collective-permute-done((bf16[4,64,256]{2,1,0:T(8,128)(2,1)S(1)}, bf16[4,64,256]{2,1,0:T(8,128)(2,1)S(1)}, u32[]{:S(2)}, u32[]{:S(2)}) %collective-permute-start.12) | collective-permute-done | bytes 131104 | tf_op jit(solution)/shard_map/ppermute | solution.py:22
  103.7 8.0 %collective-permute-done.11.refs_2_ = bf16[4,64,256]{2,1,0:T(8,128)(2,1)S(1)} collective-permute-done((bf16[4,64,256]{2,1,0:T(8,128)(2,1)S(1)}, bf16[4,64,256]{2,1,0:T(8,128)(2,1)S(1)}, u32[]{:S(2)}, u32[]{:S(2)}) %collective-permute-start.11) | collective-permute-done | bytes 131104 | tf_op jit(solution)/shard_map/ppermute | solution.py:22
  111.7 0.6 copy-done.16
  112.3 0.7 copy-done.17
  113.0 3.1 %parent_panels.1 = (bf16[256,1024]{1,0:T(8,128)(2,1)}, bf16[8,256,256]{2,1,0:T(8,128)(2,1)}) custom-call(bf16[256,256]{1,0:T(8,128)(2,1)} %fusion.inverse_ref, bf16[4,64,256]{2,1,0:T(8,128)(2,1)} %bitcast.75, bf16[4,64,256]{2,1,0:T(8,128)(2,1)} %copy-done.17, bf16[4,64,256]{2,1,0:T(8,128)(2,1)} %copy-done.16, bf16[4,64,256]{2,1,0:T(8,128)(2,1)} %copy-done.15, ...), custom_call_target="tpu_custom_call" | custom-call | flops 134217728 | bytes 3145728 | tf_op jit(solution)/shard_map/parent_panels/pallas_call | solution.py:129
  116.1 1.0 copy-done.3
  117.1 11.6 %front.1 = bf16[8,256,4,256]{3,2,1,0:T(4,128)(2,1)} custom-call(s32[10,8]{1,0:T(8,128)} %concatenate.24.picks, bf16[8,1,256,256]{3,2,1,0:T(8,128)(2,1)} %copy-done.2, bf16[8,2,256,256]{3,2,1,0:T(8,128)(2,1)} %copy-done.1, bf16[8,1,256,256]{3,2,1,0:T(8,128)(2,1)} %copy-done.3, bf16[8,256,256]{2,1,0:T(8,128)(2,1)} %get-tuple-element.29.refs_3_, ...), custom_call_target="tpu_custom_call" | custom-call | flops 2147483648 | bytes 12582912 | tf_op jit(solution)/shard_map/front/pallas_call | solution.py:215
  (76 shorter events, 0.9 us)
Async XLA Ops:
  0.0 12.1 %copy-start = (bf16[1,256,256]{2,1,0:T(8,128)(2,1)S(1)}, bf16[1,256,256]{2,1,0:T(8,128)(2,1)}, u32[]{:S(2)}) copy-start(bf16[1,256,256]{2,1,0:T(8,128)(2,1)} %param.12) | copy-start | bytes 393220
  1.0 19.2 %copy-start.10 = (bf16[1,64,4,1,256]{4,1,2,3,0:T(8,128)(2,1)}, bf16[1,64,4,1,256]{4,1,2,3,0:T(8,128)(2,1)S(1)}, u32[]{:S(2)}) copy-start(bf16[1,64,4,1,256]{4,1,2,3,0:T(8,128)(2,1)S(1)} %copy.36) | copy-start | bytes 393220
  1.0 19.2 %collective-permute-start.2 = (bf16[4,64,256]{2,1,0:T(8,128)(2,1)S(1)}, bf16[4,64,256]{2,1,0:T(8,128)(2,1)S(1)}, u32[]{:S(2)}, u32[]{:S(2)}) collective-permute-start(bf16[4,64,256]{2,1,0:T(8,128)(2,1)S(1)} %bitcast.68), channel_id=1, source_target_pairs={{0,12},{4,0},{8,4},{12,8},{1,13},{5,1},{9,5},{13,9},{2,14},{6,2},{... | collective-permute-start | bytes 393224 | tf_op jit(solution)/shard_map/ppermute | solution.py:22
  6.1 14.1 %collective-permute-start.1 = (bf16[4,64,256]{2,1,0:T(8,128)(2,1)S(1)}, bf16[4,64,256]{2,1,0:T(8,128)(2,1)S(1)}, u32[]{:S(2)}, u32[]{:S(2)}) collective-permute-start(bf16[4,64,256]{2,1,0:T(8,128)(2,1)S(1)} %bitcast.69), channel_id=1, source_target_pairs={{0,8},{4,12},{8,0},{12,4},{1,9},{5,13},{9,1},{13,5},{2,10},{6,14},... | collective-permute-start | bytes 393224 | tf_op jit(solution)/shard_map/ppermute | solution.py:22
  6.1 14.2 %collective-permute-start = (bf16[4,64,256]{2,1,0:T(8,128)(2,1)S(1)}, bf16[4,64,256]{2,1,0:T(8,128)(2,1)S(1)}, u32[]{:S(2)}, u32[]{:S(2)}) collective-permute-start(bf16[4,64,256]{2,1,0:T(8,128)(2,1)S(1)} %bitcast.70), channel_id=1, source_target_pairs={{0,4},{4,8},{8,12},{12,0},{1,5},{5,9},{9,13},{13,1},{2,6},{6,10},{... | collective-permute-start | bytes 393224 | tf_op jit(solution)/shard_map/ppermute | solution.py:22
  9.0 11.2 %copy-start.4 = (bf16[512,256]{1,0:T(8,128)(2,1)}, bf16[512,256]{1,0:T(8,128)(2,1)S(1)}, u32[]{:S(2)}) copy-start(bf16[512,256]{1,0:T(8,128)(2,1)S(1)} %pad_maximum_fusion.2.refs_6_.refs_4_) | copy-start | bytes 786436
  9.0 7.3 %collective-permute-start.4 = (bf16[512,256]{1,0:T(8,128)(2,1)S(1)}, bf16[512,256]{1,0:T(8,128)(2,1)S(1)}, u32[]{:S(2)}, u32[]{:S(2)}) collective-permute-start(bf16[512,256]{1,0:T(8,128)(2,1)S(1)} %pad_maximum_fusion.2.refs_6_.refs_4_), channel_id=1, source_target_pairs={{0,2},{1,3},{2,0},{3,1},{4,6},{5,7},{6,4},{7,5},{8,10},{9,11},{10,... | collective-permute-start | bytes 786440 | tf_op jit(solution)/shard_map/ppermute | solution.py:26
  10.5 9.7 %collective-permute-start.3 = (bf16[512,256]{1,0:T(8,128)(2,1)S(1)}, bf16[512,256]{1,0:T(8,128)(2,1)S(1)}, u32[]{:S(2)}, u32[]{:S(2)}) collective-permute-start(bf16[512,256]{1,0:T(8,128)(2,1)S(1)} %pad_maximum_fusion.2.refs_6_.refs_4_), channel_id=1, source_target_pairs={{0,1},{1,0},{2,3},{3,2},{4,5},{5,4},{6,7},{7,6},{8,9},{9,8},{10,11... | collective-permute-start | bytes 786440 | tf_op jit(solution)/shard_map/ppermute | solution.py:26
  16.3 3.9 %copy-start.5 = (bf16[512,256]{1,0:T(8,128)(2,1)}, bf16[512,256]{1,0:T(8,128)(2,1)S(1)}, u32[]{:S(2)}) copy-start(bf16[512,256]{1,0:T(8,128)(2,1)S(1)} %collective-permute-done.4.refs_8_.refs_6_) | copy-start | bytes 786436
  16.3 4.0 %collective-permute-start.5 = (bf16[512,256]{1,0:T(8,128)(2,1)S(1)}, bf16[512,256]{1,0:T(8,128)(2,1)S(1)}, u32[]{:S(2)}, u32[]{:S(2)}) collective-permute-start(bf16[512,256]{1,0:T(8,128)(2,1)S(1)} %collective-permute-done.4.refs_8_.refs_6_), channel_id=1, source_target_pairs={{0,1},{1,0},{2,3},{3,2},{4,5},{5,4},{6,7},{7,6},{8,9},{9,8},{10,11... | collective-permute-start | bytes 786440 | tf_op jit(solution)/shard_map/ppermute | solution.py:26
  20.2 0.6 copy-start.12
  20.2 0.7 copy-start.13
  20.2 0.7 copy-start.14
  20.3 0.8 copy-start.6
  20.3 0.8 copy-start.8
  25.5 3.9 %copy-start.7 = (bf16[512,256]{1,0:T(8,128)(2,1)S(1)}, bf16[512,256]{1,0:T(8,128)(2,1)}, u32[]{:S(2)}) copy-start(bf16[512,256]{1,0:T(8,128)(2,1)} %copy-done.6) | copy-start | bytes 786436
  25.5 7.8 %copy-start.9 = (bf16[512,256]{1,0:T(8,128)(2,1)S(1)}, bf16[512,256]{1,0:T(8,128)(2,1)}, u32[]{:S(2)}) copy-start(bf16[512,256]{1,0:T(8,128)(2,1)} %copy-done.8) | copy-start | bytes 786436
  25.5 31.6 %all-to-all-start = ((bf16[8,1,256,256]{3,2,1,0:T(8,128)(2,1)}), bf16[8,1,256,256]{3,2,1,0:T(8,128)(2,1)S(1)}, u32[]{:S(2)}, u32[]{:S(2)}) async-start(bf16[8,1,256,256]{3,2,1,0:T(8,128)(2,1)} %bitcast.66), calls=%async_computation | async-start | bytes 2097152 | tf_op jit(solution)/shard_map/all_to_all | solution.py:289
  29.4 16.8 %collective-permute-start.6 = (bf16[4,256,256]{2,1,0:T(8,128)(2,1)}, bf16[4,256,256]{2,1,0:T(8,128)(2,1)S(1)}, u32[]{:S(2)}, u32[]{:S(2)}) collective-permute-start(bf16[4,256,256]{2,1,0:T(8,128)(2,1)} %get-tuple-element.19), channel_id=1, source_target_pairs={{0,4},{4,8},{8,12},{12,0},{1,5},{5,9},{9,13},{13,1},{2,6},{6,10},{... | collective-permute-start | bytes 1572872 | tf_op jit(solution)/shard_map/ppermute | solution.py:22
  31.9 25.1 %collective-permute-start.7 = (bf16[4,256,256]{2,1,0:T(8,128)(2,1)}, bf16[4,256,256]{2,1,0:T(8,128)(2,1)S(1)}, u32[]{:S(2)}, u32[]{:S(2)}) collective-permute-start(bf16[4,256,256]{2,1,0:T(8,128)(2,1)} %get-tuple-element.20), channel_id=1, source_target_pairs={{0,12},{4,0},{8,4},{12,8},{1,13},{5,1},{9,5},{13,9},{2,14},{6,2},{... | collective-permute-start | bytes 1572872 | tf_op jit(solution)/shard_map/ppermute | solution.py:22
  33.4 23.7 %collective-permute-start.8 = (bf16[4,256,256]{2,1,0:T(8,128)(2,1)S(1)}, bf16[4,256,256]{2,1,0:T(8,128)(2,1)}, u32[]{:S(2)}, u32[]{:S(2)}) collective-permute-start(bf16[4,256,256]{2,1,0:T(8,128)(2,1)S(1)} %pad_maximum_fusion.1), channel_id=1, source_target_pairs={{0,16},{16,0},{1,17},{17,1},{2,18},{18,2},{3,19},{19,3},{4,20},{20... | collective-permute-start | bytes 1572872 | tf_op jit(solution)/shard_map/ppermute | solution.py:26
  57.0 1.6 %copy-start.2 = (bf16[8,1,256,256]{3,2,1,0:T(8,128)(2,1)}, bf16[8,1,256,256]{3,2,1,0:T(8,128)(2,1)S(1)}, u32[]{:S(2)}) copy-start(bf16[8,1,256,256]{3,2,1,0:T(8,128)(2,1)S(1)} %all-to-all-done.refs_0_) | copy-start | bytes 3145732
  58.7 6.7 %copy-start.18 = (bf16[64,4,1,256]{3,1,2,0:T(4,128)(2,1)S(1)}, bf16[64,4,1,256]{3,1,2,0:T(4,128)(2,1)}, u32[]{:S(2)}) copy-start(bf16[64,4,1,256]{3,1,2,0:T(4,128)(2,1)} %param.14) | copy-start | bytes 393220
  58.7 30.6 %all-to-all-start.1 = ((bf16[8,2,256,256]{3,2,1,0:T(8,128)(2,1)}), bf16[8,2,256,256]{3,2,1,0:T(8,128)(2,1)S(1)}, u32[]{:S(2)}, u32[]{:S(2)}) async-start(bf16[8,2,256,256]{3,2,1,0:T(8,128)(2,1)} %maximum_maximum_fusion), calls=%async_computation.1 | async-start | bytes 4194304 | tf_op jit(solution)/shard_map/all_to_all | solution.py:230
  62.7 26.7 %collective-permute-start.9 = (bf16[4,256,256]{2,1,0:T(8,128)(2,1)}, bf16[4,256,256]{2,1,0:T(8,128)(2,1)S(1)}, u32[]{:S(2)}, u32[]{:S(2)}) collective-permute-start(bf16[4,256,256]{2,1,0:T(8,128)(2,1)} %get-tuple-element.26), channel_id=1, source_target_pairs={{0,8},{4,12},{8,0},{12,4},{1,9},{5,13},{9,1},{13,5},{2,10},{6,14},... | collective-permute-start | bytes 1572872 | tf_op jit(solution)/shard_map/ppermute | solution.py:22
  65.4 35.7 %copy-start.11 = (bf16[64,4,1,256]{3,0,1,2:T(8,128)(2,1)}, bf16[64,4,1,256]{3,0,1,2:T(8,128)(2,1)S(1)}, u32[]{:S(2)}) copy-start(bf16[64,4,1,256]{3,0,1,2:T(8,128)(2,1)S(1)} %copy.35) | copy-start | bytes 393220
  65.4 29.0 %copy-start.20 = (s32[1,8]{1,0:T(1,128)S(1)}, s32[1,8]{1,0:T(1,128)}, u32[]{:S(2)}) copy-start(s32[1,8]{1,0:T(1,128)} %pad.20) | copy-start | bytes 100
  65.4 29.0 %copy-start.21 = (s32[1,8]{1,0:T(1,128)S(1)}, s32[1,8]{1,0:T(1,128)}, u32[]{:S(2)}) copy-start(s32[1,8]{1,0:T(1,128)} %pad.21) | copy-start | bytes 100
  65.4 30.2 %copy-start.19 = (s32[256]{0:T(256)S(1)}, s32[256]{0:T(256)}, u32[]{:S(2)}) copy-start(s32[256]{0:T(256)} %add.234) | copy-start | bytes 3076
  89.3 11.7 %copy-start.1 = (bf16[8,2,256,256]{3,2,1,0:T(8,128)(2,1)}, bf16[8,2,256,256]{3,2,1,0:T(8,128)(2,1)S(1)}, u32[]{:S(2)}) copy-start(bf16[8,2,256,256]{3,2,1,0:T(8,128)(2,1)S(1)} %all-to-all-done.1.refs_1_) | copy-start | bytes 6291460
  90.5 25.6 %all-to-all-start.2 = ((bf16[8,1,256,256]{3,2,1,0:T(8,128)(2,1)}), bf16[8,1,256,256]{3,2,1,0:T(8,128)(2,1)S(1)}, u32[]{:S(2)}, u32[]{:S(2)}) async-start(bf16[8,1,256,256]{3,2,1,0:T(8,128)(2,1)} %pad_maximum_fusion), calls=%async_computation.2 | async-start | bytes 2097152 | tf_op jit(solution)/shard_map/all_to_all | solution.py:230
  97.5 6.2 %collective-permute-start.12 = (bf16[4,64,256]{2,1,0:T(8,128)(2,1)S(1)}, bf16[4,64,256]{2,1,0:T(8,128)(2,1)S(1)}, u32[]{:S(2)}, u32[]{:S(2)}) collective-permute-start(bf16[4,64,256]{2,1,0:T(8,128)(2,1)S(1)} %bitcast.72), channel_id=1, source_target_pairs={{0,12},{4,0},{8,4},{12,8},{1,13},{5,1},{9,5},{13,9},{2,14},{6,2},{... | collective-permute-start | bytes 393224 | tf_op jit(solution)/shard_map/ppermute | solution.py:22
  99.7 12.0 %collective-permute-start.11 = (bf16[4,64,256]{2,1,0:T(8,128)(2,1)S(1)}, bf16[4,64,256]{2,1,0:T(8,128)(2,1)S(1)}, u32[]{:S(2)}, u32[]{:S(2)}) collective-permute-start(bf16[4,64,256]{2,1,0:T(8,128)(2,1)S(1)} %bitcast.73), channel_id=1, source_target_pairs={{0,8},{4,12},{8,0},{12,4},{1,9},{5,13},{9,1},{13,5},{2,10},{6,14},... | collective-permute-start | bytes 393224 | tf_op jit(solution)/shard_map/ppermute | solution.py:22
  99.7 12.0 %collective-permute-start.10 = (bf16[4,64,256]{2,1,0:T(8,128)(2,1)S(1)}, bf16[4,64,256]{2,1,0:T(8,128)(2,1)S(1)}, u32[]{:S(2)}, u32[]{:S(2)}) collective-permute-start(bf16[4,64,256]{2,1,0:T(8,128)(2,1)S(1)} %bitcast.74), channel_id=1, source_target_pairs={{0,4},{4,8},{8,12},{12,0},{1,5},{5,9},{9,13},{13,1},{2,6},{6,10},{... | collective-permute-start | bytes 393224 | tf_op jit(solution)/shard_map/ppermute | solution.py:22
  103.7 8.0 %copy-start.15 = (bf16[4,64,256]{2,1,0:T(8,128)(2,1)}, bf16[4,64,256]{2,1,0:T(8,128)(2,1)S(1)}, u32[]{:S(2)}) copy-start(bf16[4,64,256]{2,1,0:T(8,128)(2,1)S(1)} %collective-permute-done.12.refs_3_) | copy-start | bytes 393220
  111.7 0.7 copy-start.16
  112.3 0.7 copy-start.17
  116.1 1.0 copy-start.3

commit v4 on v3

--- a/solution.py
+++ b/solution.py
@@ -36,12 +36,13 @@
     return [parts[d] for d in range(count)]
 
 
-def gathered_by_bits(value, axis):
+def gathered_by_bits(value, axis, meanwhile):
     count = lax.axis_size(axis)
     parts = {0: value}
     mask = count // 2
     while mask:
-        parts.update({e ^ mask: exchanged(part, axis, mask) for e, part in parts.items()})
+        sent = {**parts, 0: value if mask > 1 else after(value, meanwhile)}
+        parts.update({e ^ mask: exchanged(part, axis, mask) for e, part in sent.items()})
         mask //= 2
     return [parts[e] for e in range(count)]
 
@@ -55,9 +56,8 @@
         wanted = (jnp.stack(chunks)[:, None] * width + jnp.arange(width)).reshape(size, 1)
         return (wanted == place).astype(BF16)
 
-    if row_chunks is not None:
-        matrix = jnp.dot(chooser(row_chunks), matrix)
-    return jnp.dot(matrix, chooser(col_chunks).T)
+    matrix = jnp.dot(chooser(row_chunks), matrix)
+    return matrix if col_chunks is None else jnp.dot(matrix, chooser(col_chunks).T)
 
 
 def scaled_rows(inverse, parts, scaled):
@@ -110,12 +110,12 @@
     )(picks, block, inverse, *rows, *cols)
 
 
-def panels_kernel(grid, inverse_ref, *refs):
-    rows, cols = refs[:grid], refs[grid : 2 * grid]
-    other_ref, scaled, turned = refs[2 * grid :]
+def panels_kernel(grid, inverse_ref, rows_ref, *refs):
+    cols = refs[:grid]
+    other_ref, scaled, turned = refs[grid:]
     tile = inverse_ref.shape[0]
     width = tile // (2 * grid)
-    scaled_rows(inverse_ref[...], rows, scaled)
+    scaled_rows(inverse_ref[...], [rows_ref], scaled)
     for k in range(2 * grid):
         here = slice(tile + k * width, tile + (k + 1) * width)
         there = slice(k * width, (k + 1) * width)
@@ -124,11 +124,11 @@
 
 
 def panels(inverse, rows, cols, other):
-    grid, tile = len(rows), inverse.shape[0]
+    grid, tile = len(cols), inverse.shape[0]
     vmem = pl.BlockSpec(memory_space=pltpu.VMEM)
     return pl.pallas_call(
         functools.partial(panels_kernel, grid),
-        in_specs=[vmem] * (2 + 2 * grid),
+        in_specs=[vmem] * (3 + grid),
         out_specs=[vmem] * 2,
         out_shape=[
             jax.ShapeDtypeStruct((tile, grid * tile), BF16),
@@ -139,33 +139,47 @@
             flops=2 * grid * tile**3, bytes_accessed=12 * grid * tile * tile, transcendentals=0
         ),
         name="parent_panels",
-    )(inverse, *rows, *cols, other)
-
-
-def front_kernel(where, picks, *refs):
-    grid = len(where)
-    count = 1 + max(i for i, _ in where)
+    )(inverse, rows, *cols, other)
+
+
+def front_kernel(where, count, picks, *refs):
     arrived = refs[:count]
-    col_ref, scaled_ref, diag_ref, weave_ref, out_ref, held, sems = refs[count:]
+    col_ref, scaled_ref, diag_ref, weave_ref = refs[count : count + 4]
+    out_ref, held, sems = refs[-3:]
     tile = weave_ref.shape[0]
+    grid = held.shape[2]
     step = pl.program_id(0)
-    copies = [
-        pltpu.make_async_copy(arrived[i].at[:, j], held.at[d], sems.at[d])
-        for d, (i, j) in enumerate(where)
-    ]
+    here = picks[0, step]
+    slot = lax.rem(step, 2)
+
+    def pieces(place, child, slot):
+        i, j = place
+        return pltpu.make_async_copy(
+            arrived[i].at[child * grid : (child + 1) * grid, j],
+            held.at[slot, child],
+            sems.at[slot, child],
+        )
+
+    def fetch(at, slot):
+        for child in range(2):
+            wanted = picks[1 + child, picks[0, at]]
+            for d, place in where.items():
+
+                @pl.when(wanted == d)
+                def _():
+                    pieces(place, child, slot).start()
 
     @pl.when(step == 0)
     def _():
-        for copy in copies:
-            copy.start()
-
-    for d in range(grid):
-
-        @pl.when(picks[9, d] == step)
-        def _():
-            copies[d].wait()
+        fetch(0, 0)
+
+    @pl.when(step + 1 < pl.num_programs(0))
+    def _():
+        fetch(step + 1, 1 - slot)
 
     update = jnp.dot(col_ref[0], scaled_ref[...], preferred_element_type=F32)
+    for child in range(2):
+        pieces((0, 0), child, slot).wait()
     height = tile // grid
     lanes = 128 if height <= 128 else tile
     for part in range(grid):
@@ -178,10 +192,10 @@
         for q in range(grid):
             value = -update[rows, q * tile : (q + 1) * tile]
             for child in range(2):
-                usable = picks[2 + child, step] * picks[6 + child, q]
-                piece = held[picks[child, step], picks[4 + child, q], rows]
+                usable = picks[3 + child, here] * picks[7 + child, q]
+                piece = held[slot, child, picks[5 + child, q], rows]
                 value = value + jnp.where(usable > 0, piece.astype(F32), 0.0)
-            entries = jnp.where(picks[8, q] == step, diag_ref[0, :, near : near + lanes], 0.0)
+            entries = jnp.where(picks[9, q] == here, diag_ref[0, :, near : near + lanes], 0.0)
             bands = [value[:, at : at + lanes] for at in range(0, tile, lanes)]
             bands[near // lanes] += jnp.where(on, entries, 0.0)
             stacked.append(jnp.concatenate(bands, axis=1).astype(BF16))
@@ -191,39 +205,48 @@
         out_ref[0, rows] = woven.reshape(height, grid, tile).astype(BF16)
 
 
-def front(arrived, where, col, scaled, diag, picks):
-    grid, tile = len(where), col.shape[-1]
+def front(arrived, where, steps, col, scaled, diag, picks, begun=None):
+    tile = col.shape[-1]
+    grid = scaled.shape[-1] // tile
     height = tile // grid
     place = jnp.arange(tile, dtype=jnp.int32)
     weave = (place[None, :] == (place % grid * height + place // grid)[:, None]).astype(BF16)
+    hbm = pl.BlockSpec(memory_space=pl.ANY)
+    operands = [*arrived, col, scaled, diag, weave]
+    in_specs = [hbm] * len(arrived) + [
+        pl.BlockSpec((1, tile, tile), lambda s, picks: (picks[0, s], 0, 0)),
+        pl.BlockSpec((tile, grid * tile), lambda s, picks: (0, 0)),
+        pl.BlockSpec((1, 1, tile), lambda s, picks: (picks[0, s], 0, 0)),
+        pl.BlockSpec((tile, tile), lambda s, picks: (0, 0)),
+    ]
+    aliases = {}
+    if begun is not None:
+        aliases[1 + len(operands)] = 0
+        operands.append(begun)
+        in_specs.append(hbm)
     spec = pltpu.PrefetchScalarGridSpec(
         num_scalar_prefetch=1,
-        grid=(2 * grid,),
-        in_specs=[pl.BlockSpec(memory_space=pl.ANY)] * len(arrived)
-        + [
-            pl.BlockSpec((1, tile, tile), lambda s, picks: (s, 0, 0)),
-            pl.BlockSpec((tile, grid * tile), lambda s, picks: (0, 0)),
-            pl.BlockSpec((1, 1, tile), lambda s, picks: (s, 0, 0)),
-            pl.BlockSpec((tile, tile), lambda s, picks: (0, 0)),
+        grid=(steps,),
+        in_specs=in_specs,
+        out_specs=pl.BlockSpec((1, tile, grid, tile), lambda s, picks: (picks[0, s], 0, 0, 0)),
+        scratch_shapes=[
+            pltpu.VMEM((2, 2, grid, tile, tile), BF16),
+            pltpu.SemaphoreType.DMA((2, 2)),
         ],
-        out_specs=pl.BlockSpec((1, tile, grid, tile), lambda s, picks: (s, 0, 0, 0)),
-        scratch_shapes=[
-            pltpu.VMEM((grid, 2 * grid, tile, tile), BF16),
-            pltpu.SemaphoreType.DMA((grid,)),
-        ],
     )
     return pl.pallas_call(
-        functools.partial(front_kernel, where),
+        functools.partial(front_kernel, where, len(arrived)),
         grid_spec=spec,
         out_shape=jax.ShapeDtypeStruct((2 * grid, tile, grid, tile), BF16),
-        compiler_params=pltpu.CompilerParams(vmem_limit_bytes=56 * 2**20),
+        input_output_aliases=aliases,
+        compiler_params=pltpu.CompilerParams(vmem_limit_bytes=48 * 2**20),
         cost_estimate=pl.CostEstimate(
-            flops=8 * grid * grid * tile**3,
-            bytes_accessed=12 * grid * grid * tile * tile,
+            flops=4 * steps * grid * tile**3,
+            bytes_accessed=6 * steps * grid * tile * tile,
             transcendentals=0,
         ),
-        name="front",
-    )(picks, *arrived, col, scaled, diag, weave)
+        name="front" if begun is None else "front_end",
+    )(picks, *operands)
 
 
 def to_plane(*block_rows):
@@ -264,6 +287,7 @@
     col_chunks = [my_col ^ e for e in range(grid)]
     plane_chunks = [(my_half ^ h) * grid + c for h in range(2) for c in col_chunks]
 
+    blocks = child_block[0, :, 0, :, :, 0].transpose(0, 2, 1, 3)
     child_rows = gathered(child_row[0, :, :, 0].transpose(1, 0, 2), "row")
     cols = gathered_by_bits(
         jnp.concatenate(
@@ -273,10 +297,11 @@
             ]
         ),
         "col",
+        blocks,
     )
     other_cols = exchanged(jnp.stack([part[tile:] for part in cols]), "half", 1)
     block_rows = contribution(
-        child_block[0, :, 0, :, :, 0].transpose(0, 2, 1, 3),
+        blocks,
         reordered(child_pivot_inv[0], col_chunks, row_chunks),
         child_rows,
         cols,
@@ -291,31 +316,49 @@
     )
     last = shifted(after(block_rows[far], moved), "row", far)
     middle = to_plane(*after(moved, other_cols, staying))
-    parent_rows = gathered(after(parent_row[:, :, 0].transpose(1, 0, 2), last), "row")
-    ending = to_plane(after(last, middle))
+    parent_rows = lax.all_gather(
+        after(parent_row[:, :, 0].transpose(1, 0, 2), moved), "row", axis=1, tiled=True
+    )
+    ending = to_plane(after(last, middle, parent_rows))
     scaled, turned = panels(
-        reordered(parent_pivot_inv, plane_chunks, row_chunks), parent_rows, cols, other_cols
-    )
-    where = {0: (0, 0), far: (2, 0), **{d: (1, i) for i, d in enumerate(first)}}
+        reordered(parent_pivot_inv, plane_chunks, None), parent_rows, cols, other_cols
+    )
 
     targets = jnp.arange(2 * grid, dtype=jnp.int32)
     row_shift = jnp.repeat(shift, 2, axis=1)
     row_usable = (my_row < row_shift) == (targets % 2 == 1)[None, :]
-    source = (my_col - shift) % grid + grid * jnp.arange(2, dtype=jnp.int32)[:, None]
+    row_shift = jnp.where(row_usable, row_shift, 0)
+    source = (my_col - shift) % grid
     col_usable = (my_col < shift) == (my_half == 1)
     on_diagonal = jnp.where(my_row == my_col, 2 * places + my_half, -1)[None]
-    first_used = 2 * jnp.min(unshift, axis=0)[None]
+    reached = jnp.any(row_shift == far, axis=0)
+    spare = jnp.sum((targets[None, :] <= targets[:, None]) & ~reached[None, :], axis=1)
+    early = jnp.minimum(targets, spare[-1] - 1)
+    early = jnp.sum(
+        jnp.where((spare - 1 == early[:, None]) & ~reached[None, :], targets[None, :], 0), axis=1
+    )
+    late = jnp.max(jnp.where(row_shift == far, targets[None, :], -1), axis=1)
     wide = lambda a: jnp.pad(a.astype(jnp.int32), ((0, 0), (0, 2 * grid - a.shape[1])))
-    picks = jnp.concatenate(
-        [wide(a) for a in (row_shift, row_usable, source, col_usable, on_diagonal, first_used)]
-    )
-    return front(
-        [staying, middle, ending],
-        [where[d] for d in range(grid)],
+    picks = [wide(a) for a in (row_shift, row_usable, source, col_usable, on_diagonal)]
+    kept = {0: (0, 0), **{d: (1, i) for i, d in enumerate(first)}}
+    begun = front(
+        [staying, middle],
+        kept,
+        2 * grid - 1,
         turned,
         scaled,
         parent_diag,
-        picks,
+        jnp.concatenate([early[None], *picks]),
+    )
+    return front(
+        [staying, middle, ending],
+        {**kept, far: (2, 0)},
+        2,
+        turned,
+        scaled,
+        parent_diag,
+        jnp.concatenate([wide(late[None]), *picks]),
+        begun,
     ).reshape(2 * grid, 1, tile, grid, 1, tile)
 
 

time: 129 us -> 131 us (1.016)
  blocking collectives: 0 us -> 36.6 us
  waiting for transfers between devices: 59.3 us -> 22.8 us
  starting transfers between devices: 28.8 us -> 26.6 us
  other arithmetic: 4.94 us -> 6.5 us
    all_gather x0 -> x1, blocking collectives: none -> 36.6 us  [shards(): lax.all_gather(after(parent_row[:, :, 0].transpose(1, 0, 2), moved), 'row...]
    ppermute x9 -> x6, waiting for transfers between devices: 56.2 us -> 21.8 us  [shifted(): lax.ppermute(value, axis, [(i, (i + step) % count) for i in range(count)])]
    unnamed x47, local copies, waits for them, and re-layouts: 7.5 us -> 10.3 us
    ppermute x9 -> x6, starting transfers between devices: 13.4 us -> 10.7 us  [shifted(): lax.ppermute(value, axis, [(i, (i + step) % count) for i in range(count)])]
    ppermute x4, waiting for transfers between devices: 3.14 us -> 0.98 us  [exchanged(): lax.ppermute(value, axis, [(i, i ^ mask) for i in range(lax.axis_size(axi...]
    pallas_call x1 -> x2, Pallas kernels: 11.6 us -> 12.8 us  [front(): pl.pallas_call(functools.partial(front_kernel, where, len(arrived)), grid...]
  transfers between devices with their start and end apart: 16 -> 13, of which waited for: 6 -> 5; matrix products, arithmetic and copies ran while one was open for 11% -> 9% of each run, Pallas kernels for 2% -> 9%
where the time goes in v4:
time: 131 us; the launch traced here: 130 us
  blocking collectives  36.6 us (28%)
  starting transfers between devices  26.6 us (20%)
  waiting for transfers between devices  22.8 us (17%)
  Pallas kernels  20.1 us (15%)
  local copies, waits for them, and re-layouts  13.8 us (11%)
  other arithmetic  6.5 us (5%)
  matrix products  2.82 us (2%)
    all_gather x1, blocking collectives, shards(): lax.all_gather(after(parent_row[:, :, 0].transpose(1, 0, 2), moved), 'row...  36.6 us
    ppermute x6, waiting for transfers between devices, shifted(): lax.ppermute(value, axis, [(i, (i + step) % count) for i in range(count)])  21.8 us
    pallas_call x2, Pallas kernels, front(): pl.pallas_call(functools.partial(front_kernel, where, len(arrived)), grid...  12.8 us
    ppermute x6, starting transfers between devices, shifted(): lax.ppermute(value, axis, [(i, (i + step) % count) for i in range(count)])  10.7 us
    unnamed x47, local copies, waits for them, and re-layouts  10.3 us
    all_to_all x2, starting transfers between devices, to_plane(): lax.all_to_all(jnp.concatenate([jnp.stack(block_rows, axis=1)] * 2), PLAN...  8.34 us
    pallas_call x1, Pallas kernels, contribution(): pl.pallas_call(functools.partial(update_kernel, grid), in_specs=[pl.Block...  4.34 us
    all_to_all x1, starting transfers between devices, shards(): lax.all_to_all(block_rows[0][:, None], PLANE, split_axis=0, concat_axis=0...  3.87 us
  transfers between devices with their start and end apart: 13, of which 5 were waited for; matrix products, arithmetic and copies ran while one was open for 9% of the time, Pallas kernels for 9%

profile of v4, /device:TPU:0, one launch (start us, length us, event | category | flops | bytes accessed | tf_op | source)
XLA Modules:
  0.0 130.3 jit_solution(17116721825968586230)
XLA Ops:
  0.0 1.0 copy.37
  1.0 5.1 %collective-permute-start.2 = (bf16[4,64,256]{2,1,0:T(8,128)(2,1)S(1)}, bf16[4,64,256]{2,1,0:T(8,128)(2,1)S(1)}, u32[]{:S(2)}, u32[]{:S(2)}) collective-permute-start(bf16[4,64,256]{2,1,0:T(8,128)(2,1)S(1)} %bitcast.68), channel_id=1, source_target_pairs={{0,12},{4,0},{8,4},{12,8},{1,13},{5,1},{9,5},{13,9},{2,14},{6,2},{... | collective-permute-start | bytes 393224 | tf_op jit(solution)/shard_map/ppermute | solution.py:22
  6.1 1.0 collective-permute-start
  7.1 0.9 copy.28
  8.0 0.9 copy.27
  9.0 1.6 %collective-permute-start.4 = (bf16[512,256]{1,0:T(8,128)(2,1)S(1)}, bf16[512,256]{1,0:T(8,128)(2,1)S(1)}, u32[]{:S(2)}, u32[]{:S(2)}) collective-permute-start(bf16[512,256]{1,0:T(8,128)(2,1)S(1)} %pad_maximum_fusion.2.refs_6_.refs_0_), channel_id=1, source_target_pairs={{0,2},{1,3},{2,0},{3,1},{4,6},{5,7},{6,4},{7,5},{8,10},{9,11},{10,... | collective-permute-start | bytes 786440 | tf_op jit(solution)/shard_map/ppermute | solution.py:26
  10.5 3.3 %copy.35 = bf16[1,4,1,256,4,1,256]{6,3,4,1,5,2,0:T(8,128)(2,1)} copy(bf16[1,4,1,256,4,1,256]{6,4,5,3,2,1,0:T(4,128)(2,1)} %param.9) | data formatting | bytes 4194304 | tf_op args[0]
  13.9 0.1 slice.15
  14.0 0.1 select_reduce_fusion.1
  14.8 1.0 fusion.refs_1_
  15.8 0.5 collective-permute-done.4.refs_8_.refs_2_
  16.3 0.6 pad_add_fusion.picks
  16.9 0.3 collective-permute-done.1.refs_4_
  17.3 0.5 collective-permute-done.5.refs_9_.refs_3_
  17.8 0.1 copy-done.14
  18.0 0.1 copy-done.8
  18.1 0.7 copy-done.10
  18.8 4.3 %child_update.1 = (bf16[8,256,256]{2,1,0:T(8,128)(2,1)}, bf16[4,256,256]{2,1,0:T(8,128)(2,1)}, bf16[4,256,256]{2,1,0:T(8,128)(2,1)}, bf16[4,256,256]{2,1,0:T(8,128)(2,1)}) custom-call(s32[2,4]{1,0:T(2,128)} %pad_add_fusion.picks, bf16[4,4,256,256]{3,2,1,0:T(8,128)(2,1)} %bitcast.64, bf16[256,256]{1,0:T(8,128)(2,1)} %fusion.refs_1_, ...), custom_call_target="tpu_custom_call" | custom-call | flops 671088640 | bytes 5242880 | tf_op jit(solution)/shard_map/child_update/pallas_call | solution.py:95
  23.2 3.9 %all-to-all-start = ((bf16[8,1,256,256]{3,2,1,0:T(8,128)(2,1)}), bf16[8,1,256,256]{3,2,1,0:T(8,128)(2,1)S(1)}, u32[]{:S(2)}, u32[]{:S(2)}) async-start(bf16[8,1,256,256]{3,2,1,0:T(8,128)(2,1)} %bitcast.67), calls=%async_computation | async-start | bytes 2097152 | tf_op jit(solution)/shard_map/all_to_all | solution.py:314
  27.1 2.3 %collective-permute-start.6 = (bf16[4,256,256]{2,1,0:T(8,128)(2,1)}, bf16[4,256,256]{2,1,0:T(8,128)(2,1)S(1)}, u32[]{:S(2)}, u32[]{:S(2)}) collective-permute-start(bf16[4,256,256]{2,1,0:T(8,128)(2,1)} %get-tuple-element.21), channel_id=1, source_target_pairs={{0,4},{4,8},{8,12},{12,0},{1,5},{5,9},{9,13},{13,1},{2,6},{6,10},{... | collective-permute-start | bytes 1572872 | tf_op jit(solution)/shard_map/ppermute | solution.py:22
  29.4 1.6 %collective-permute-start.7 = (bf16[4,256,256]{2,1,0:T(8,128)(2,1)S(1)}, bf16[4,256,256]{2,1,0:T(8,128)(2,1)S(1)}, u32[]{:S(2)}, u32[]{:S(2)}) collective-permute-start(bf16[4,256,256]{2,1,0:T(8,128)(2,1)S(1)} %copy-done.21), channel_id=1, source_target_pairs={{0,12},{4,0},{8,4},{12,8},{1,13},{5,1},{9,5},{13,9},{2,14},{6,2},{... | collective-permute-start | bytes 1572872 | tf_op jit(solution)/shard_map/ppermute | solution.py:22
  31.0 2.1 %collective-permute-start.8 = (bf16[4,256,256]{2,1,0:T(8,128)(2,1)S(1)}, bf16[4,256,256]{2,1,0:T(8,128)(2,1)}, u32[]{:S(2)}, u32[]{:S(2)}) collective-permute-start(bf16[4,256,256]{2,1,0:T(8,128)(2,1)S(1)} %pad_maximum_fusion.1), channel_id=1, source_target_pairs={{0,16},{16,0},{1,17},{17,1},{2,18},{18,2},{3,19},{19,3},{4,20},{20... | collective-permute-start | bytes 1572872 | tf_op jit(solution)/shard_map/ppermute | solution.py:26
  33.1 10.8 %collective-permute-done.6 = bf16[4,256,256]{2,1,0:T(8,128)(2,1)S(1)} collective-permute-done((bf16[4,256,256]{2,1,0:T(8,128)(2,1)}, bf16[4,256,256]{2,1,0:T(8,128)(2,1)S(1)}, u32[]{:S(2)}, u32[]{:S(2)}) %collective-permute-start.6) | collective-permute-done | bytes 524320 | tf_op jit(solution)/shard_map/ppermute | solution.py:22
  43.9 10.8 %collective-permute-done.7 = bf16[4,256,256]{2,1,0:T(8,128)(2,1)S(1)} collective-permute-done((bf16[4,256,256]{2,1,0:T(8,128)(2,1)S(1)}, bf16[4,256,256]{2,1,0:T(8,128)(2,1)S(1)}, u32[]{:S(2)}, u32[]{:S(2)}) %collective-permute-start.7) | collective-permute-done | bytes 524320 | tf_op jit(solution)/shard_map/ppermute | solution.py:22
  54.7 1.5 %maximum_maximum_fusion = bf16[8,2,256,256]{3,2,1,0:T(8,128)(2,1)} fusion(bf16[4,1,256,256]{3,2,1,0:T(8,128)(2,1)S(1)} %bitcast.75, bf16[4,1,256,256]{3,2,1,0:T(8,128)(2,1)S(1)} %bitcast.74), kind=kLoop, calls=%fused_computation | loop fusion | flops 3145728 | bytes 3145728 | tf_op jit(solution)/shard_map/concatenate | solution.py:254
  56.2 4.0 %all-to-all-start.1 = ((bf16[8,2,256,256]{3,2,1,0:T(8,128)(2,1)}), bf16[8,2,256,256]{3,2,1,0:T(8,128)(2,1)S(1)}, u32[]{:S(2)}, u32[]{:S(2)}) async-start(bf16[8,2,256,256]{3,2,1,0:T(8,128)(2,1)} %maximum_maximum_fusion), calls=%async_computation.1 | async-start | bytes 4194304 | tf_op jit(solution)/shard_map/all_to_all | solution.py:253
  60.3 0.1 convert_reduce_fusion
  60.4 0.5 copy-done.18
  60.9 0.7 slice.19
  62.4 0.1 stack.116
  62.6 0.6 iota_minimum_fusion
  63.2 0.7 collective-permute-start.9
  63.9 0.1 select_reduce_fusion.2
  64.1 36.6 %all_gather.3.rows_ref = bf16[4,256,256]{2,1,0:T(8,128)(2,1)} all-gather(bf16[4,64,256]{2,1,0:T(8,128)(2,1)S(1)} %bitcast.72), channel_id=1, replica_groups=mesh['half'=2,'row'=4,'col'=4] {'row'}, dimensions={1}, use_global_device_ids=true | all-gather | bytes 655360 | tf_op jit(solution)/shard_map/all_gather | solution.py:319
  100.7 2.3 %pad_maximum_fusion = bf16[8,1,256,256]{3,2,1,0:T(8,128)(2,1)} fusion(bf16[4,1,256,256]{3,2,1,0:T(8,128)(2,1)} %bitcast.34), kind=kLoop, calls=%fused_computation.4 | loop fusion | flops 524288 | bytes 1572864 | tf_op jit(solution)/shard_map/concatenate | solution.py:254
  103.1 4.4 %all-to-all-start.2 = ((bf16[8,1,256,256]{3,2,1,0:T(8,128)(2,1)}), bf16[8,1,256,256]{3,2,1,0:T(8,128)(2,1)}, u32[]{:S(2)}, u32[]{:S(2)}) async-start(bf16[8,1,256,256]{3,2,1,0:T(8,128)(2,1)} %pad_maximum_fusion), calls=%async_computation.2 | async-start | bytes 2097152 | tf_op jit(solution)/shard_map/all_to_all | solution.py:253
  107.6 0.2 select_reduce_fusion
  107.7 0.1 concatenate.31.picks
  107.9 0.1 concatenate.27.picks
  108.0 0.1 fusion.4.refs_5_.refs_6_
  108.1 1.8 %fusion.3.inverse_ref = bf16[256,256]{1,0:T(8,128)(2,1)} fusion(bf16[256,256]{1,0:T(8,128)(2,1)} %param.16, s32[256]{0:T(256)S(1)} %add.240), kind=kOutput, calls=%fused_computation.11 | convolution fusion | flops 33619968 | bytes 263168 | tf_op jit(solution)/shard_map/dot_general | solution.py:59
  109.9 3.0 %parent_panels.1 = (bf16[256,1024]{1,0:T(8,128)(2,1)}, bf16[8,256,256]{2,1,0:T(8,128)(2,1)}) custom-call(bf16[256,256]{1,0:T(8,128)(2,1)} %fusion.3.inverse_ref, bf16[4,256,256]{2,1,0:T(8,128)(2,1)} %all_gather.3.rows_ref, bf16[512,256]{1,0:T(8,128)(2,1)} %copy-done.6, bf16[512,256]{1,0:T(8,128)(2,1)} %copy-done.8, bf16[512,256]{1,0:T(8,128)(2,1)} %copy-done.7, ...), custom_call_target="tpu_custom_call" | custom-call | flops 134217728 | bytes 3145728 | tf_op jit(solution)/shard_map/parent_panels/pallas_call | solution.py:129
  112.9 1.2 copy-done.1
  114.2 1.0 copy-done.3
  115.2 8.6 %front.1.refs_7_ = bf16[8,256,4,256]{3,2,1,0:T(4,128)(2,1)} custom-call(s32[10,8]{1,0:T(8,128)S(1)} %concatenate.31.picks, bf16[8,1,256,256]{3,2,1,0:T(8,128)(2,1)S(1)} %all-to-all-done.refs_0_, bf16[8,2,256,256]{3,2,1,0:T(8,128)(2,1)S(1)} %all-to-all-done.1.refs_1_, bf16[8,256,256]{2,1,0:T(8,128)(2,1)S(1)} %copy-done.1, bf16[256,1024]{1,0:T(8,128)(2,1)S(1)} %copy-done.3, ...), custom_call_target="tpu_custom_call" | custom-call | flops 1879048192 | bytes 11010048 | tf_op jit(solution)/shard_map/front/pallas_call | solution.py:237
  123.8 1.2 copy-done.2
  125.0 1.0 copy-done.4
  126.0 4.2 %front_end.1 = bf16[8,256,4,256]{3,2,1,0:T(4,128)(2,1)} custom-call(s32[10,8]{1,0:T(8,128)S(1)} %concatenate.27.picks, bf16[8,1,256,256]{3,2,1,0:T(8,128)(2,1)S(1)} %all-to-all-done.refs_0_, bf16[8,2,256,256]{3,2,1,0:T(8,128)(2,1)S(1)} %all-to-all-done.1.refs_1_, bf16[8,1,256,256]{3,2,1,0:T(8,128)(2,1)} %all-to-all-done.2.refs_2_, ...), custom_call_target="tpu_custom_call", output_to_operand_aliasing={{}: (8, {})} | custom-call | flops 536870912 | bytes 3145728 | tf_op jit(solution)/shard_map/front_end/pallas_call | solution.py:237
  (83 shorter events, 1.4 us)
Async XLA Ops:
  0.0 14.8 %copy-start = (bf16[1,256,256]{2,1,0:T(8,128)(2,1)S(1)}, bf16[1,256,256]{2,1,0:T(8,128)(2,1)}, u32[]{:S(2)}) copy-start(bf16[1,256,256]{2,1,0:T(8,128)(2,1)} %param.12) | copy-start | bytes 393220
  1.0 12.9 %copy-start.12 = (bf16[1,64,4,1,256]{4,1,2,3,0:T(8,128)(2,1)}, bf16[1,64,4,1,256]{4,1,2,3,0:T(8,128)(2,1)S(1)}, u32[]{:S(2)}) copy-start(bf16[1,64,4,1,256]{4,1,2,3,0:T(8,128)(2,1)S(1)} %copy.37) | copy-start | bytes 393220
  1.0 16.0 %collective-permute-start.2 = (bf16[4,64,256]{2,1,0:T(8,128)(2,1)S(1)}, bf16[4,64,256]{2,1,0:T(8,128)(2,1)S(1)}, u32[]{:S(2)}, u32[]{:S(2)}) collective-permute-start(bf16[4,64,256]{2,1,0:T(8,128)(2,1)S(1)} %bitcast.68), channel_id=1, source_target_pairs={{0,12},{4,0},{8,4},{12,8},{1,13},{5,1},{9,5},{13,9},{2,14},{6,2},{... | collective-permute-start | bytes 393224 | tf_op jit(solution)/shard_map/ppermute | solution.py:22
  6.1 11.2 %collective-permute-start.1 = (bf16[4,64,256]{2,1,0:T(8,128)(2,1)S(1)}, bf16[4,64,256]{2,1,0:T(8,128)(2,1)S(1)}, u32[]{:S(2)}, u32[]{:S(2)}) collective-permute-start(bf16[4,64,256]{2,1,0:T(8,128)(2,1)S(1)} %bitcast.69), channel_id=1, source_target_pairs={{0,8},{4,12},{8,0},{12,4},{1,9},{5,13},{9,1},{13,5},{2,10},{6,14},... | collective-permute-start | bytes 393224 | tf_op jit(solution)/shard_map/ppermute | solution.py:22
  6.1 11.2 %collective-permute-start = (bf16[4,64,256]{2,1,0:T(8,128)(2,1)S(1)}, bf16[4,64,256]{2,1,0:T(8,128)(2,1)S(1)}, u32[]{:S(2)}, u32[]{:S(2)}) collective-permute-start(bf16[4,64,256]{2,1,0:T(8,128)(2,1)S(1)} %bitcast.70), channel_id=1, source_target_pairs={{0,4},{4,8},{8,12},{12,0},{1,5},{5,9},{9,13},{13,1},{2,6},{6,10},{... | collective-permute-start | bytes 393224 | tf_op jit(solution)/shard_map/ppermute | solution.py:22
  9.0 4.9 %copy-start.6 = (bf16[512,256]{1,0:T(8,128)(2,1)}, bf16[512,256]{1,0:T(8,128)(2,1)S(1)}, u32[]{:S(2)}) copy-start(bf16[512,256]{1,0:T(8,128)(2,1)S(1)} %pad_maximum_fusion.2.refs_6_.refs_0_) | copy-start | bytes 786436
  9.0 4.9 %copy-start.17 = (s32[2,16]{1,0:T(2,128)S(1)}, s32[2,16]{1,0:T(2,128)}, u32[]{:S(2)}) copy-start(s32[2,16]{1,0:T(2,128)} %param.13) | copy-start | bytes 388
  9.0 7.3 %collective-permute-start.4 = (bf16[512,256]{1,0:T(8,128)(2,1)S(1)}, bf16[512,256]{1,0:T(8,128)(2,1)S(1)}, u32[]{:S(2)}, u32[]{:S(2)}) collective-permute-start(bf16[512,256]{1,0:T(8,128)(2,1)S(1)} %pad_maximum_fusion.2.refs_6_.refs_0_), channel_id=1, source_target_pairs={{0,2},{1,3},{2,0},{3,1},{4,6},{5,7},{6,4},{7,5},{8,10},{9,11},{10,... | collective-permute-start | bytes 786440 | tf_op jit(solution)/shard_map/ppermute | solution.py:26
  13.8 3.5 %collective-permute-start.3 = (bf16[512,256]{1,0:T(8,128)(2,1)S(1)}, bf16[512,256]{1,0:T(8,128)(2,1)S(1)}, u32[]{:S(2)}, u32[]{:S(2)}) collective-permute-start(bf16[512,256]{1,0:T(8,128)(2,1)S(1)} %pad_maximum_fusion.2.refs_6_.refs_0_), channel_id=1, source_target_pairs={{0,1},{1,0},{2,3},{3,2},{4,5},{5,4},{6,7},{7,6},{8,9},{9,8},{10,11... | collective-permute-start | bytes 786440 | tf_op jit(solution)/shard_map/ppermute | solution.py:26
  16.3 1.5 %copy-start.7 = (bf16[512,256]{1,0:T(8,128)(2,1)}, bf16[512,256]{1,0:T(8,128)(2,1)S(1)}, u32[]{:S(2)}) copy-start(bf16[512,256]{1,0:T(8,128)(2,1)S(1)} %collective-permute-done.4.refs_8_.refs_2_) | copy-start | bytes 786436
  16.3 1.5 %collective-permute-start.5 = (bf16[512,256]{1,0:T(8,128)(2,1)S(1)}, bf16[512,256]{1,0:T(8,128)(2,1)S(1)}, u32[]{:S(2)}, u32[]{:S(2)}) collective-permute-start(bf16[512,256]{1,0:T(8,128)(2,1)S(1)} %collective-permute-done.4.refs_8_.refs_2_), channel_id=1, source_target_pairs={{0,1},{1,0},{2,3},{3,2},{4,5},{5,4},{6,7},{7,6},{8,9},{9,8},{10,11... | collective-permute-start | bytes 786440 | tf_op jit(solution)/shard_map/ppermute | solution.py:26
  16.9 0.9 copy-start.13
  17.3 0.7 copy-start.14
  17.3 0.7 copy-start.15
  17.3 0.8 copy-start.8
  18.1 0.7 copy-start.10
  23.2 3.9 %copy-start.9 = (bf16[512,256]{1,0:T(8,128)(2,1)S(1)}, bf16[512,256]{1,0:T(8,128)(2,1)}, u32[]{:S(2)}) copy-start(bf16[512,256]{1,0:T(8,128)(2,1)} %copy-done.8) | copy-start | bytes 786436
  23.2 6.2 %copy-start.21 = (bf16[4,256,256]{2,1,0:T(8,128)(2,1)S(1)}, bf16[4,256,256]{2,1,0:T(8,128)(2,1)}, u32[]{:S(2)}) copy-start(bf16[4,256,256]{2,1,0:T(8,128)(2,1)} %get-tuple-element.22) | copy-start | bytes 1572868
  23.2 7.8 %copy-start.11 = (bf16[512,256]{1,0:T(8,128)(2,1)S(1)}, bf16[512,256]{1,0:T(8,128)(2,1)}, u32[]{:S(2)}) copy-start(bf16[512,256]{1,0:T(8,128)(2,1)} %copy-done.10) | copy-start | bytes 786436
  23.2 31.5 %all-to-all-start = ((bf16[8,1,256,256]{3,2,1,0:T(8,128)(2,1)}), bf16[8,1,256,256]{3,2,1,0:T(8,128)(2,1)S(1)}, u32[]{:S(2)}, u32[]{:S(2)}) async-start(bf16[8,1,256,256]{3,2,1,0:T(8,128)(2,1)} %bitcast.67), calls=%async_computation | async-start | bytes 2097152 | tf_op jit(solution)/shard_map/all_to_all | solution.py:314
  27.1 16.8 %collective-permute-start.6 = (bf16[4,256,256]{2,1,0:T(8,128)(2,1)}, bf16[4,256,256]{2,1,0:T(8,128)(2,1)S(1)}, u32[]{:S(2)}, u32[]{:S(2)}) collective-permute-start(bf16[4,256,256]{2,1,0:T(8,128)(2,1)} %get-tuple-element.21), channel_id=1, source_target_pairs={{0,4},{4,8},{8,12},{12,0},{1,5},{5,9},{9,13},{13,1},{2,6},{6,10},{... | collective-permute-start | bytes 1572872 | tf_op jit(solution)/shard_map/ppermute | solution.py:22
  29.4 25.3 %collective-permute-start.7 = (bf16[4,256,256]{2,1,0:T(8,128)(2,1)S(1)}, bf16[4,256,256]{2,1,0:T(8,128)(2,1)S(1)}, u32[]{:S(2)}, u32[]{:S(2)}) collective-permute-start(bf16[4,256,256]{2,1,0:T(8,128)(2,1)S(1)} %copy-done.21), channel_id=1, source_target_pairs={{0,12},{4,0},{8,4},{12,8},{1,13},{5,1},{9,5},{13,9},{2,14},{6,2},{... | collective-permute-start | bytes 1572872 | tf_op jit(solution)/shard_map/ppermute | solution.py:22
  31.0 23.6 %collective-permute-start.8 = (bf16[4,256,256]{2,1,0:T(8,128)(2,1)S(1)}, bf16[4,256,256]{2,1,0:T(8,128)(2,1)}, u32[]{:S(2)}, u32[]{:S(2)}) collective-permute-start(bf16[4,256,256]{2,1,0:T(8,128)(2,1)S(1)} %pad_maximum_fusion.1), channel_id=1, source_target_pairs={{0,16},{16,0},{1,17},{17,1},{2,18},{18,2},{3,19},{19,3},{4,20},{20... | collective-permute-start | bytes 1572872 | tf_op jit(solution)/shard_map/ppermute | solution.py:26
  56.2 5.6 %copy-start.16 = (bf16[64,4,1,256]{3,1,2,0:T(4,128)(2,1)S(1)}, bf16[64,4,1,256]{3,1,2,0:T(4,128)(2,1)}, u32[]{:S(2)}) copy-start(bf16[64,4,1,256]{3,1,2,0:T(4,128)(2,1)} %param.14) | copy-start | bytes 393220
  56.2 44.6 %all-to-all-start.1 = ((bf16[8,2,256,256]{3,2,1,0:T(8,128)(2,1)}), bf16[8,2,256,256]{3,2,1,0:T(8,128)(2,1)S(1)}, u32[]{:S(2)}, u32[]{:S(2)}) async-start(bf16[8,2,256,256]{3,2,1,0:T(8,128)(2,1)} %maximum_maximum_fusion), calls=%async_computation.1 | async-start | bytes 4194304 | tf_op jit(solution)/shard_map/all_to_all | solution.py:253
  60.3 0.6 copy-start.18
  60.9 0.7 copy-start.20
  63.2 37.5 %collective-permute-start.9 = (bf16[4,256,256]{2,1,0:T(8,128)(2,1)}, bf16[4,256,256]{2,1,0:T(8,128)(2,1)}, u32[]{:S(2)}, u32[]{:S(2)}) collective-permute-start(bf16[4,256,256]{2,1,0:T(8,128)(2,1)} %get-tuple-element.28), channel_id=1, source_target_pairs={{0,8},{4,12},{8,0},{12,4},{1,9},{5,13},{9,1},{13,5},{2,10},{6,14},... | collective-permute-start | bytes 1572872 | tf_op jit(solution)/shard_map/ppermute | solution.py:22
  64.1 43.4 %copy-start.19 = (pred[8]{0:T(512)(128)(4,1)S(1)}, pred[8]{0:T(512)(128)(4,1)}, u32[]{:S(2)}) copy-start(pred[8]{0:T(512)(128)(4,1)} %copy-done.18) | copy-start | bytes 28
  103.0 9.9 %copy-start.5 = (f32[8,1,256]{2,1,0:T(1,128)S(1)}, f32[8,1,256]{2,1,0:T(1,128)}, u32[]{:S(2)}) copy-start(f32[8,1,256]{2,1,0:T(1,128)} %refs_5_.1) | copy-start | bytes 24580
  103.1 20.7 %all-to-all-start.2 = ((bf16[8,1,256,256]{3,2,1,0:T(8,128)(2,1)}), bf16[8,1,256,256]{3,2,1,0:T(8,128)(2,1)}, u32[]{:S(2)}, u32[]{:S(2)}) async-start(bf16[8,1,256,256]{3,2,1,0:T(8,128)(2,1)} %pad_maximum_fusion), calls=%async_computation.2 | async-start | bytes 2097152 | tf_op jit(solution)/shard_map/all_to_all | solution.py:253
  112.9 1.2 copy-start.1
  114.2 1.0 copy-start.3
  123.8 1.2 copy-start.2
  125.0 1.0 copy-start.4
